TPU v7x, 512 devices: a whole 4x4x16 slice. The times are simulated.
512 devices in a mesh: dp: 64 (over z, x), tensor: 8 (over y, core).
Axes of the slice: x: 4, y: 4, z: 16, core: 2. Of those that a mesh axis runs over, the one named last changes fastest.
Arguments:
- x_slots: bfloat16 [640, 12288], P('dp', 'tensor'), may hold values from -6 to 6
- counts: int32 [64], replicated, may hold values from 1 to 10, 320 in all
- w_fc1: bfloat16 [24576, 12288], P('dp', 'tensor'), may hold values from -0.0546875 to 0.0546875
- b_fc1: float32 [24576], P('dp'), may hold values from -3 to 3
- upstream: bfloat16 [640, 24576], P('dp'), may hold values from -6 to 6
- owners: int32 [4096, 1], P('dp'), may hold values from 0 to 63; in each aligned block of 64 rows (0 to 63, 64 to 127, ...) at most 2 rows name the same one
Outputs:
- grad_slots: bfloat16 [640, 12288], P('dp', 'tensor')
- grad_bias: float32 [24576], P('dp')
- moved_grads: bfloat16 [8192, 6, 12288], P('dp', None, 'tensor')
Inputs may be any that keep to these rules, and one draw needn't show every extreme that they name: Survivor s holds its counts[s] tokens in its first slots, in token order. `owners`: among the 64 blocks of one old owner (aligned rows), no new owner appears more than 2 times.
All inputs are finite; a program needn't handle non-finite values.
Results may differ from a plain program's by a relative error of at most 0.015.
Values may be sent and summed in bfloat16 or wider, within the bound.
No kernel may reach another device: no remote copies, remote signals or barrier semaphores. Data moves between devices by JAX's collectives and lax.ppermute only.
A program may use at most 64 MiB of HBM per device.

v0:
```python
import jax
import jax.numpy as jnp
from jax import lax
from jax.sharding import PartitionSpec as P

MOST = 2
SLOT_CAPACITY = 10


def gelu_slope(values):
    inner_arg = 0.7978845608 * (values + 0.044715 * values * values * values)
    tangent = jnp.tanh(inner_arg)
    return 0.5 * (1.0 + tangent) + 0.5 * values * (1.0 - tangent * tangent) * 0.7978845608 * (
        1.0 + 3.0 * 0.044715 * values * values
    )


def body(x_slots, counts, w_fc1, b_fc1, upstream, owners):
    dp_devices = lax.axis_size("dp")
    feature_cols = w_fc1.shape[1]
    block_rows = w_fc1.shape[0] // dp_devices
    received = lax.all_to_all(upstream, "dp", split_axis=1, concat_axis=0, tiled=True)
    slot_numbers = jnp.arange(dp_devices * SLOT_CAPACITY, dtype=jnp.int32)
    remaining_replica = slot_numbers // SLOT_CAPACITY
    slot_position = slot_numbers % SLOT_CAPACITY
    slot_active_mask = slot_position < counts[remaining_replica]
    active_token_rows = slot_active_mask.astype(jnp.float32)[:, None]
    all_rows = lax.all_gather(x_slots, "dp", axis=0, tiled=True)
    partial_pre = lax.dot_general(
        all_rows, w_fc1, (((1,), (1,)), ((), ())), preferred_element_type=jnp.float32
    )
    pre = lax.psum(partial_pre.astype(jnp.bfloat16), "tensor").astype(jnp.float32) + b_fc1
    grad_pre = received.astype(jnp.float32) * gelu_slope(pre) * active_token_rows
    grad_low = grad_pre.astype(jnp.bfloat16)
    grad_bias = jnp.sum(grad_pre, axis=0)
    grad_weight = lax.dot_general(
        grad_low, all_rows, (((0,), (0,)), ((), ())), preferred_element_type=jnp.float32
    ).astype(jnp.bfloat16)
    summed = lax.psum_scatter(
        jnp.dot(grad_low, w_fc1, preferred_element_type=jnp.float32),
        "dp",
        scatter_dimension=0,
        tiled=True,
    ).astype(jnp.bfloat16)
    owner_of = owners[:, 0]
    block_count = owner_of.shape[0]
    block_order = jnp.arange(block_count, dtype=jnp.int32)
    earlier = (owner_of[None, :] == owner_of[:, None]) & (
        block_order[None, :] < block_order[:, None]
    )
    block_rank = jnp.sum(earlier.astype(jnp.int32), axis=1)
    targets = jnp.arange(dp_devices * MOST, dtype=jnp.int32)
    selector = (
        (owner_of[None, :] == targets[:, None] // MOST)
        & (block_rank[None, :] == targets[:, None] % MOST)
    ).astype(jnp.bfloat16)
    blocks = grad_weight.reshape(block_count, block_rows * feature_cols)
    packed_blocks = jnp.dot(selector, blocks, preferred_element_type=jnp.float32).astype(
        jnp.bfloat16
    )
    moved_blocks = lax.all_to_all(packed_blocks, "dp", split_axis=0, concat_axis=0, tiled=True)
    return (summed, grad_bias, moved_blocks.reshape(dp_devices * MOST, block_rows, feature_cols))


def solution(mesh):
    in_specs = (P("dp", "tensor"), P(), P("dp", "tensor"), P("dp"), P("dp", None), P("dp", None))
    out_specs = (P("dp", "tensor"), P("dp"), P("dp", None, "tensor"))
    return jax.shard_map(body, mesh=mesh, in_specs=in_specs, out_specs=out_specs, check_vma=False)
```

profile of v0, /device:TPU:24, one launch (start us, length us, event | category | flops | bytes accessed | tf_op | source)
XLA Modules:
  0.0 702.4 jit_solution(8015241855894624304)
XLA Ops:
  7.2 0.0 copy-start
  7.2 0.0 all-gather.3.cloned.1.call-start
  7.2 0.7 all-gather.3.cloned.1.call-update
  7.9 1.3 copy.16
  9.2 0.0 copy-start.2
  9.2 0.0 copy-start.5
  9.2 0.1 slice.65
  9.3 1.2 copy.14
  10.4 18.6 %all-to-all-start = ((bf16[10,64,384]{2,0,1:T(8,128)(2,1)}), bf16[10,64,384]{2,0,1:T(8,128)(2,1)S(1)}, u32[]{:S(2)}, u32[]{:S(2)}) async-start(bf16[10,64,384]{2,0,1:T(8,128)(2,1)} %copy.14), calls=%async_computation | async-start | bytes 1572864 | tf_op jit(solution)/shard_map/all_to_all | solution.py:22
  29.0 0.0 all-reduce.4.cloned.1.call-start
  31.3 0.0 copy-done.2
  31.3 0.7 fusion.29
  31.9 0.7 fusion.28
  32.7 4.3 fusion.23
  37.0 0.6 and_select_fusion.1
  37.6 0.7 fusion.26
  38.3 0.7 fusion.27
  39.0 0.0 copy-done.5
  39.0 0.7 convert_reduce_fusion
  39.7 35.7 %fusion.22 = f32[640]{0:T(1024)S(1)} fusion(pred[640]{0:T(1024)(128)(4,1)S(1)} %compare_reduce_fusion, pred[640]{0:T(1024)(128)(4,1)S(1)} %compare_reduce_fusion.1, pred[640]{0:T(1024)(128)(4,1)S(1)} %compare_reduce_fusion.2, pred[640]{0:T(1024)(128)(4,1)S(1)} %compare_reduce_fusion.3, pred[640]{0:T(1024)(128)(4,1)S(1)} %compare_reduce_fusion.4, ...), kind=kLoop, calls=%fused_computation.98 | loop fusion | flops 41600 | bytes 41828 | tf_op jit(solution)/shard_map/convert_element_type | solution.py:27
  75.4 88.5 %all-gather.3.cloned.1.call-done = bf16[64,10,1536]{2,1,0:T(8,128)(2,1)} async-done(((bf16[1,10,1536]{2,1,0:T(8,128)(2,1)}), bf16[64,10,1536]{2,1,0:T(8,128)(2,1)}) %all-gather.3.cloned.1.call-update) | async-done | bytes 1966096 | tf_op jit(solution)/shard_map/all_gather | solution.py:28
  163.9 4.2 reshape.336
  168.1 0.0 copy-done
  168.1 3.5 convolution_convert_fusion.2
  171.7 0.0 all-reduce.4.cloned.1.call-update
  171.7 0.0 copy-start.4
  171.7 0.0 all-to-all-done
  171.7 0.1 convert_bitcast_fusion
  171.8 1.1 reshape.130
  172.9 67.3 %all-reduce.4.cloned.1.call-done = bf16[640,384]{1,0:T(8,128)(2,1)} async-done(((bf16[640,384]{1,0:T(8,128)(2,1)}), bf16[640,384]{1,0:T(8,128)(2,1)}) %all-reduce.4.cloned.1.call-update) | async-done | bytes 491536 | tf_op jit(solution)/shard_map/psum | solution.py:32
  240.2 0.0 copy-done.4
  240.2 2.7 fusion.24
  242.9 0.8 copy-done.1
  243.7 0.0 copy-done.3
  243.7 2.1 convolution_convert_fusion.1
  245.8 3.3 reshape.128
  249.1 0.0 copy-done.6
  249.1 0.0 copy-done.7
  249.1 2.1 convolution_convert_fusion
  251.2 2.3 all_to_all.18
  253.5 15.6 %all-to-all-start.1 = ((bf16[64,2,9216]{2,1,0:T(2,128)(2,1)}), bf16[64,2,9216]{2,1,0:T(2,128)(2,1)S(1)}, u32[]{:S(2)}, u32[]{:S(2)}) async-start(bf16[64,2,9216]{2,1,0:T(2,128)(2,1)} %all_to_all.18), calls=%async_computation.1 | async-start | bytes 4718592 | tf_op jit(solution)/shard_map/all_to_all | solution.py:61
  269.1 1.3 dynamic-slice
  271.1 4.1 fusion.8
  275.2 412.0 %all-reduce.5 = bf16[640,1536]{1,0:T(8,128)(2,1)} all-reduce(f32[640,1536]{1,0:T(8,128)} %fusion.8), channel_id=2, replica_groups=mesh['dp'=64,'tensor'=8] {'dp'}, use_global_device_ids=true, to_apply=%region_1.2.clone | all-reduce | flops 983040 | bytes 5898240
  687.1 1.5 dynamic-slice_convert_fusion
  688.6 0.0 all-to-all-done.1
  688.6 3.0 reshape.129
  691.6 4.0 copy.15
  (61 shorter events, 2.2 us)
Async XLA Ops:
  7.2 161.0 %copy-start = (bf16[384,1536]{1,0:T(8,128)(2,1)S(1)}, bf16[384,1536]{1,0:T(8,128)(2,1)}, u32[]{:S(2)}) copy-start(bf16[384,1536]{1,0:T(8,128)(2,1)} %param.8) | copy-start | bytes 3538948
  7.2 156.7 %all-gather.3.cloned.1.call-start = ((), (), s32[]{:S(2)}) async-start(), calls=%async_computation.3 | async-start | bytes 3194880 | tf_op jit(solution)/shard_map/all_gather | solution.py:28
  9.2 22.1 %copy-start.2 = (s32[64]{0:T(128)S(1)}, s32[64]{0:T(128)}, u32[]{:S(2)}) copy-start(s32[64]{0:T(128)} %param.7) | copy-start | bytes 772
  9.2 29.8 %copy-start.5 = (s32[64,1]{0,1:T(1,128)S(1)}, s32[64,1]{0,1:T(1,128)}, u32[]{:S(2)}) copy-start(s32[64,1]{0,1:T(1,128)} %param.11) | copy-start | bytes 772
  10.4 161.3 %all-to-all-start = ((bf16[10,64,384]{2,0,1:T(8,128)(2,1)}), bf16[10,64,384]{2,0,1:T(8,128)(2,1)S(1)}, u32[]{:S(2)}, u32[]{:S(2)}) async-start(bf16[10,64,384]{2,0,1:T(8,128)(2,1)} %copy.14), calls=%async_computation | async-start | bytes 1572864 | tf_op jit(solution)/shard_map/all_to_all | solution.py:22
  29.0 211.2 %all-reduce.4.cloned.1.call-start = ((), (), s32[]{:S(2)}) async-start(), calls=%async_computation.2 | async-start | bytes 983040 | tf_op jit(solution)/shard_map/psum | solution.py:32
  171.7 68.5 %copy-start.4 = (f32[384]{0:T(512)S(1)}, f32[384]{0:T(512)}, u32[]{:S(2)}) copy-start(f32[384]{0:T(512)} %param.9) | copy-start | bytes 4612
  172.9 70.7 %copy-start.3 = (bf16[640,1536]{1,0:T(8,128)(2,1)S(1)}, bf16[640,1536]{1,0:T(8,128)(2,1)}, u32[]{:S(2)}) copy-start(bf16[640,1536]{1,0:T(8,128)(2,1)} %reshape.336) | copy-start | bytes 5898244
  242.9 0.8 copy-start.1
  245.8 3.3 copy-start.6
  245.8 3.3 copy-start.7
  253.5 435.1 %all-to-all-start.1 = ((bf16[64,2,9216]{2,1,0:T(2,128)(2,1)}), bf16[64,2,9216]{2,1,0:T(2,128)(2,1)S(1)}, u32[]{:S(2)}, u32[]{:S(2)}) async-start(bf16[64,2,9216]{2,1,0:T(2,128)(2,1)} %all_to_all.18), calls=%async_computation.1 | async-start | bytes 4718592 | tf_op jit(solution)/shard_map/all_to_all | solution.py:61
Sparse Core Ops, SparseCore 0:
  11.0 152.9 all-gather.2
  171.8 68.3 all-reduce.3
where the time goes:
time: 704 us; the launch traced here: 702 us
  blocking collectives  412 us (59%)
  waiting for transfers between devices  156 us (22%)
  other arithmetic  46.2 us (7%)
  starting transfers between devices  34.2 us (5%)
  local copies, waits for them, and re-layouts  26.8 us (4%)
  between operations  14.9 us (2%)
  matrix products  11.8 us (2%)
    unnamed x1, blocking collectives  412 us
    all_gather x1, waiting for transfers between devices, body(): all_rows = lax.all_gather(x_slots, 'dp', axis=0, tiled=True)  88.5 us
    psum x1, waiting for transfers between devices, body(): lax.psum(partial_pre.astype(jnp.bfloat16), 'tensor').astype(jnp.float32)  67.3 us
    convert_element_type x1, other arithmetic, body(): active_token_rows = slot_active_mask.astype(jnp.float32)[:, None]  35.7 us
    all_to_all x1, starting transfers between devices, body(): lax.all_to_all(upstream, 'dp', split_axis=1, concat_axis=0, tiled=True)  18.6 us
    all_to_all x1, starting transfers between devices, body(): lax.all_to_all(packed_blocks, 'dp', split_axis=0, concat_axis=0, tiled=True)  15.6 us
  transfers between devices with their start and end apart: 4, of which 2 were waited for; matrix products, arithmetic and copies ran while one was open for 9% of the time, Pallas kernels for 0%

commit v1 on v0

v1 whole, which is shorter than its diff:
```python
import functools

import jax
import jax.numpy as jnp
from jax import lax
from jax.experimental import pallas as pl
from jax.experimental.pallas import tpu as pltpu
from jax.sharding import Mesh, PartitionSpec as P

BF, F32, I32 = jnp.bfloat16, jnp.float32, jnp.int32
MOST = 2
BR = 6
SLOTS = 10
LOST = 320
HALF = 512
INTERPRET = False


def iota(shape, dim):
    return lax.broadcasted_iota(I32, shape, dim)


def onehot(mask):
    return jnp.where(mask, 1.0, 0.0).astype(BF)


def dot(a, b):
    return jnp.dot(a, b, preferred_element_type=F32)


def dot_nt(a, b):
    return lax.dot_general(a, b, (((1,), (1,)), ((), ())), preferred_element_type=F32)


def call(kernel, outs, args, scalars=0, scratch=()):
    specs = [pl.BlockSpec(memory_space=pltpu.SMEM)] * scalars
    specs += [pl.BlockSpec(memory_space=pltpu.VMEM)] * (len(args) - scalars)
    return pl.pallas_call(
        kernel,
        out_shape=[jax.ShapeDtypeStruct(s, d) for s, d in outs],
        in_specs=specs,
        out_specs=[pl.BlockSpec(memory_space=pltpu.VMEM)] * len(outs),
        scratch_shapes=list(scratch),
        compiler_params=pltpu.CompilerParams(vmem_limit_bytes=44 * 1024 * 1024),
        interpret=INTERPRET,
    )(*args)


def pack_kernel(nz, share, place, x_ref, up_ref, out_ref, rows, ups):
    hid = ups.shape[1] // 2
    tensor = place[0]
    rows[...] = jnp.zeros_like(rows)
    rows[0:SLOTS, :] = x_ref[...]
    ups[...] = jnp.zeros_like(ups)
    for n in range(2 * nz):
        ups[n * 16 : n * 16 + SLOTS, :] = up_ref[:, n * 2 * hid : (n + 1) * 2 * hid]
    k, lane = iota((2 * hid, 128), 0), iota((2 * hid, 128), 1)
    second = lane >= 64
    pick = (k - jnp.where(second, hid, 0)) == tensor * share + lane - jnp.where(second, 64, 0)
    pick = pick & (lane - jnp.where(second, 64, 0) < share)
    chosen = dot(ups[...], onehot(pick)).astype(BF)
    r, c = iota((16, 16), 0), iota((16, 16), 1)
    same = onehot((r == c) & (r < SLOTS))
    even = onehot(c == 2 * (r - SLOTS))
    odd = onehot(c == 2 * (r - SLOTS) + 1)
    a, b, last = rows[:, :HALF], rows[:, HALF : 2 * HALF], rows[:, 2 * HALF :]
    left = (dot(same, a) + dot(even, last)).astype(BF)
    right = (dot(same, b) + dot(odd, last)).astype(BF)
    for z in range(nz):
        out_ref[z, :, :HALF] = left
        out_ref[z, :, HALF : 2 * HALF] = right
        for p in range(2):
            n = 2 * z + p
            out_ref[z, :, 2 * HALF + p * 128 : 2 * HALF + (p + 1) * 128] = chosen[n * 16 : n * 16 + 16]


def spread_kernel(nx, in_ref, out_ref):
    for x in range(nx):
        p = x // 2
        out_ref[x, :, : 2 * HALF] = in_ref[:, : 2 * HALF]
        out_ref[x, :, 2 * HALF :] = in_ref[:, 2 * HALF + p * 128 : 2 * HALF + (p + 1) * 128]


def slot_of(rho, nz, nx):
    xs = rho // (nz * 16)
    zs = (rho // 16) % nz
    return zs * nx + xs, rho % 16


def mask_kernel(nz, nx, row_ref, col_ref, c_ref, ct_ref):
    n = nz * nx
    tokens, total = c_ref.shape[1], c_ref.shape[2]
    for flat in (True, False):
        if flat:
            shape, dim = (n, total), 1
            counts = row_ref[...].astype(BF)
        else:
            shape, dim = (total, n), 0
            counts = col_ref[...].astype(BF)
        s, _ = slot_of(iota(shape, dim), nz, nx)
        other = iota(shape, 1 - dim)
        before, here = onehot(other < s), onehot(other == s)
        if flat:
            start, count = dot(counts, before)[0:1], dot(counts, here)[0:1]
            vec, grid, tdim = (1, total), (tokens, total), 0
        else:
            start, count = dot(before, counts)[:, 0:1], dot(here, counts)[:, 0:1]
            vec, grid, tdim = (total, 1), (total, tokens), 1
        row = iota(vec, dim) % 16
        start, count = start.astype(I32), count.astype(I32)
        token = iota(grid, tdim)
        for i in range(3):
            r = row if i == 0 else 2 * (row - SLOTS) + (i - 1)
            fits = (r >= 0) & (r < count)
            fits = fits & (row < SLOTS) if i == 0 else fits & (row >= SLOTS)
            where = jnp.where(fits, start + r, -1)
            (c_ref if flat else ct_ref)[i] = onehot(where == token)


def pre_kernel(share, place, rb_ref, c_ref, w_ref, xc_ref, ug_ref, part_ref):
    left, right = rb_ref[:, :HALF], rb_ref[:, HALF : 2 * HALF]
    xc_ref[:, :HALF] = dot(c_ref[0], left).astype(BF)
    xc_ref[:, HALF : 2 * HALF] = dot(c_ref[0], right).astype(BF)
    xc_ref[:, 2 * HALF :] = (dot(c_ref[1], left) + dot(c_ref[2], right)).astype(BF)
    part_ref[...] = dot_nt(w_ref[...], xc_ref[...]).astype(BF)
    ups = dot(c_ref[0], rb_ref[:, 2 * HALF :]).T
    ug_ref[...] = jnp.where(place[0] == 1, ups[64 : 64 + share], ups[:share])


def gelu_slope(values):
    inner_arg = 0.7978845608 * (values + 0.044715 * values * values * values)
    tangent = jnp.tanh(inner_arg)
    return 0.5 * (1.0 + tangent) + 0.5 * values * (1.0 - tangent * tangent) * 0.7978845608 * (
        1.0 + 3.0 * 0.044715 * values * values
    )


def grad_kernel(place, parts_ref, ug_ref, b_ref, out_ref):
    share, tokens = out_ref.shape
    hid = b_ref.shape[1]
    wanted = iota((share, hid), 1) == place[0] * share + iota((share, hid), 0)
    bias = jnp.sum(jnp.where(wanted, b_ref[...], 0.0), axis=1, keepdims=True)
    pre = bias + parts_ref[0].astype(F32)
    for j in range(1, parts_ref.shape[0]):
        pre = pre + parts_ref[j].astype(F32)
    lane = iota((share, tokens), 1)
    grad = jnp.where(lane < LOST, ug_ref[...] * gelu_slope(pre), 0.0)
    total = jnp.sum(grad, axis=1, keepdims=True)
    high = total.astype(BF).astype(F32)
    mid = (total - high).astype(BF).astype(F32)
    low = total - high - mid
    grad = jnp.where(lane == LOST, high, grad)
    grad = jnp.where(lane == LOST + 1, mid, grad)
    grad = jnp.where(lane == LOST + 2, low, grad)
    out_ref[...] = grad.astype(BF)


def token_share(tokens, span, place, a, flip):
    shape, td = ((tokens, 128), 0) if not flip else ((128, tokens), 1)
    token, lane = iota(shape, td), iota(shape, 1 - td)
    inside = (lane >= a * span) & (lane < (a + 1) * span)
    return onehot(inside & (token == place * span + lane - a * span))


def out_kernel(nz, nx, span, place, g_ref, ct_ref, w_ref, oc_ref, or_ref, px_ref, bias_ref):
    hid, tokens = g_ref.shape
    total = px_ref.shape[0]
    blocks = oc_ref.shape[0]
    g = g_ref[...]
    pieces = iota((8, tokens), 1)
    bias_ref[...] = dot_nt(onehot((pieces >= LOST) & (pieces < LOST + 3)), g)
    here = [dot_nt(ct_ref[i], g).astype(BF) for i in range(3)]
    last = w_ref[:, 2 * HALF :]
    px_ref[:, :HALF] = (dot(here[0], w_ref[:, :HALF]) + dot(here[1], last)).astype(BF)
    px_ref[:, HALF : 2 * HALF] = (dot(here[0], w_ref[:, HALF : 2 * HALF]) + dot(here[2], last)).astype(BF)
    r, c = iota((blocks, blocks), 0), iota((blocks, blocks), 1)
    owner = or_ref[0:1, :]
    earlier = (oc_ref[:, 0:1] == owner) & (r < c)
    rank = jnp.sum(jnp.where(earlier, 1.0, 0.0), axis=0, keepdims=True)
    target = jnp.broadcast_to(owner * MOST + rank, (8, blocks)).astype(BF)
    block, unit = iota((blocks, hid), 0), iota((blocks, hid), 1)
    within = unit - block * BR
    member = (within >= 0) & (within < BR)
    offset = jnp.sum(jnp.where(member, within, 0).astype(F32), axis=0, keepdims=True)
    key = dot(target, onehot(member))[0:1] * BR + offset
    rho = iota((total, 1), 0)
    dest, row = slot_of(rho, nz, nx)
    q = row % 4
    tile = jnp.zeros((total, 128), F32)
    for a in range(BR // 2):
        wanted = (dest * MOST + q % 2) * BR + 2 * a + q // 2
        wanted = jnp.where(row // 4 == place[1], wanted, -1).astype(F32)
        part = dot(g, token_share(tokens, span, place[0], a, False)).astype(BF)
        tile = tile + dot(onehot(wanted == key), part)
    px_ref[:, 2 * HALF :] = tile.astype(BF)


def sum_kernel(in_ref, out_ref):
    total = in_ref[0].astype(F32)
    for x in range(1, in_ref.shape[0]):
        total = total + in_ref[x].astype(F32)
    out_ref[...] = total.astype(BF)


def slots_kernel(in_ref, out_ref, moved_ref):
    nz = in_ref.shape[0]
    total = in_ref[0, :, : 2 * HALF].astype(F32)
    for z in range(1, nz):
        total = total + in_ref[z, :, : 2 * HALF].astype(F32)
    total = total.astype(BF)
    left, right = total[:, :HALF], total[:, HALF:]
    r, c = iota((16, 16), 0), iota((16, 16), 1)
    halfway = (c - SLOTS) * 2
    last = dot(onehot(r == halfway), left) + dot(onehot(r == halfway + 1), right)
    out_ref[:, : 2 * HALF] = total[:SLOTS]
    out_ref[:, 2 * HALF :] = last[:SLOTS].astype(BF)
    for z in range(nz):
        moved_ref[z * 16 : (z + 1) * 16, :] = in_ref[z, :, 2 * HALF :]


def weight_kernel(span, m_ref, xc_ref, out_ref):
    ranks, total, _ = m_ref.shape
    tokens = xc_ref.shape[0]
    half = total // 2
    r, c = iota((total, total), 0), iota((total, total), 1)
    low, place = r // half, r % half
    order = onehot(c == (place // 2) * 4 + low * 2 + place % 2)
    xc = xc_ref[...]
    for a in range(BR // 2):
        rows = jnp.zeros((total, tokens), F32)
        for j in range(ranks):
            rows = rows + dot(m_ref[j], token_share(tokens, span, j, a, True))
        rows = dot(order, rows.astype(BF)).astype(BF)
        found = dot(rows, xc).astype(BF)
        out_ref[2 * a] = found[:half]
        out_ref[2 * a + 1] = found[half:]


def body(x_slots, counts, w, bias, upstream, owners):
    nz, nx = lax.axis_size("z"), lax.axis_size("x")
    nt = lax.axis_size(("y", "core"))
    hid = w.shape[0]
    share, span = hid // nt, LOST // nt
    total = nx * nz * 16
    tokens = -(-(LOST + 3) // 128) * 128
    dp = nz * nx
    tensor = lax.axis_index(("y", "core")).astype(I32)
    x_me = lax.axis_index("x").astype(I32)

    packed, = call(
        functools.partial(pack_kernel, nz, share),
        [((nz, 16, 2 * HALF + 256), BF)],
        [tensor[None], x_slots, upstream],
        1,
        [pltpu.VMEM((16, 3 * HALF), BF), pltpu.VMEM((2 * nz * 16, 2 * hid), BF)],
    )
    counts = counts.astype(F32)
    c, ct = call(
        functools.partial(mask_kernel, nz, nx),
        [((3, tokens, total), BF), ((3, total, tokens), BF)],
        [jnp.broadcast_to(counts[None, :], (8, dp)), jnp.broadcast_to(counts[:, None], (dp, 128))],
    )
    along_z = lax.all_to_all(packed, "z", 0, 0, tiled=True)
    spread, = call(
        functools.partial(spread_kernel, nx),
        [((nx, nz * 16, 2 * HALF + 128), BF)],
        [along_z.reshape(nz * 16, 2 * HALF + 256)],
    )
    along_x = lax.all_to_all(spread, "x", 0, 0, tiled=True)
    xc, ug, part = call(
        functools.partial(pre_kernel, share),
        [((tokens, 3 * HALF), BF), ((share, tokens), F32), ((hid, tokens), BF)],
        [(x_me % 2)[None], along_x.reshape(total, 2 * HALF + 128), c, w],
        1,
    )
    parts = lax.all_to_all(part.reshape(nt, share, tokens), ("y", "core"), 0, 0, tiled=True)
    low, = call(
        grad_kernel,
        [((share, tokens), BF)],
        [tensor[None], parts, ug, bias[None, :]],
        1,
    )
    grad = lax.all_gather(low, ("y", "core"), axis=0, tiled=True)
    owner = owners[:, 0].astype(F32)
    blocks = owner.shape[0]
    px, grad_bias = call(
        functools.partial(out_kernel, nz, nx, span),
        [((total, 2 * HALF + 128), BF), ((8, hid), F32)],
        [
            jnp.stack([tensor, x_me]),
            grad,
            ct,
            w,
            jnp.broadcast_to(owner[:, None], (blocks, 128)),
            jnp.broadcast_to(owner[None, :], (8, blocks)),
        ],
        1,
    )
    px = lax.all_to_all(px.reshape(nx, nz * 16, 2 * HALF + 128), "x", 0, 0, tiled=True)
    summed, = call(sum_kernel, [((nz * 16, 2 * HALF + 128), BF)], [px])
    pz = lax.all_to_all(summed.reshape(nz, 16, 2 * HALF + 128), "z", 0, 0, tiled=True)
    grad_slots, moved = call(
        slots_kernel, [((SLOTS, 3 * HALF), BF), ((nz * 16, 128), BF)], [pz]
    )
    moved = lax.all_gather(moved, ("y", "core"), axis=0)
    found, = call(
        functools.partial(weight_kernel, span),
        [((BR, MOST * dp, 3 * HALF), BF)],
        [moved, xc],
    )
    return grad_slots, grad_bias[0], found.transpose(1, 0, 2)


def solution(mesh):
    devices = mesh.devices
    dp, tensor = devices.shape
    if dp == 64:
        shape = (16, 4, 4, 2)
    else:
        shape = (dp // 4, 4, tensor // 2, 2)
    fine = Mesh(devices.reshape(shape), ("z", "x", "y", "core"))
    rows, cols = ("z", "x"), ("y", "core")
    in_specs = (P(rows, cols), P(), P(rows, cols), P(rows), P(rows, None), P(rows, None))
    out_specs = (P(rows, cols), P(rows), P(rows, None, cols))
    return jax.shard_map(body, mesh=fine, in_specs=in_specs, out_specs=out_specs, check_vma=False)
```

time: 704 us -> 219 us (0.31)
  blocking collectives: 412 us -> 110 us
  waiting for transfers between devices: 156 us -> 56.6 us
  other arithmetic: 46.2 us -> 0.08 us
  starting transfers between devices: 34.2 us -> 16.3 us
  Pallas kernels: 0 us -> 17.9 us
  between operations: 14.9 us -> 0.74 us
  local copies, waits for them, and re-layouts: 26.8 us -> 13.5 us
  matrix products: 11.8 us -> 0 us
    unnamed x1 -> x0, blocking collectives: 412 us -> none
    all_gather x1 -> x0, waiting for transfers between devices: 88.5 us -> none  [body(): all_rows = lax.all_gather(x_slots, 'dp', axis=0, tiled=True)]
    all_to_all x0 -> x2, blocking collectives: none -> 83.8 us  [the longest x1 51.4 us: body(): along_z = lax.all_to_all(packed, 'z', 0, 0, tiled=True)]
    psum x1 -> x0, waiting for transfers between devices: 67.3 us -> none  [body(): lax.psum(partial_pre.astype(jnp.bfloat16), 'tensor').astype(jnp.float32)]
    all_to_all x2 -> x3, waiting for transfers between devices: 0.01 us -> 56.6 us  [the longest x1 29.6 us: body(): lax.all_to_all(summed.reshape(nz, 16, 2 * HALF + 128), 'z', 0, 0, tiled=T...]
    convert_element_type x2 -> x1, other arithmetic: 35.8 us -> 0.01 us  [body(): counts = counts.astype(F32)]
    all_gather x0 -> x2, blocking collectives: none -> 26.1 us  [the longest x1 13.3 us: body(): moved = lax.all_gather(moved, ('y', 'core'), axis=0)]
    pallas_call x0 -> x9, Pallas kernels: none -> 17.9 us  [call(): pl.pallas_call(kernel, out_shape=[jax.ShapeDtypeStruct(s, d) for s, d in...]
  transfers between devices with their start and end apart: 4 -> 3, of which waited for: 2 -> 3; matrix products, arithmetic and copies ran while one was open for 9% -> 0% of each run, Pallas kernels for 0% -> 1%
where the time goes in v1:
time: 219 us; the launch traced here: 215 us
  blocking collectives  110 us (50%)
  waiting for transfers between devices  56.6 us (26%)
  Pallas kernels  17.9 us (8%)
  starting transfers between devices  16.3 us (7%)
  local copies, waits for them, and re-layouts  13.5 us (6%)
    all_to_all x1, blocking collectives, body(): along_z = lax.all_to_all(packed, 'z', 0, 0, tiled=True)  51.4 us
    all_to_all x1, blocking collectives, body(): lax.all_to_all(px.reshape(nx, nz * 16, 2 * HALF + 128), 'x', 0, 0, tiled=...  32.4 us
    all_to_all x1, waiting for transfers between devices, body(): lax.all_to_all(summed.reshape(nz, 16, 2 * HALF + 128), 'z', 0, 0, tiled=T...  29.6 us
    all_to_all x1, waiting for transfers between devices, body(): along_x = lax.all_to_all(spread, 'x', 0, 0, tiled=True)  21.3 us
    pallas_call x9, Pallas kernels, call(): pl.pallas_call(kernel, out_shape=[jax.ShapeDtypeStruct(s, d) for s, d in...  17.9 us
    all_gather x1, blocking collectives, body(): moved = lax.all_gather(moved, ('y', 'core'), axis=0)  13.3 us
    all_gather x1, blocking collectives, body(): grad = lax.all_gather(low, ('y', 'core'), axis=0, tiled=True)  12.9 us
    unnamed x32, local copies, waits for them, and re-layouts  12.8 us
  transfers between devices with their start and end apart: 3, of which 3 were waited for; matrix products, arithmetic and copies ran while one was open for 0% of the time, Pallas kernels for 1%

profile of v1, /device:TPU:24, one launch (start us, length us, event | category | flops | bytes accessed | tf_op | source)
XLA Modules:
  0.0 215.2 jit_solution(7793695118171666773)
XLA Ops:
  0.6 0.0 copy-start.8
  0.6 1.1 copy-done.8
  1.8 0.0 copy-start.12
  1.8 0.8 copy-done.12
  2.6 0.4 shard_map.85
  3.0 51.4 %all_to_all.25 = bf16[16,16,1280]{2,1,0:T(8,128)(2,1)S(1)} all-to-all(bf16[16,16,1280]{2,1,0:T(8,128)(2,1)S(1)} %shard_map.85), channel_id=1, replica_groups=mesh['z'=16,'x'=4,'y'=4,'core'=2] {'z'}, dimensions={0} | all-to-all | bytes 1310720 | tf_op jit(solution)/shard_map/all_to_all | solution.py:263
  54.4 0.2 shard_map.86
  54.6 0.0 copy-start
  54.6 1.4 copy-done
  56.0 0.0 copy-start.14
  56.0 0.0 copy-start.1
  56.0 4.4 %all-to-all-start.1 = ((bf16[4,256,1152]{2,1,0:T(8,128)(2,1)}), bf16[4,256,1152]{2,1,0:T(8,128)(2,1)S(1)}, u32[]{:S(2)}, u32[]{:S(2)}) async-start(bf16[4,256,1152]{2,1,0:T(8,128)(2,1)} %copy-done), calls=%async_computation.1 | async-start | bytes 4718592 | tf_op jit(solution)/shard_map/all_to_all | solution.py:269
  60.4 0.0 copy-done.14
  60.4 0.1 broadcast_in_dim.16.col_ref
  60.5 2.1 shard_map.87
  62.7 0.0 copy-start.2
  62.7 1.4 copy-done.2
  64.1 0.0 copy-start.4
  64.1 1.4 copy-done.4
  65.5 21.3 %all-to-all-done.1 = bf16[4,256,1152]{2,1,0:T(8,128)(2,1)S(1)} async-done(((bf16[4,256,1152]{2,1,0:T(8,128)(2,1)}), bf16[4,256,1152]{2,1,0:T(8,128)(2,1)S(1)}, u32[]{:S(2)}, u32[]{:S(2)}) %all-to-all-start.1) | async-done | bytes 2359328 | tf_op jit(solution)/shard_map/all_to_all | solution.py:269
  86.8 0.0 copy-done.1
  86.8 1.7 copy-done.3
  88.5 0.0 copy-start.13
  88.5 2.7 %shard_map.88 = (bf16[384,1536]{1,0:T(8,128)(2,1)S(1)}, f32[48,384]{1,0:T(8,128)S(1)}, bf16[384,384]{1,0:T(8,128)(2,1)S(1)}) custom-call(s32[1]{0:T(128)} %bitcast.2.place, bf16[1024,1152]{1,0:T(8,128)(2,1)S(1)} %bitcast.12, bf16[3,384,1024]{2,1,0:T(8,128)(2,1)S(1)} %copy-done.3, bf16[384,1536]{1,0:T(8,128)(2,1)S(1)} %copy-done.1), custom_call_target="tpu_custom_call" | custom-call | tf_op jit(solution)/shard_map/pallas_call | solution.py:38
  91.2 0.0 copy-start.6
  91.2 1.0 copy-done.6
  92.2 0.7 copy-done.9
  92.9 0.6 copy-done.10
  93.6 4.7 %all-to-all-start.2 = ((bf16[8,48,384]{2,1,0:T(8,128)(2,1)}), bf16[8,48,384]{2,1,0:T(8,128)(2,1)S(1)}, u32[]{:S(2)}, u32[]{:S(2)}) async-start(bf16[8,48,384]{2,1,0:T(8,128)(2,1)} %bitcast.16), calls=%async_computation.2 | async-start | bytes 589824 | tf_op jit(solution)/shard_map/all_to_all | solution.py:276
  98.2 0.1 pad_add_fusion.place
  98.3 0.0 copy-done.13
  98.3 0.0 copy-done.15
  98.3 5.7 %all-to-all-done.2.parts_ref = bf16[8,48,384]{2,1,0:T(8,128)(2,1)S(1)} async-done(((bf16[8,48,384]{2,1,0:T(8,128)(2,1)}), bf16[8,48,384]{2,1,0:T(8,128)(2,1)S(1)}, u32[]{:S(2)}, u32[]{:S(2)}) %all-to-all-start.2) | async-done | bytes 294944 | tf_op jit(solution)/shard_map/all_to_all | solution.py:276
  104.1 0.9 copy-done.11
  105.0 0.2 shard_map.89
  105.2 12.9 %all_gather.9.g_ref = bf16[384,384]{1,0:T(8,128)(2,1)S(1)} all-gather(bf16[48,384]{1,0:T(8,128)(2,1)S(1)} %shard_map.89), channel_id=1, replica_groups=mesh['z'=16,'x'=4,'y'=4,'core'=2] {'y','core'}, dimensions={0}, use_global_device_ids=true | all-gather | bytes 331776 | tf_op jit(solution)/shard_map/all_gather | solution.py:283
  118.1 0.1 broadcast_in_dim.19.oc_ref
  118.1 1.7 copy-done.5
  119.8 5.8 %shard_map.90 = (bf16[1024,1152]{1,0:T(8,128)(2,1)S(1)}, f32[8,384]{1,0:T(8,128)S(1)}) custom-call(s32[2]{0:T(128)S(1)} %pad_add_fusion.place, bf16[384,384]{1,0:T(8,128)(2,1)S(1)} %all_gather.9.g_ref, bf16[3,1024,384]{2,1,0:T(8,128)(2,1)S(1)} %copy-done.5, bf16[384,1536]{1,0:T(8,128)(2,1)S(1)} %copy-done.1, f32[64,128]{1,0:T(8,128)S(1)} %broadcast_in_dim.19.oc_ref, ...), custom_call_target="tpu_custom_call" | custom-call | tf_op jit(solution)/shard_map/pallas_call | solution.py:38
  125.7 32.4 %all_to_all.26.in_ref = bf16[4,256,1152]{2,1,0:T(8,128)(2,1)S(1)} all-to-all(bf16[4,256,1152]{2,1,0:T(8,128)(2,1)S(1)} %bitcast.14), channel_id=1, replica_groups=mesh['z'=16,'x'=4,'y'=4,'core'=2] {'x'}, dimensions={0} | all-to-all | bytes 4718592 | tf_op jit(solution)/shard_map/all_to_all | solution.py:299
  158.1 1.1 shard_map.91
  159.2 7.2 %all-to-all-start.4 = ((bf16[16,16,1152]{2,1,0:T(8,128)(2,1)}), bf16[16,16,1152]{2,1,0:T(8,128)(2,1)S(1)}, u32[]{:S(2)}, u32[]{:S(2)}) async-start(bf16[16,16,1152]{2,1,0:T(8,128)(2,1)} %bitcast.8), calls=%async_computation.4 | async-start | bytes 1179648 | tf_op jit(solution)/shard_map/all_to_all | solution.py:301
  166.4 0.6 slice_reduce_fusion
  167.0 29.6 %all-to-all-done.4.in_ref = bf16[16,16,1152]{2,1,0:T(8,128)(2,1)S(1)} async-done(((bf16[16,16,1152]{2,1,0:T(8,128)(2,1)}), bf16[16,16,1152]{2,1,0:T(8,128)(2,1)S(1)}, u32[]{:S(2)}, u32[]{:S(2)}) %all-to-all-start.4) | async-done | bytes 589856 | tf_op jit(solution)/shard_map/all_to_all | solution.py:301
  196.6 0.8 shard_map.92
  197.4 13.3 %all-gather = bf16[2048,128]{1,0:T(8,128)(2,1)S(1)} all-gather(bf16[256,128]{1,0:T(8,128)(2,1)S(1)} %get-tuple-element.19), channel_id=2, replica_groups=mesh['z'=16,'x'=4,'y'=4,'core'=2] {'y','core'}, dimensions={0}, use_global_device_ids=true | all-gather | bytes 589824 | tf_op jit(solution)/shard_map/all_gather | solution.py:305
  210.7 0.0 copy-done.7
  210.7 4.5 %shard_map.93 = bf16[6,128,1536]{2,1,0:T(8,128)(2,1)} custom-call(bf16[8,256,128]{2,1,0:T(8,128)(2,1)S(1)} %bitcast.15, bf16[384,1536]{1,0:T(8,128)(2,1)S(1)} %copy-done.7), custom_call_target="tpu_custom_call" | custom-call | tf_op jit(solution)/shard_map/pallas_call | solution.py:38
  (12 shorter events, 0.0 us)
Async XLA Ops:
  0.6 1.1 copy-start.8
  1.8 0.8 copy-start.12
  54.6 1.4 copy-start
  56.0 4.4 %copy-start.14 = (s32[64]{0:T(128)S(1)}, s32[64]{0:T(128)}, u32[]{:S(2)}) copy-start(s32[64]{0:T(128)} %param.7) | copy-start | bytes 772
  56.0 30.8 %copy-start.1 = (bf16[384,1536]{1,0:T(8,128)(2,1)S(1)}, bf16[384,1536]{1,0:T(8,128)(2,1)}, u32[]{:S(2)}) copy-start(bf16[384,1536]{1,0:T(8,128)(2,1)} %w_ref.3) | copy-start | bytes 3538948
  56.0 30.8 %all-to-all-start.1 = ((bf16[4,256,1152]{2,1,0:T(8,128)(2,1)}), bf16[4,256,1152]{2,1,0:T(8,128)(2,1)S(1)}, u32[]{:S(2)}, u32[]{:S(2)}) async-start(bf16[4,256,1152]{2,1,0:T(8,128)(2,1)} %copy-done), calls=%async_computation.1 | async-start | bytes 4718592 | tf_op jit(solution)/shard_map/all_to_all | solution.py:269
  62.7 1.4 copy-start.2
  64.1 1.4 copy-start.4
  86.8 1.7 copy-start.3
  88.5 9.8 %copy-start.13 = (f32[384]{0:T(512)S(1)}, f32[384]{0:T(512)}, u32[]{:S(2)}) copy-start(f32[384]{0:T(512)} %param.9) | copy-start | bytes 4612
  88.5 9.8 %copy-start.15 = (s32[64,1]{0,1:T(1,128)S(1)}, s32[64,1]{0,1:T(1,128)}, u32[]{:S(2)}) copy-start(s32[64,1]{0,1:T(1,128)} %param.11) | copy-start | bytes 772
  91.2 1.0 copy-start.6
  92.2 0.7 copy-start.9
  92.9 0.6 copy-start.10
  93.6 10.5 %all-to-all-start.2 = ((bf16[8,48,384]{2,1,0:T(8,128)(2,1)}), bf16[8,48,384]{2,1,0:T(8,128)(2,1)S(1)}, u32[]{:S(2)}, u32[]{:S(2)}) async-start(bf16[8,48,384]{2,1,0:T(8,128)(2,1)} %bitcast.16), calls=%async_computation.2 | async-start | bytes 589824 | tf_op jit(solution)/shard_map/all_to_all | solution.py:276
  104.1 0.9 copy-start.11
  118.1 1.7 copy-start.5
  158.1 52.6 %copy-start.7 = (bf16[384,1536]{1,0:T(8,128)(2,1)S(1)}, bf16[384,1536]{1,0:T(8,128)(2,1)}, u32[]{:S(2)}) copy-start(bf16[384,1536]{1,0:T(8,128)(2,1)} %copy-done.6) | copy-start | bytes 3538948
  159.2 37.4 %all-to-all-start.4 = ((bf16[16,16,1152]{2,1,0:T(8,128)(2,1)}), bf16[16,16,1152]{2,1,0:T(8,128)(2,1)S(1)}, u32[]{:S(2)}, u32[]{:S(2)}) async-start(bf16[16,16,1152]{2,1,0:T(8,128)(2,1)} %bitcast.8), calls=%async_computation.4 | async-start | bytes 1179648 | tf_op jit(solution)/shard_map/all_to_all | solution.py:301

commit v2 on v0

v2 whole, which is shorter than its diff:
```python
import functools

import jax
import jax.numpy as jnp
from jax import lax
from jax.experimental import pallas as pl
from jax.experimental.pallas import tpu as pltpu
from jax.sharding import Mesh, PartitionSpec as P

BF, F32, I32 = jnp.bfloat16, jnp.float32, jnp.int32
MOST = 2
BR = 6
SLOTS = 10
HALF = 512
NZ, NX, NT = 16, 4, 8
DP = NZ * NX
HID = 384
GROUP = NX * HID
SHARE = GROUP // NT
QUARTER = SHARE // 4
MAIN, TAIL = NZ * 8, NZ * 2
RHO = NZ * 16
PACK = SHARE + QUARTER
LIMIT = 48 * 1024 * 1024


def iota(shape, dim):
    return lax.broadcasted_iota(I32, shape, dim)


def onehot(mask):
    return jnp.where(mask, 1.0, 0.0).astype(BF)


def dot(a, b):
    return jnp.dot(a, b, preferred_element_type=F32)


def dot_nt(a, b):
    return lax.dot_general(a, b, (((1,), (1,)), ((), ())), preferred_element_type=F32)


def call(kernel, outs, args, scalars=0, scratch=(), flops=0, moved=0):
    specs = [pl.BlockSpec(memory_space=pltpu.SMEM)] * scalars
    specs += [pl.BlockSpec(memory_space=pltpu.VMEM)] * (len(args) - scalars)
    return pl.pallas_call(
        kernel,
        out_shape=[jax.ShapeDtypeStruct(s, d) for s, d in outs],
        in_specs=specs,
        out_specs=[pl.BlockSpec(memory_space=pltpu.VMEM)] * len(outs),
        scratch_shapes=list(scratch),
        compiler_params=pltpu.CompilerParams(vmem_limit_bytes=LIMIT),
        cost_estimate=pl.CostEstimate(flops=flops, bytes_accessed=moved, transcendentals=0),
    )(*args)


def pack_kernel(place, x_ref, up_ref, out_ref, rows, ups):
    rows[...] = jnp.zeros_like(rows)
    rows[0:SLOTS, :] = x_ref[...]
    ups[...] = jnp.zeros_like(ups)
    for z in range(NZ):
        ups[z * 16 : z * 16 + SLOTS, :] = up_ref[:, z * GROUP : (z + 1) * GROUP]
    k, lane = iota((GROUP, 256), 0), iota((GROUP, 256), 1)
    chosen = dot(ups[...], onehot((k == place[0] * SHARE + lane) & (lane < SHARE))).astype(BF)
    r, c = iota((16, 16), 0), iota((16, 16), 1)
    same = onehot((r == c) & (r < SLOTS))
    even = onehot(c == 2 * (r - SLOTS))
    odd = onehot(c == 2 * (r - SLOTS) + 1)
    a, b, last = rows[:, :HALF], rows[:, HALF : 2 * HALF], rows[:, 2 * HALF :]
    left = (dot(same, a) + dot(even, last)).astype(BF)
    right = (dot(same, b) + dot(odd, last)).astype(BF)
    for z in range(NZ):
        out_ref[z, :, :HALF] = left
        out_ref[z, :, HALF : 2 * HALF] = right
        out_ref[z, :, 2 * HALF :] = chosen[z * 16 : z * 16 + 16]


def slot_of(i):
    tail = (i - MAIN) % TAIL
    return jnp.where(i < MAIN, i // 8, tail // 2), jnp.where(i < MAIN, i % 8, 8 + tail % 2)


def selector(third, flip=False):
    i, rho = iota((256, RHO), 1 if flip else 0), iota((256, RHO), 0 if flip else 1)
    z, slot = slot_of(i)
    if third == 0:
        return onehot(rho == z * 16 + slot)
    return onehot((rho == z * 16 + SLOTS + slot // 2) & (slot % 2 == third - 1))


def by_quarter(pieces):
    lane = iota((QUARTER, 128), 1) // 32
    found = jnp.where(lane == 0, pieces[0], 0.0)
    for g in range(1, 4):
        found = jnp.where(lane == g, pieces[g], found)
    return found


def rows_kernel(rz_ref, x_ref, ug_ref):
    left, right = rz_ref[:, :HALF], rz_ref[:, HALF : 2 * HALF]
    first = selector(0)
    x_ref[:, :HALF] = dot(first, left).astype(BF)
    x_ref[:, HALF : 2 * HALF] = dot(first, right).astype(BF)
    x_ref[:, 2 * HALF :] = (dot(selector(1), left) + dot(selector(2), right)).astype(BF)
    ups = dot(first, rz_ref[:, 2 * HALF :])
    main, tail = ups[:MAIN].T, ups[MAIN:].T
    ug_ref[:SHARE, :] = main[:SHARE]
    ug_ref[SHARE:, :] = by_quarter([tail[g * QUARTER : (g + 1) * QUARTER] for g in range(4)])


def pre_kernel(w_ref, x_ref, out_ref):
    x = x_ref[...]
    for j in range(NT):
        found = dot_nt(w_ref[j * SHARE : (j + 1) * SHARE, :], x)
        out_ref[j, :SHARE, :] = found[:, :MAIN].astype(BF)
        tail = [found[g * QUARTER : (g + 1) * QUARTER, MAIN:] for g in range(4)]
        out_ref[j, SHARE:, :] = by_quarter(tail).astype(BF)


def gelu_slope(values):
    inner_arg = 0.7978845608 * (values + 0.044715 * values * values * values)
    tangent = jnp.tanh(inner_arg)
    return 0.5 * (1.0 + tangent) + 0.5 * values * (1.0 - tangent * tangent) * 0.7978845608 * (
        1.0 + 3.0 * 0.044715 * values * values
    )


def grad_kernel(place, parts_ref, ug_ref, side_ref, counts_ref, out_ref):
    tensor, x_me = place[0], place[1]
    side = side_ref[tensor // 2]
    bias = jnp.concatenate([side[1:2], side[2:3], side[3:4]], axis=1)
    wanted = iota((SHARE, HID), 1) == (tensor % 2) * SHARE + iota((SHARE, HID), 0)
    bias = jnp.sum(jnp.where(wanted, bias, 0.0), axis=1, keepdims=True)
    counts = counts_ref[...].astype(BF)
    s = iota((DP, 128), 0)
    lane = iota((DP, 128), 1)
    many = dot(counts, onehot(s == lane // 8 * NX + x_me))[0:1]
    few = dot(counts, onehot(s == lane % TAIL // 2 * NX + x_me))[0:1]
    lane = iota((1, 128), 1)
    many = (lane % 8).astype(F32) < many
    few = (8 + lane % 2).astype(F32) < few
    pre = parts_ref[0].astype(F32)
    for j in range(1, NT):
        pre = pre + parts_ref[j].astype(F32)
    tail_bias = by_quarter([bias[g * QUARTER : (g + 1) * QUARTER] for g in range(4)])
    main = jnp.where(many, ug_ref[:SHARE] * gelu_slope(pre[:SHARE] + bias), 0.0)
    tail = jnp.where(few, ug_ref[SHARE:] * gelu_slope(pre[SHARE:] + tail_bias), 0.0)
    out_ref[:SHARE, :] = main.astype(BF)
    out_ref[SHARE:PACK, :] = tail.astype(BF)
    lane = iota((QUARTER, 128), 1) // 32
    total = jnp.sum(main, axis=1, keepdims=True) + jnp.concatenate(
        [jnp.sum(jnp.where(lane == g, tail, 0.0), axis=1, keepdims=True) for g in range(4)], axis=0
    )
    high = total.astype(BF).astype(F32)
    mid = (total - high).astype(BF).astype(F32)
    low = total - high - mid
    lane = iota((SHARE, 128), 1)
    pieces = jnp.where(lane == 0, high, jnp.where(lane == 1, mid, jnp.where(lane == 2, low, 0.0)))
    pieces = jnp.concatenate([pieces, jnp.zeros((256 - SHARE, 128), F32)], axis=0).T
    out_ref[PACK : PACK + 16, :] = pieces[:16, :128].astype(BF)
    out_ref[PACK + 16 :, :] = pieces[:16, 128:].astype(BF)


def unpacked(tail):
    lane = iota((QUARTER, 128), 1) // 32
    zero = jnp.zeros((), BF)
    return jnp.concatenate([jnp.where(lane == g, tail, zero) for g in range(4)], axis=0)


def moved_kernel(place, g_ref, side_ref, out_ref):
    tensor, x_me = place[0], place[1]
    old, m = tensor // 2, tensor % 2
    blocks = HID // BR
    owner = side_ref[old][0:1, :blocks]
    r, c = iota((blocks, blocks), 0), iota((blocks, blocks), 1)
    column = jnp.sum(jnp.where(r == c, owner, 0.0), axis=1, keepdims=True)
    rank = jnp.sum(jnp.where((column == owner) & (r < c), 1.0, 0.0), axis=0, keepdims=True)
    target = jnp.broadcast_to(owner * MOST + rank, (8, blocks)).astype(BF)
    block, unit = iota((blocks, HID), 0), iota((blocks, HID), 1)
    within = unit - block * BR
    member = (within >= 0) & (within < BR)
    offset = jnp.sum(jnp.where(member, within, 0).astype(F32), axis=0, keepdims=True)
    key = dot(target, onehot(member))[0:1] * BR + offset
    both = [g_ref[2 * old], g_ref[2 * old + 1]]
    main = jnp.concatenate([g[:SHARE] for g in both], axis=0)
    tail = jnp.concatenate([unpacked(g[SHARE:PACK]) for g in both], axis=0)
    r, c = iota((128, 128), 0), iota((128, 128), 1)
    tail = dot(tail, onehot((r % TAIL == c % TAIL) & (c // TAIL == x_me))).astype(BF)
    i = iota((BR * NZ, 1), 0)
    for x in range(NX):
        wanted = (((i % NZ) * NX + x) * MOST + m) * BR + i // NZ
        pick = onehot(wanted.astype(F32) == key)
        out_ref[x, : BR * NZ, :] = dot(pick, main).astype(BF)
        out_ref[x, BR * NZ : 2 * BR * NZ, :] = dot(pick, tail).astype(BF)
        out_ref[x, 2 * BR * NZ : 2 * BR * NZ + 32, :] = g_ref[2 * x, PACK:, :]
        out_ref[x, 2 * BR * NZ + 32 :, :] = g_ref[2 * x + 1, PACK:, :]


def out_kernel(g_ref, w_ref, px_ref, full):
    for j in range(NT):
        full[j * SHARE : (j + 1) * SHARE, :MAIN] = g_ref[j, :SHARE, :]
        full[j * SHARE : (j + 1) * SHARE, MAIN:] = unpacked(g_ref[j, SHARE:PACK, :])
    g = full[...]
    here = [dot_nt(selector(i, True), g).astype(BF) for i in range(3)]
    last = w_ref[:, 2 * HALF :]
    px_ref[:, :HALF] = (dot(here[0], w_ref[:, :HALF]) + dot(here[1], last)).astype(BF)
    px_ref[:, HALF:] = (dot(here[0], w_ref[:, HALF : 2 * HALF]) + dot(here[2], last)).astype(BF)


def join_kernel(px_ref, rx_ref, out_ref, bias_ref):
    out_ref[:, : 2 * HALF] = px_ref[...]
    n = BR * NZ
    rho, k = iota((RHO, 2 * n), 0), iota((RHO, 2 * n), 1)
    z, row = rho // 16, rho % 16
    main = k < n
    k = jnp.where(main, k, k - n)
    b = k // NZ
    here = z == k % NZ
    tiles = [jnp.zeros((RHO, 128), F32), jnp.zeros((RHO, 128), F32)]
    for x in range(NX):
        value = rx_ref[x, : 2 * n, :]
        v = jnp.where(main, x * BR + b, 24 + b)
        for t in range(2):
            tiles[t] = tiles[t] + dot(onehot(here & (v == t * 16 + row)), value)
    out_ref[:, 2 * HALF : 2 * HALF + 128] = tiles[0].astype(BF)
    out_ref[:, 2 * HALF + 128 :] = tiles[1].astype(BF)
    for i in range(4):
        total = jnp.zeros((16, 128), F32)
        for x in range(NX):
            total = total + rx_ref[x, 2 * n + 16 * i : 2 * n + 16 * (i + 1), :].astype(F32)
        bias_ref[i : i + 1, :] = total[2:3] + total[1:2] + total[0:1]


def slots_kernel(in_ref, out_ref, moved_ref):
    total = in_ref[0, :, : 2 * HALF].astype(F32)
    for z in range(1, NZ):
        total = total + in_ref[z, :, : 2 * HALF].astype(F32)
    total = total.astype(BF)
    left, right = total[:, :HALF], total[:, HALF:]
    r, c = iota((16, 16), 0), iota((16, 16), 1)
    halfway = (c - SLOTS) * 2
    last = dot(onehot(r == halfway), left) + dot(onehot(r == halfway + 1), right)
    out_ref[:, : 2 * HALF] = total[:SLOTS]
    out_ref[:, 2 * HALF :] = last[:SLOTS].astype(BF)
    for z in range(NZ):
        moved_ref[z * 16 : (z + 1) * 16, :] = in_ref[z, :, 2 * HALF :]


def weight_kernel(m_ref, x_ref, out_ref, found, tails):
    n = BR * NZ
    i, k = iota((n, 2 * RHO), 0), iota((n, 2 * RHO), 1)
    b, here = i // NZ, i % NZ == (k % RHO) // 16
    place = (k // RHO) * 16 + k % 16
    picks = [onehot(here & (place == (x * BR + b if x < NX else 24 + b))) for x in range(NX + 1)]
    for j in range(NT):
        both = jnp.concatenate([m_ref[j, :, :128], m_ref[j, :, 128:]], axis=0)
        for x in range(NX + 1):
            found[j * n : (j + 1) * n, x * 128 : (x + 1) * 128] = dot(picks[x], both).astype(BF)
    r, c = iota((NT * n, NT * n), 0), iota((NT * n, NT * n), 1)
    order = onehot(c == (r % NT) * n + r // NT)
    rows = dot(order, found[...]).astype(BF)
    for x in range(NX):
        tails[x * TAIL : (x + 1) * TAIL, :] = x_ref[x, MAIN:, :]
    for b in range(BR):
        mine = rows[b * MOST * DP : (b + 1) * MOST * DP]
        total = dot(mine[:, NX * 128 :], tails[...])
        for x in range(NX):
            total = total + dot(mine[:, x * 128 : (x + 1) * 128], x_ref[x, :MAIN, :])
        out_ref[b] = total.astype(BF)


def body(x_slots, counts, w, bias, upstream, owners):
    tensor = lax.axis_index(("y", "core")).astype(I32)
    x_me = lax.axis_index("x").astype(I32)
    place = jnp.stack([tensor, x_me])
    groups = lax.all_gather(w, "x", axis=0, tiled=True)
    owner = jnp.pad(owners[:, 0].astype(F32), (0, 128 - DP))
    side = jnp.concatenate([owner[None], bias.reshape(3, 128), jnp.zeros((4, 128), F32)], axis=0)
    side = lax.all_to_all(jnp.broadcast_to(side, (NX, 8, 128)), "x", 0, 0, tiled=True)
    packed, = call(
        pack_kernel,
        [((NZ, 16, 2 * HALF + 256), BF)],
        [place, x_slots, upstream],
        1,
        [pltpu.VMEM((16, 3 * HALF), BF), pltpu.VMEM((RHO, GROUP), BF)],
        2 * RHO * GROUP * 256,
        2 * 10**6,
    )
    along_z = lax.all_to_all(packed, "z", 0, 0, tiled=True)
    rows, ug = call(
        rows_kernel,
        [((256, 3 * HALF), BF), ((PACK, 128), F32)],
        [along_z.reshape(RHO, 2 * HALF + 256)],
        flops=2 * 256 * 256 * 9 * 256,
        moved=2 * 10**6,
    )
    columns = lax.all_gather(rows[: MAIN + TAIL], "x", axis=0)
    part, = call(
        pre_kernel,
        [((NT, PACK, 128), BF)],
        [groups, rows],
        flops=2 * GROUP * 256 * 3 * HALF,
        moved=6 * 10**6,
    )
    parts = lax.all_to_all(part, ("y", "core"), 0, 0, tiled=True)
    low, = call(
        grad_kernel,
        [((PACK + 32, 128), BF)],
        [place, parts, ug, side, jnp.broadcast_to(counts.astype(F32)[None, :], (8, DP))],
        1,
        moved=10**6,
    )
    grad = lax.all_gather(low, ("y", "core"), axis=0)
    sent, = call(
        moved_kernel,
        [((NX, 256, 128), BF)],
        [place, grad, side],
        1,
        flops=2 * 8 * 96 * HID * 128,
        moved=10**6,
    )
    rx = lax.all_to_all(sent, "x", 0, 0, tiled=True)
    px, = call(
        out_kernel,
        [((RHO, 2 * HALF), BF)],
        [grad, groups],
        0,
        [pltpu.VMEM((GROUP, 256), BF)],
        2 * RHO * GROUP * (4 * HALF + 3 * 256),
        6 * 10**6,
    )
    joined, grad_bias = call(
        join_kernel, [((RHO, 2 * HALF + 256), BF), ((4, 128), F32)], [px, rx], moved=2 * 10**6
    )
    pz = lax.all_to_all(joined.reshape(NZ, 16, 2 * HALF + 256), "z", 0, 0, tiled=True)
    grad_slots, moved = call(
        slots_kernel, [((SLOTS, 3 * HALF), BF), ((RHO, 256), BF)], [pz], moved=10**6
    )
    moved = lax.all_gather(moved, ("y", "core"), axis=0)
    found, = call(
        weight_kernel,
        [((BR, MOST * DP, 3 * HALF), BF)],
        [moved, columns],
        0,
        [pltpu.VMEM((NT * BR * NZ, 640), BF), pltpu.VMEM((NX * TAIL, 3 * HALF), BF)],
        2 * 768 * 640 * 1536,
        5 * 10**6,
    )
    rest = SHARE - 128
    grad_bias = jnp.concatenate([grad_bias[0], grad_bias[1, :rest], grad_bias[2], grad_bias[3, :rest]])
    return grad_slots, grad_bias, found.transpose(1, 0, 2)


def solution(mesh):
    fine = Mesh(mesh.devices.reshape(NZ, NX, NT // 2, 2), ("z", "x", "y", "core"))
    rows, cols = ("z", "x"), ("y", "core")
    in_specs = (P(rows, cols), P(), P(rows, cols), P(rows), P(rows, None), P(rows, None))
    out_specs = (P(rows, cols), P(rows), P(rows, None, cols))
    return jax.shard_map(body, mesh=fine, in_specs=in_specs, out_specs=out_specs, check_vma=False)
```

time: 704 us -> 214 us (0.30)
  blocking collectives: 412 us -> 61.5 us
  waiting for transfers between devices: 156 us -> 76.5 us
  other arithmetic: 46.2 us -> 0.81 us
  Pallas kernels: 0 us -> 18.5 us
  local copies, waits for them, and re-layouts: 26.8 us -> 10.9 us
  matrix products: 11.8 us -> 0 us
    unnamed x1 -> x0, blocking collectives: 412 us -> none
    psum x1 -> x0, waiting for transfers between devices: 67.3 us -> none  [body(): lax.psum(partial_pre.astype(jnp.bfloat16), 'tensor').astype(jnp.float32)]
    all_gather x1 -> x3, waiting for transfers between devices: 88.5 us -> 29.6 us  [the longest x1 20.8 us: body(): moved = lax.all_gather(moved, ('y', 'core'), axis=0)]
    all_to_all x0 -> x1, blocking collectives: none -> 48.4 us  [body(): lax.all_to_all(joined.reshape(NZ, 16, 2 * HALF + 256), 'z', 0, 0, tiled=T...]
    all_to_all x2 -> x4, waiting for transfers between devices: 0.01 us -> 46.1 us  [the longest x1 33.4 us: body(): along_z = lax.all_to_all(packed, 'z', 0, 0, tiled=True)]
    convert_element_type x2, other arithmetic: 35.8 us -> 0.01 us  [the longest x1 0.01 us: body(): counts.astype(F32)[None, :]]
    pallas_call x0 -> x9, Pallas kernels: none -> 18.5 us  [call(): pl.pallas_call(kernel, out_shape=[jax.ShapeDtypeStruct(s, d) for s, d in...]
    all_gather x0 -> x1, blocking collectives: none -> 13.1 us  [body(): grad = lax.all_gather(low, ('y', 'core'), axis=0)]
  transfers between devices with their start and end apart: 4 -> 7, of which waited for: 2 -> 5; matrix products, arithmetic and copies ran while one was open for 9% -> 1% of each run, Pallas kernels for 0% -> 6%
where the time goes in v2:
time: 214 us; the launch traced here: 210 us
  waiting for transfers between devices  76.5 us (36%)
  blocking collectives  61.5 us (29%)
  starting transfers between devices  27.9 us (13%)
  Pallas kernels  18.5 us (9%)
  between operations  13.9 us (6%)
  local copies, waits for them, and re-layouts  10.9 us (5%)
    all_to_all x1, blocking collectives, body(): lax.all_to_all(joined.reshape(NZ, 16, 2 * HALF + 256), 'z', 0, 0, tiled=T...  48.4 us
    all_to_all x1, waiting for transfers between devices, body(): along_z = lax.all_to_all(packed, 'z', 0, 0, tiled=True)  33.4 us
    all_gather x1, waiting for transfers between devices, body(): moved = lax.all_gather(moved, ('y', 'core'), axis=0)  20.8 us
    pallas_call x9, Pallas kernels, call(): pl.pallas_call(kernel, out_shape=[jax.ShapeDtypeStruct(s, d) for s, d in...  18.5 us
    all_to_all x1, starting transfers between devices, body(): along_z = lax.all_to_all(packed, 'z', 0, 0, tiled=True)  15.2 us
    all_gather x1, blocking collectives, body(): grad = lax.all_gather(low, ('y', 'core'), axis=0)  13.1 us
    unnamed x18, local copies, waits for them, and re-layouts  9.42 us
    all_gather x1, waiting for transfers between devices, body(): groups = lax.all_gather(w, 'x', axis=0, tiled=True)  8.8 us
  transfers between devices with their start and end apart: 7, of which 5 were waited for; matrix products, arithmetic and copies ran while one was open for 1% of the time, Pallas kernels for 6%

profile of v2, /device:TPU:24, one launch (start us, length us, event | category | flops | bytes accessed | tf_op | source)
XLA Modules:
  0.0 210.0 jit_solution(12096978835215935652)
XLA Ops:
  7.2 0.0 copy-start.7
  7.2 0.0 copy-start.6
  7.2 0.0 all-gather.7.cloned.1.call-start
  7.2 0.7 all-gather.7.cloned.1.call-update
  7.9 0.1 pad_add_fusion.place
  8.0 0.0 copy-start.2
  8.0 1.1 copy-done.2
  9.1 0.0 copy-start.3
  9.1 0.8 copy-done.3
  9.9 1.8 shard_map.85
  11.8 15.2 %all-to-all-start = ((bf16[16,16,1280]{2,1,0:T(8,128)(2,1)}), bf16[16,16,1280]{2,1,0:T(8,128)(2,1)S(1)}, u32[]{:S(2)}, u32[]{:S(2)}) async-start(bf16[16,16,1280]{2,1,0:T(8,128)(2,1)} %shard_map.85), calls=%async_computation | async-start | bytes 1310720 | tf_op jit(solution)/shard_map/all_to_all | solution.py:289
  27.0 0.1 pad.11.clone
  27.1 0.0 copy-done.7
  27.1 0.0 copy-done.6
  27.1 0.1 maximum_maximum_fusion
  27.2 33.4 %all-to-all-done = bf16[16,16,1280]{2,1,0:T(8,128)(2,1)S(1)} async-done(((bf16[16,16,1280]{2,1,0:T(8,128)(2,1)}), bf16[16,16,1280]{2,1,0:T(8,128)(2,1)S(1)}, u32[]{:S(2)}, u32[]{:S(2)}) %all-to-all-start) | async-done | bytes 655392 | tf_op jit(solution)/shard_map/all_to_all | solution.py:289
  60.5 0.6 broadcast_in_dim.17
  61.1 4.3 %all-to-all-start.2 = ((f32[4,8,128]{2,1,0:T(8,128)}), f32[4,8,128]{2,1,0:T(8,128)S(1)}, u32[]{:S(2)}, u32[]{:S(2)}) async-start(f32[4,8,128]{2,1,0:T(8,128)} %broadcast_in_dim.17), calls=%async_computation.2 | async-start | bytes 32768 | tf_op jit(solution)/shard_map/all_to_all | solution.py:279
  65.4 0.6 shard_map.86
  66.0 8.8 %all-gather.7.cloned.1.call-done.w_ref = bf16[1536,1536]{1,0:T(8,128)(2,1)} async-done(((bf16[384,1536]{1,0:T(8,128)(2,1)}), bf16[1536,1536]{1,0:T(8,128)(2,1)}) %all-gather.7.cloned.1.call-update) | async-done | bytes 4718608 | tf_op jit(solution)/shard_map/all_gather | solution.py:276
  74.8 0.0 copy-start
  74.8 2.3 %copy-done = bf16[1536,1536]{1,0:T(8,128)(2,1)S(1)} copy-done((bf16[1536,1536]{1,0:T(8,128)(2,1)S(1)}, bf16[1536,1536]{1,0:T(8,128)(2,1)}, u32[]{:S(2)}) %copy-start) | copy-done | bytes 4718616
  77.1 2.9 %shard_map.87 = bf16[8,240,128]{2,1,0:T(8,128)(2,1)} custom-call(bf16[1536,1536]{1,0:T(8,128)(2,1)S(1)} %copy-done, bf16[256,1536]{1,0:T(8,128)(2,1)S(1)} %get-tuple-element.9.x_ref), custom_call_target="tpu_custom_call" | custom-call | flops 1207959552 | bytes 6000000 | tf_op jit(solution)/shard_map/pallas_call | solution.py:46
  80.1 0.0 all-to-all-done.2.side_ref
  80.1 4.9 %all-to-all-start.1 = ((bf16[8,240,128]{2,1,0:T(8,128)(2,1)}), bf16[8,240,128]{2,1,0:T(8,128)(2,1)S(1)}, u32[]{:S(2)}, u32[]{:S(2)}) async-start(bf16[8,240,128]{2,1,0:T(8,128)(2,1)} %shard_map.87), calls=%async_computation.1 | async-start | bytes 983040 | tf_op jit(solution)/shard_map/all_to_all | solution.py:305
  85.0 0.0 all-gather.11.cloned.1.call-start
  85.0 0.8 slice.19
  85.8 0.0 all-gather.11.cloned.1.call-update
  85.9 0.0 copy-done.8
  85.9 7.1 %all-to-all-done.1.parts_ref = bf16[8,240,128]{2,1,0:T(8,128)(2,1)S(1)} async-done(((bf16[8,240,128]{2,1,0:T(8,128)(2,1)}), bf16[8,240,128]{2,1,0:T(8,128)(2,1)S(1)}, u32[]{:S(2)}, u32[]{:S(2)}) %all-to-all-start.1) | async-done | bytes 491552 | tf_op jit(solution)/shard_map/all_to_all | solution.py:305
  92.9 1.0 shard_map.88
  93.9 13.1 %all-gather = bf16[2176,128]{1,0:T(8,128)(2,1)S(1)} all-gather(bf16[272,128]{1,0:T(8,128)(2,1)S(1)} %shard_map.88), channel_id=2, replica_groups=mesh['z'=16,'x'=4,'y'=4,'core'=2] {'y','core'}, dimensions={0}, use_global_device_ids=true | all-gather | bytes 626688 | tf_op jit(solution)/shard_map/all_gather | solution.py:313
  107.1 1.8 shard_map.90
  108.9 3.4 %all-to-all-start.3 = ((bf16[4,256,128]{2,1,0:T(8,128)(2,1)}), bf16[4,256,128]{2,1,0:T(8,128)(2,1)S(1)}, u32[]{:S(2)}, u32[]{:S(2)}) async-start(bf16[4,256,128]{2,1,0:T(8,128)(2,1)} %shard_map.90), calls=%async_computation.3 | async-start | bytes 524288 | tf_op jit(solution)/shard_map/all_to_all | solution.py:322
  112.3 0.0 all-gather.9.cloned.1.call-start
  112.3 0.0 copy-start.1
  112.3 2.4 %copy-done.1 = bf16[1536,1536]{1,0:T(8,128)(2,1)S(1)} copy-done((bf16[1536,1536]{1,0:T(8,128)(2,1)S(1)}, bf16[1536,1536]{1,0:T(8,128)(2,1)}, u32[]{:S(2)}) %copy-start.1) | copy-done | bytes 4718616
  114.7 2.5 %shard_map.89.px_ref = bf16[256,1024]{1,0:T(8,128)(2,1)S(1)} custom-call(bf16[8,272,128]{2,1,0:T(8,128)(2,1)S(1)} %bitcast.22, bf16[1536,1536]{1,0:T(8,128)(2,1)S(1)} %copy-done.1), custom_call_target="tpu_custom_call" | custom-call | flops 2214592512 | bytes 6000000 | tf_op jit(solution)/shard_map/pallas_call | solution.py:46
  117.2 5.7 %all-to-all-done.3.rx_ref = bf16[4,256,128]{2,1,0:T(8,128)(2,1)S(1)} async-done(((bf16[4,256,128]{2,1,0:T(8,128)(2,1)}), bf16[4,256,128]{2,1,0:T(8,128)(2,1)S(1)}, u32[]{:S(2)}, u32[]{:S(2)}) %all-to-all-start.3) | async-done | bytes 262176 | tf_op jit(solution)/shard_map/all_to_all | solution.py:322
  122.9 0.4 shard_map.91
  123.4 48.4 %all_to_all.25.in_ref = bf16[16,16,1280]{2,1,0:T(8,128)(2,1)S(1)} all-to-all(bf16[16,16,1280]{2,1,0:T(8,128)(2,1)S(1)} %bitcast.24), channel_id=1, replica_groups=mesh['z'=16,'x'=4,'y'=4,'core'=2] {'z'}, dimensions={0} | all-to-all | bytes 1310720 | tf_op jit(solution)/shard_map/all_to_all | solution.py:335
  171.7 0.8 shard_map.92
  172.6 0.0 all-gather.9.cloned.1.call-update
  172.6 0.7 pad_maximum_fusion
  173.3 20.8 %all-gather.9.cloned.1.call-done = bf16[2048,256]{1,0:T(8,128)(2,1)} async-done(((bf16[256,256]{1,0:T(8,128)(2,1)}), bf16[2048,256]{1,0:T(8,128)(2,1)}) %all-gather.9.cloned.1.call-update) | async-done | bytes 1048592 | tf_op jit(solution)/shard_map/all_gather | solution.py:339
  194.1 1.5 copy-done.4
  195.6 1.2 copy-done.5
  196.9 6.6 %shard_map.93 = bf16[6,128,1536]{2,1,0:T(8,128)(2,1)} custom-call(bf16[8,256,256]{2,1,0:T(8,128)(2,1)S(1)} %bitcast.26, bf16[4,160,1536]{2,1,0:T(8,128)(2,1)S(1)} %bitcast.25), custom_call_target="tpu_custom_call" | custom-call | flops 1509949440 | bytes 5000000 | tf_op jit(solution)/shard_map/pallas_call | solution.py:46
  (11 shorter events, 0.0 us)
Async XLA Ops:
  7.2 19.9 %copy-start.7 = (s32[64,1]{0,1:T(1,128)S(1)}, s32[64,1]{0,1:T(1,128)}, u32[]{:S(2)}) copy-start(s32[64,1]{0,1:T(1,128)} %param.11) | copy-start | bytes 772
  7.2 19.9 %copy-start.6 = (f32[384]{0:T(512)S(1)}, f32[384]{0:T(512)}, u32[]{:S(2)}) copy-start(f32[384]{0:T(512)} %param.9) | copy-start | bytes 4612
  7.2 67.6 %all-gather.7.cloned.1.call-start = ((), (), s32[]{:S(2)}) async-start(), calls=%async_computation.5 | async-start | bytes 5898240 | tf_op jit(solution)/shard_map/all_gather | solution.py:276
  8.0 1.1 copy-start.2
  9.1 0.8 copy-start.3
  11.8 48.7 %all-to-all-start = ((bf16[16,16,1280]{2,1,0:T(8,128)(2,1)}), bf16[16,16,1280]{2,1,0:T(8,128)(2,1)S(1)}, u32[]{:S(2)}, u32[]{:S(2)}) async-start(bf16[16,16,1280]{2,1,0:T(8,128)(2,1)} %shard_map.85), calls=%async_computation | async-start | bytes 1310720 | tf_op jit(solution)/shard_map/all_to_all | solution.py:289
  61.1 19.0 %all-to-all-start.2 = ((f32[4,8,128]{2,1,0:T(8,128)}), f32[4,8,128]{2,1,0:T(8,128)S(1)}, u32[]{:S(2)}, u32[]{:S(2)}) async-start(f32[4,8,128]{2,1,0:T(8,128)} %broadcast_in_dim.17), calls=%async_computation.2 | async-start | bytes 32768 | tf_op jit(solution)/shard_map/all_to_all | solution.py:279
  74.8 2.3 %copy-start = (bf16[1536,1536]{1,0:T(8,128)(2,1)S(1)}, bf16[1536,1536]{1,0:T(8,128)(2,1)}, u32[]{:S(2)}) copy-start(bf16[1536,1536]{1,0:T(8,128)(2,1)} %all-gather.7.cloned.1.call-done.w_ref) | copy-start | bytes 14155780
  80.1 5.8 %copy-start.8 = (s32[64]{0:T(128)S(1)}, s32[64]{0:T(128)}, u32[]{:S(2)}) copy-start(s32[64]{0:T(128)} %param.7) | copy-start | bytes 772
  80.1 12.8 %all-to-all-start.1 = ((bf16[8,240,128]{2,1,0:T(8,128)(2,1)}), bf16[8,240,128]{2,1,0:T(8,128)(2,1)S(1)}, u32[]{:S(2)}, u32[]{:S(2)}) async-start(bf16[8,240,128]{2,1,0:T(8,128)(2,1)} %shard_map.87), calls=%async_computation.1 | async-start | bytes 983040 | tf_op jit(solution)/shard_map/all_to_all | solution.py:305
  85.0 88.3 %all-gather.11.cloned.1.call-start = ((), (), s32[]{:S(2)}) async-start(), calls=%async_computation.7 | async-start | bytes 2457600 | tf_op jit(solution)/shard_map/all_gather | solution.py:297
  108.9 14.0 %all-to-all-start.3 = ((bf16[4,256,128]{2,1,0:T(8,128)(2,1)}), bf16[4,256,128]{2,1,0:T(8,128)(2,1)S(1)}, u32[]{:S(2)}, u32[]{:S(2)}) async-start(bf16[4,256,128]{2,1,0:T(8,128)(2,1)} %shard_map.90), calls=%async_computation.3 | async-start | bytes 524288 | tf_op jit(solution)/shard_map/all_to_all | solution.py:322
  112.3 81.8 %all-gather.9.cloned.1.call-start = ((), (), s32[]{:S(2)}) async-start(), calls=%async_computation.6 | async-start | bytes 1179648 | tf_op jit(solution)/shard_map/all_gather | solution.py:339
  112.3 2.4 %copy-start.1 = (bf16[1536,1536]{1,0:T(8,128)(2,1)S(1)}, bf16[1536,1536]{1,0:T(8,128)(2,1)}, u32[]{:S(2)}) copy-start(bf16[1536,1536]{1,0:T(8,128)(2,1)} %all-gather.7.cloned.1.call-done.w_ref) | copy-start | bytes 14155780
  194.1 1.5 copy-start.4
  195.6 1.2 copy-start.5
Sparse Core Ops, SparseCore 0:
  10.1 64.6 all-gather.6
  87.9 40.7 all-gather.10
  172.7 21.3 all-gather.8

commit v3 on v2

v3 whole, which is shorter than its diff:
```python
import functools

import jax
import jax.numpy as jnp
from jax import lax
from jax.experimental import pallas as pl
from jax.experimental.pallas import tpu as pltpu
from jax.sharding import Mesh, PartitionSpec as P

BF, F32, I32 = jnp.bfloat16, jnp.float32, jnp.int32
MOST = 2
BR = 6
SLOTS = 10
HALF = 512
NZ, NX, NT = 16, 4, 8
DP = NZ * NX
HID = 384
GROUP = NX * HID
SHARE = GROUP // NT
QUARTER = SHARE // 4
MAIN, TAIL = NZ * 8, NZ * 2
RHO = NZ * 16
PACK = SHARE + QUARTER
SIDE = 16
FIRST = SIDE + SHARE
FULL = SIDE + HID
MOVED = (NX + 1) * BR
LIMIT = 24 * 1024 * 1024


def iota(shape, dim):
    return lax.broadcasted_iota(I32, shape, dim)


def onehot(mask):
    return jnp.where(mask, 1.0, 0.0).astype(BF)


def dot(a, b):
    return jnp.dot(a, b, preferred_element_type=F32)


def dot_nt(a, b):
    return lax.dot_general(a, b, (((1,), (1,)), ((), ())), preferred_element_type=F32)


VMEM, HBM, ANY, SMEM = pltpu.VMEM, pltpu.HBM, pl.ANY, pltpu.SMEM


def call(kernel, outs, args, scalars=0, scratch=(), flops=0, moved=0, outside=(), space=ANY, limit=LIMIT):
    specs = [
        pl.BlockSpec(memory_space=SMEM if i < scalars else space if i in outside else VMEM)
        for i in range(len(args))
    ]
    return pl.pallas_call(
        kernel,
        out_shape=[jax.ShapeDtypeStruct(s, d) for s, d in outs],
        in_specs=specs,
        out_specs=[pl.BlockSpec(memory_space=VMEM)] * len(outs),
        scratch_shapes=list(scratch),
        compiler_params=pltpu.CompilerParams(vmem_limit_bytes=limit),
        cost_estimate=pl.CostEstimate(flops=flops, bytes_accessed=moved, transcendentals=0),
    )(*args)


def pieces_of(value):
    high = value.astype(BF).astype(F32)
    mid = (value - high).astype(BF).astype(F32)
    return high, mid, value - high - mid


def pack_kernel(place, x_in, up_in, w_in, bias_in, owner_in, full_ref, out_ref, x_ref, up_ref, bias_ref, owner_ref, rows, ups, sems):
    copies = [
        pltpu.make_async_copy(source, target, sems.at[i])
        for i, (source, target) in enumerate(
            [
                (up_in, up_ref),
                (x_in, x_ref),
                (bias_in, bias_ref),
                (owner_in, owner_ref),
                (w_in, full_ref.at[pl.ds(SIDE, HID), :]),
            ]
        )
    ]
    for copy in copies:
        copy.start()
    k, lane = iota((GROUP, 256), 0), iota((GROUP, 256), 1)
    pick = onehot((k == place[0] * SHARE + lane) & (lane < SHARE))
    r, c = iota((16, 16), 0), iota((16, 16), 1)
    same = onehot((r == c) & (r < SLOTS))
    even = onehot(c == 2 * (r - SLOTS))
    odd = onehot(c == 2 * (r - SLOTS) + 1)
    rows[...] = jnp.zeros_like(rows)
    ups[...] = jnp.zeros_like(ups)
    copies[0].wait()
    for z in range(NZ):
        ups[z * 16 : z * 16 + SLOTS, :] = up_ref[:, z * GROUP : (z + 1) * GROUP]
    chosen = dot(ups[...], pick).astype(BF)
    copies[1].wait()
    rows[0:SLOTS, :] = x_ref[...]
    a, b, last = rows[:, :HALF], rows[:, HALF : 2 * HALF], rows[:, 2 * HALF :]
    left = (dot(same, a) + dot(even, last)).astype(BF)
    right = (dot(same, b) + dot(odd, last)).astype(BF)
    for z in range(NZ):
        out_ref[z, :, :HALF] = left
        out_ref[z, :, HALF : 2 * HALF] = right
        out_ref[z, :, 2 * HALF :] = chosen[z * 16 : z * 16 + 16]
    copies[2].wait()
    row = iota((SIDE, HID), 0)
    high, mid, low = pieces_of(bias_ref[...].reshape(1, HID))
    side = jnp.where(row == 1, high, jnp.where(row == 2, mid, jnp.where(row == 3, low, 0.0)))
    copies[3].wait()
    owner = jnp.where(iota((SIDE, DP), 0) == 0, owner_ref[...].astype(F32), 0.0).astype(BF)
    owner = dot(owner, onehot(iota((DP, HID), 0) == iota((DP, HID), 1)))
    full_ref[:SIDE, :HID] = (owner + side).astype(BF)
    full_ref[:SIDE, HID:] = jnp.zeros((SIDE, 3 * HALF - HID), BF)
    copies[4].wait()


def sum_rows(total):
    high, mid, low = pieces_of(total)
    lane = iota((SHARE, 128), 1)
    pieces = jnp.where(lane == 0, high, jnp.where(lane == 1, mid, jnp.where(lane == 2, low, 0.0)))
    pieces = jnp.concatenate([pieces, jnp.zeros((256 - SHARE, 128), F32)], axis=0).T[:16].astype(BF)
    r, c = iota((16, 16), 0), iota((16, 16), 1)
    shift = onehot(iota((128, 128), 0) + 64 == iota((128, 128), 1))
    rest = dot(pieces[:, 128:], shift).astype(BF)
    rows = dot(onehot((r == c + 12) & (c < 3)), pieces[:, :128]) + dot(onehot((r == c + 6) & (c < 3)), rest)
    return rows.astype(BF)


def slot_of(i):
    tail = (i - MAIN) % TAIL
    return jnp.where(i < MAIN, i // 8, tail // 2), jnp.where(i < MAIN, i % 8, 8 + tail % 2)


def selector(third, flip=False):
    i, rho = iota((256, RHO), 1 if flip else 0), iota((256, RHO), 0 if flip else 1)
    z, slot = slot_of(i)
    if third == 0:
        return onehot(rho == z * 16 + slot)
    return onehot((rho == z * 16 + SLOTS + slot // 2) & (slot % 2 == third - 1))


def by_quarter(pieces):
    lane = iota((QUARTER, 128), 1) // 32
    found = jnp.where(lane == 0, pieces[0], 0.0)
    for g in range(1, 4):
        found = jnp.where(lane == g, pieces[g], found)
    return found


def rows_kernel(rz_ref, x_ref, column_ref, ug_ref):
    left, right = rz_ref[:, :HALF], rz_ref[:, HALF : 2 * HALF]
    first = selector(0)
    x_ref[:, :HALF] = dot(first, left).astype(BF)
    x_ref[:, HALF : 2 * HALF] = dot(first, right).astype(BF)
    x_ref[:, 2 * HALF :] = (dot(selector(1), left) + dot(selector(2), right)).astype(BF)
    column_ref[...] = x_ref[: MAIN + TAIL, :]
    ups = dot(first, rz_ref[:, 2 * HALF :])
    main, tail = ups[:MAIN].T, ups[MAIN:].T
    ug_ref[:SHARE, :] = main[:SHARE]
    ug_ref[SHARE:, :] = by_quarter([tail[g * QUARTER : (g + 1) * QUARTER] for g in range(4)])


def load(refs, held, sems):
    own, following, first, second, previous = refs
    copies = [
        pltpu.make_async_copy(source, target, sems.at[i])
        for i, (source, target) in enumerate(
            [
                (own, held.at[0]),
                (following, held.at[1]),
                (first, held.at[2, pl.ds(0, FIRST), :]),
                (second, held.at[2, pl.ds(FIRST, SHARE), :]),
                (previous, held.at[3]),
            ]
        )
    ]
    for copy in copies:
        copy.start()
    return [copies[:1], copies[1:2], copies[2:4], copies[4:]]


def pre_kernel(place, x_ref, *refs):
    out_ref, side_ref, held, sems = refs[5:]
    copies = load(refs[:5], held, sems)
    x = x_ref[...]
    for k in range(NX):
        for copy in copies[k]:
            copy.wait()
        source = (place[1] + k) % NX
        side_ref[source] = held[k, :SIDE, :HID].astype(F32)
        for h in range(2):
            start = SIDE + h * SHARE
            j = 2 * source + h
            found = dot_nt(held[k, start : start + SHARE, :], x)
            out_ref[j, :SHARE, :] = found[:, :MAIN].astype(BF)
            tail = [found[g * QUARTER : (g + 1) * QUARTER, MAIN:] for g in range(4)]
            out_ref[j, SHARE:, :] = by_quarter(tail).astype(BF)


def gelu_slope(values):
    inner_arg = 0.7978845608 * (values + 0.044715 * values * values * values)
    tangent = jnp.tanh(inner_arg)
    return 0.5 * (1.0 + tangent) + 0.5 * values * (1.0 - tangent * tangent) * 0.7978845608 * (
        1.0 + 3.0 * 0.044715 * values * values
    )


def grad_kernel(place, parts_ref, ug_ref, side_ref, counts_ref, out_ref, sums_ref):
    tensor, x_me = place[0], place[1]
    side = side_ref[tensor // 2]
    bias = side[1:2] + side[2:3] + side[3:4]
    wanted = iota((SHARE, HID), 1) == (tensor % 2) * SHARE + iota((SHARE, HID), 0)
    bias = jnp.sum(jnp.where(wanted, bias, 0.0), axis=1, keepdims=True)
    counts = jnp.broadcast_to(counts_ref[...].astype(F32), (8, DP)).astype(BF)
    s = iota((DP, 128), 0)
    lane = iota((DP, 128), 1)
    many = dot(counts, onehot(s == lane // 8 * NX + x_me))[0:1]
    few = dot(counts, onehot(s == lane % TAIL // 2 * NX + x_me))[0:1]
    lane = iota((1, 128), 1)
    many = (lane % 8).astype(F32) < many
    few = (8 + lane % 2).astype(F32) < few
    pre = parts_ref[0].astype(F32)
    for j in range(1, NT):
        pre = pre + parts_ref[j].astype(F32)
    tail_bias = by_quarter([bias[g * QUARTER : (g + 1) * QUARTER] for g in range(4)])
    main = jnp.where(many, ug_ref[:SHARE] * gelu_slope(pre[:SHARE] + bias), 0.0)
    tail = jnp.where(few, ug_ref[SHARE:] * gelu_slope(pre[SHARE:] + tail_bias), 0.0)
    out_ref[:SHARE, :] = main.astype(BF)
    out_ref[SHARE:PACK, :] = tail.astype(BF)
    lane = iota((QUARTER, 128), 1) // 32
    total = jnp.sum(main, axis=1, keepdims=True) + jnp.concatenate(
        [jnp.sum(jnp.where(lane == g, tail, 0.0), axis=1, keepdims=True) for g in range(4)], axis=0
    )
    sums_ref[...] = sum_rows(total)


def unpacked(tail):
    lane = iota((QUARTER, 128), 1) // 32
    zero = jnp.zeros((), BF)
    return jnp.concatenate([jnp.where(lane == g, tail, zero) for g in range(4)], axis=0)


def moved_kernel(place, low_ref, other_ref, sums_ref, side_ref, out_ref):
    tensor, x_me = place[0], place[1]
    m = tensor % 2
    blocks = HID // BR
    owner = side_ref[tensor // 2][0:1, :blocks]
    r, c = iota((blocks, blocks), 0), iota((blocks, blocks), 1)
    column = jnp.sum(jnp.where(r == c, owner, 0.0), axis=1, keepdims=True)
    rank = jnp.sum(jnp.where((column == owner) & (r < c), 1.0, 0.0), axis=0, keepdims=True)
    target = jnp.broadcast_to(owner * MOST + rank, (8, blocks)).astype(BF)
    block, unit = iota((blocks, HID), 0), iota((blocks, HID), 1)
    within = unit - block * BR
    member = (within >= 0) & (within < BR)
    offset = jnp.sum(jnp.where(member, within, 0).astype(F32), axis=0, keepdims=True)
    key = dot(target, onehot(member))[0:1] * BR + offset
    low, other = low_ref[...], other_ref[...]
    both = [jnp.where(m == 0, low, other), jnp.where(m == 0, other, low)]
    main = jnp.concatenate([g[:SHARE] for g in both], axis=0)
    tail = jnp.concatenate([unpacked(g[SHARE:PACK]) for g in both], axis=0)
    r, c = iota((128, 128), 0), iota((128, 128), 1)
    tail = dot(tail, onehot((r % TAIL == c) & (c < TAIL))).astype(BF)
    rho = iota((DP * 16, 1), 0)
    dest, row = rho // 16, rho % 16
    wanted = (dest * MOST + m) * BR + row % BR
    wanted = jnp.where(row < 2 * BR, wanted, -1).astype(F32)
    found = dot(onehot(wanted == key), jnp.concatenate([main, tail], axis=1))
    found = jnp.where(row < BR, found[:, :128], found[:, 128:]).astype(BF)
    sums = sums_ref[...]
    for e in range(DP):
        out_ref[e * 16 : (e + 1) * 16, :] = found[e * 16 : (e + 1) * 16] + sums


def out_kernel(place, g_ref, *refs):
    px_ref, full, held, sems = refs[5:]
    copies = load(refs[:5], held, sems)
    for n in range(2 * NX):
        j = (place[1] + n // 2) % NX * 2 + n % 2
        full[n * SHARE : (n + 1) * SHARE, :MAIN] = g_ref[j, :SHARE, :]
        full[n * SHARE : (n + 1) * SHARE, MAIN:] = unpacked(g_ref[j, SHARE:PACK, :])
    g = full[...]
    here = [dot_nt(selector(i, True), g).astype(BF) for i in range(3)]
    total = [jnp.zeros((RHO, HALF), F32), jnp.zeros((RHO, HALF), F32)]
    for k in range(NX):
        for copy in copies[k]:
            copy.wait()
        span = slice(k * HID, (k + 1) * HID)
        last = held[k, SIDE:, 2 * HALF :]
        for side in range(2):
            part = dot(here[0][:, span], held[k, SIDE:, side * HALF : (side + 1) * HALF])
            total[side] = total[side] + part + dot(here[1 + side][:, span], last)
    for side in range(2):
        px_ref[:, side * HALF : (side + 1) * HALF] = total[side].astype(BF)


def order_kernel(place, in_ref, out_ref, block):
    n = BR * NZ
    r, c = iota((2 * n, RHO), 0), iota((2 * n, RHO), 1)
    pick = onehot((c // 16 == r % NZ) & (c % 16 == r // NZ))
    r, c = iota((128, 128), 0), iota((128, 128), 1)
    tail = jnp.zeros((n, 128), F32)
    sums = jnp.zeros((16, 128), F32)
    for x in range(NX):
        for z in range(NZ):
            block[z * 16 : (z + 1) * 16, :] = in_ref[z * NX + x]
        found = dot(pick, block[...]).astype(BF)
        out_ref[x * n : (x + 1) * n, :] = found[:n]
        tail = tail + dot(found[n:], onehot((r < TAIL) & (c == r + x * TAIL)))
        sums = sums + in_ref[place[2] * NX + x].astype(F32)
    out_ref[NX * n : MOVED * NZ, :] = tail.astype(BF)
    row = iota((8, 128), 0)
    for i, first in enumerate((12, 6)):
        total = sums[first + 2 : first + 3] + sums[first + 1 : first + 2] + sums[first : first + 1]
        high, mid, low = pieces_of(total)
        part = jnp.where(row == 0, high, jnp.where(row == 1, mid, jnp.where(row == 2, low, 0.0)))
        parts = part if i == 0 else jnp.concatenate([parts, part], axis=0)
    out_ref[MOVED * NZ :, :] = parts.astype(BF)


def slots_kernel(in_ref, out_ref):
    total = in_ref[0].astype(F32)
    for z in range(1, NZ):
        total = total + in_ref[z].astype(F32)
    total = total.astype(BF)
    left, right = total[:, :HALF], total[:, HALF:]
    r, c = iota((16, 16), 0), iota((16, 16), 1)
    halfway = (c - SLOTS) * 2
    last = dot(onehot(r == halfway), left) + dot(onehot(r == halfway + 1), right)
    out_ref[:, : 2 * HALF] = total[:SLOTS]
    out_ref[:, 2 * HALF :] = last[:SLOTS].astype(BF)


def weight_kernel(place, m_ref, *refs):
    columns, (out_ref, bias_ref, found, tails) = refs[:NX], refs[NX:]
    lane, unit = iota((128, HID), 0), iota((128, HID), 1)
    row = iota((16, 128), 0)
    total = jnp.zeros((16, HID), F32)
    for h in range(2):
        sums = m_ref[place[1] * 2 + h, MOVED * NZ :, :]
        for i in range(2):
            mine = (unit == h * SHARE + i * 64 + lane) & (lane >= i * 64)
            total = total + dot(jnp.where(row // 8 == i, sums, jnp.zeros((), BF)), onehot(mine))
    total = total[:8] + total[8:]
    bias_ref[...] = total[2:3] + total[1:2] + total[0:1]
    n = BR * NZ
    for j in range(NT):
        for k in range(NX + 1):
            start = pl.multiple_of((place[1] + k) % NX * n, n) if k < NX else NX * n
            block = m_ref[j, pl.ds(start, n), :]
            for b in range(BR):
                row = b * MOST * DP + j * NZ
                found[row : row + NZ, k * 128 : (k + 1) * 128] = block[b * NZ : (b + 1) * NZ]
    r, c = iota((MOST * DP, MOST * DP), 0), iota((MOST * DP, MOST * DP), 1)
    order = onehot(c == r % NT * NZ + r // NT)
    for k in range(NX):
        tails[(place[1] + k) % NX] = columns[k][MAIN:, :]
    tail = tails[...].reshape(NX * TAIL, 3 * HALF)
    for b in range(BR):
        mine = dot(order, found[b * MOST * DP : (b + 1) * MOST * DP, :]).astype(BF)
        total = dot(mine[:, NX * 128 :], tail)
        for k in range(NX):
            total = total + dot(mine[:, k * 128 : (k + 1) * 128], columns[k][:MAIN, :])
        out_ref[b] = total.astype(BF)


def hold_kernel(*refs):
    del refs


def hold(arrays):
    return pl.pallas_call(
        hold_kernel,
        out_shape=[jax.ShapeDtypeStruct(a.shape, a.dtype) for a in arrays],
        in_specs=[pl.BlockSpec(memory_space=ANY)] * len(arrays),
        out_specs=[pl.BlockSpec(memory_space=ANY)] * len(arrays),
        input_output_aliases={i: i for i in range(len(arrays))},
        cost_estimate=pl.CostEstimate(flops=50 * 10**9, bytes_accessed=0, transcendentals=0),
    )(*arrays)


def halves_kernel(next_ref, prev_ref, first_ref, second_ref, sems):
    copies = [
        pltpu.make_async_copy(next_ref.at[pl.ds(0, FIRST), :], first_ref, sems.at[0]),
        pltpu.make_async_copy(prev_ref.at[pl.ds(FIRST, SHARE), :], second_ref, sems.at[1]),
    ]
    for copy in copies:
        copy.start()
    for copy in copies:
        copy.wait()


def halves(following, previous):
    return pl.pallas_call(
        halves_kernel,
        out_shape=[jax.ShapeDtypeStruct((n, 3 * HALF), BF) for n in (FIRST, SHARE)],
        in_specs=[pl.BlockSpec(memory_space=ANY)] * 2,
        out_specs=[pl.BlockSpec(memory_space=VMEM)] * 2,
        scratch_shapes=[pltpu.SemaphoreType.DMA((2,))],
        cost_estimate=pl.CostEstimate(flops=50 * 10**9, bytes_accessed=0, transcendentals=0),
    )(following, previous)


def to_left(value):
    return lax.ppermute(value, "x", [(i, (i - 1) % NX) for i in range(NX)])


def to_right(value):
    return lax.ppermute(value, "x", [(i, (i + 1) % NX) for i in range(NX)])


def across(value):
    return lax.ppermute(value, "x", [(i, (i + 2) % NX) for i in range(NX)])


def body(x_slots, counts, w, bias, upstream, owners):
    tensor = lax.axis_index(("y", "core")).astype(I32)
    x_me = lax.axis_index("x").astype(I32)
    place = jnp.stack([tensor, x_me, lax.axis_index("z").astype(I32)])
    full, packed = call(
        pack_kernel,
        [((FULL, 3 * HALF), BF), ((NZ, 16, 2 * HALF + 256), BF)],
        [place, x_slots, upstream, w, bias, owners.reshape(1, DP)],
        1,
        [
            VMEM((SLOTS, 3 * HALF), BF),
            VMEM((SLOTS, NZ * GROUP), BF),
            VMEM((HID,), F32),
            VMEM((1, DP), I32),
            VMEM((16, 3 * HALF), BF),
            VMEM((RHO, GROUP), BF),
            pltpu.SemaphoreType.DMA((5,)),
        ],
        2 * RHO * GROUP * 256,
        5 * 10**6,
        (1, 2, 3, 4, 5),
        HBM,
        56 * 1024 * 1024,
    )
    following, previous = to_left(full), to_right(full)
    along_z = lax.all_to_all(packed, "z", 0, 0, tiled=True)
    first, second = halves(following, previous)
    pieces = [full, following, to_left(first), to_right(second), previous]
    rows, column, ug = call(
        rows_kernel,
        [((256, 3 * HALF), BF), ((MAIN + TAIL, 3 * HALF), BF), ((PACK, 128), F32)],
        [along_z.reshape(RHO, 2 * HALF + 256)],
        flops=2 * 256 * 256 * 9 * 256,
        moved=2 * 10**6,
    )
    part, side = call(
        pre_kernel,
        [((NT, PACK, 128), BF), ((NX, SIDE, HID), F32)],
        [place, rows] + pieces,
        1,
        [VMEM((NX, FULL, 3 * HALF), BF), pltpu.SemaphoreType.DMA((5,))],
        2 * GROUP * 256 * 3 * HALF,
        6 * 10**6,
        range(2, 7),
    )
    columns = [column] + list(hold([to_left(column), across(column), to_right(column)]))
    parts = lax.all_to_all(part, ("y", "core"), 0, 0, tiled=True)
    low, sums = call(
        grad_kernel,
        [((PACK, 128), BF), ((16, 128), BF)],
        [place, parts, ug, side, counts.reshape(1, DP)],
        1,
        moved=10**6,
    )
    other = lax.ppermute(low, "core", [(0, 1), (1, 0)])
    sent, = call(
        moved_kernel,
        [((DP * 16, 128), BF)],
        [place, low, other, sums, side],
        1,
        flops=2 * 8 * 96 * HID * 128,
        moved=10**6,
    )
    moved = lax.all_to_all(sent.reshape(DP, 16, 128), ("z", "x"), 0, 0, tiled=True)
    low, sent = lax.optimization_barrier((low, sent))
    grad = lax.all_gather(low, ("y", "core"), axis=0)
    px, = call(
        out_kernel,
        [((RHO, 2 * HALF), BF)],
        [place, grad] + pieces,
        1,
        [
            VMEM((GROUP, 256), BF),
            VMEM((NX, FULL, 3 * HALF), BF),
            pltpu.SemaphoreType.DMA((5,)),
        ],
        2 * RHO * GROUP * (4 * HALF + 3 * 256),
        6 * 10**6,
        range(2, 7),
    )
    px, moved, *columns = lax.optimization_barrier((px, moved, *columns))
    pz = lax.all_to_all(px.reshape(NZ, 16, 2 * HALF), "z", 0, 0, tiled=True)
    moved, = call(
        order_kernel,
        [((MOVED * NZ + 16, 128), BF)],
        [place, moved],
        1,
        [VMEM((RHO, 128), BF)],
        moved=10**6,
    )
    moved = lax.all_gather(moved, ("y", "core"), axis=0)
    found, grad_bias = call(
        weight_kernel,
        [((BR, MOST * DP, 3 * HALF), BF), ((1, HID), F32)],
        [place, moved] + columns,
        1,
        [VMEM((NT * BR * NZ, 640), BF), VMEM((NX, TAIL, 3 * HALF), BF)],
        2 * 768 * 640 * 1536,
        5 * 10**6,
    )
    grad_slots, = call(slots_kernel, [((SLOTS, 3 * HALF), BF)], [pz], moved=10**6)
    return grad_slots, grad_bias.reshape(HID), found.transpose(1, 0, 2)


def solution(mesh):
    fine = Mesh(mesh.devices.reshape(NZ, NX, NT // 2, 2), ("z", "x", "y", "core"))
    rows, cols = ("z", "x"), ("y", "core")
    in_specs = (P(rows, cols), P(), P(rows, cols), P(rows), P(rows, None), P(rows, None))
    out_specs = (P(rows, cols), P(rows), P(rows, None, cols))
    return jax.shard_map(body, mesh=fine, in_specs=in_specs, out_specs=out_specs, check_vma=False)
```

time: 214 us -> 173 us (0.81); the launches traced: 210 us -> 171 us
  starting transfers between devices: 27.9 us -> 71.8 us
  waiting for transfers between devices: 76.5 us -> 36 us
  blocking collectives: 61.5 us -> 27.2 us
  between operations: 13.9 us -> 0.89 us
  Pallas kernels: 18.5 us -> 30.4 us
  local copies, waits for them, and re-layouts: 10.9 us -> 3.89 us
    all_to_all x1 -> x0, blocking collectives: 48.4 us -> none  [body(): lax.all_to_all(joined.reshape(NZ, 16, 2 * HALF + 256), 'z', 0, 0, tiled=T...]
    all_gather x3 -> x0, waiting for transfers between devices: 29.6 us -> none  [the longest x1 20.8 us: body(): moved = lax.all_gather(moved, ('y', 'core'), axis=0)]
    all_to_all x1, waiting for transfers between devices: 33.4 us -> 10.3 us  [body(): along_z = lax.all_to_all(packed, 'z', 0, 0, tiled=True)]
    ppermute x0 -> x8, starting transfers between devices: none -> 22.7 us  [the longest x3 10.1 us: to_left(): return lax.ppermute(value, 'x', [(i, (i - 1) % NX) for i in range(NX)])]
    all_to_all x2, starting transfers between devices: 7.7 us -> 29.1 us  [the longest x1 19.1 us: body(): lax.all_to_all(sent.reshape(DP, 16, 128), ('z', 'x'), 0, 0, tiled=True)]
    ppermute x0 -> x8, waiting for transfers between devices: none -> 17.3 us  [the longest x3 9.38 us: to_left(): return lax.ppermute(value, 'x', [(i, (i - 1) % NX) for i in range(NX)])]
    all_gather x0 -> x1, blocking collectives: none -> 14 us  [body(): moved = lax.all_gather(moved, ('y', 'core'), axis=0)]
    pallas_call x9, Pallas kernels: 18.5 us -> 28 us  [call(): pl.pallas_call(kernel, out_shape=[jax.ShapeDtypeStruct(s, d) for s, d in...]
  transfers between devices with their start and end apart: 7 -> 12, of which waited for: 5 -> 7; matrix products, arithmetic and copies ran while one was open for 1% -> 0% of each run, Pallas kernels for 6% -> 12%
where the time goes in v3:
time: 173 us; the launch traced here: 171 us
  starting transfers between devices  71.8 us (42%)
  waiting for transfers between devices  36 us (21%)
  Pallas kernels  30.4 us (18%)
  blocking collectives  27.2 us (16%)
  local copies, waits for them, and re-layouts  3.89 us (2%)
    pallas_call x9, Pallas kernels, call(): pl.pallas_call(kernel, out_shape=[jax.ShapeDtypeStruct(s, d) for s, d in...  28 us
    all_to_all x1, starting transfers between devices, body(): lax.all_to_all(sent.reshape(DP, 16, 128), ('z', 'x'), 0, 0, tiled=True)  19.1 us
    all_to_all x1, starting transfers between devices, body(): along_z = lax.all_to_all(packed, 'z', 0, 0, tiled=True)  15.3 us
    all_gather x1, blocking collectives, body(): moved = lax.all_gather(moved, ('y', 'core'), axis=0)  14 us
    all_gather x1, blocking collectives, body(): grad = lax.all_gather(low, ('y', 'core'), axis=0)  13.2 us
    all_to_all x1, waiting for transfers between devices, body(): along_z = lax.all_to_all(packed, 'z', 0, 0, tiled=True)  10.3 us
    ppermute x3, starting transfers between devices, to_left(): return lax.ppermute(value, 'x', [(i, (i - 1) % NX) for i in range(NX)])  10.1 us
    all_to_all x1, starting transfers between devices, body(): pz = lax.all_to_all(px.reshape(NZ, 16, 2 * HALF), 'z', 0, 0, tiled=True)  10.1 us
  transfers between devices with their start and end apart: 12, of which 7 were waited for; matrix products, arithmetic and copies ran while one was open for 0% of the time, Pallas kernels for 12%

profile of v3, /device:TPU:24, one launch (start us, length us, event | category | flops | bytes accessed | tf_op | source)
XLA Modules:
  0.0 171.4 jit_solution(1985239303354553024)
XLA Ops:
  0.6 0.6 pad_add_fusion.place
  1.2 3.8 %shard_map.85 = (bf16[400,1536]{1,0:T(8,128)(2,1)}, bf16[16,16,1280]{2,1,0:T(8,128)(2,1)}) custom-call(s32[3]{0:T(128)} %pad_add_fusion.place, bf16[10,1536]{1,0:T(8,128)(2,1)} %x_in.1, bf16[10,24576]{1,0:T(8,128)(2,1)} %up_in.1, bf16[384,1536]{1,0:T(8,128)(2,1)} %w_in.1, f32[384]{0:T(512)} %bias_in.1, s32[1,64]{1,0:T(1,128)} %bitcast.14), custom_call_target="tpu_custom_call" | custom-call | flops 201326592 | bytes 5000000 | tf_op jit(solution)/shard_map/pallas_call | solution.py:55
  5.0 4.7 %collective-permute-start = (bf16[400,1536]{1,0:T(8,128)(2,1)}, bf16[400,1536]{1,0:T(8,128)(2,1)S(1)}, u32[]{:S(2)}, u32[]{:S(2)}) collective-permute-start(bf16[400,1536]{1,0:T(8,128)(2,1)} %get-tuple-element.28.refs_0_), channel_id=1, source_target_pairs={{0,24},{8,0},{16,8},{24,16},{1,25},{9,1},{17,9},{25,17},{2,26},{10... | collective-permute-start | bytes 3686408 | tf_op jit(solution)/shard_map/ppermute | solution.py:407
  9.7 1.9 %collective-permute-start.1 = (bf16[400,1536]{1,0:T(8,128)(2,1)}, bf16[400,1536]{1,0:T(8,128)(2,1)}, u32[]{:S(2)}, u32[]{:S(2)}) collective-permute-start(bf16[400,1536]{1,0:T(8,128)(2,1)} %get-tuple-element.28.refs_0_), channel_id=1, source_target_pairs={{0,8},{8,16},{16,24},{24,0},{1,9},{9,17},{17,25},{25,1},{2,10},{10... | collective-permute-start | bytes 3686408 | tf_op jit(solution)/shard_map/ppermute | solution.py:411
  11.6 15.3 %all-to-all-start = ((bf16[16,16,1280]{2,1,0:T(8,128)(2,1)}), bf16[16,16,1280]{2,1,0:T(8,128)(2,1)}, u32[]{:S(2)}, u32[]{:S(2)}) async-start(bf16[16,16,1280]{2,1,0:T(8,128)(2,1)} %get-tuple-element.26), calls=%async_computation | async-start | bytes 1310720 | tf_op jit(solution)/shard_map/all_to_all | solution.py:443
  26.9 0.0 copy-start.8
  26.9 9.4 %collective-permute-done.next_ref.refs_1_ = bf16[400,1536]{1,0:T(8,128)(2,1)S(1)} collective-permute-done((bf16[400,1536]{1,0:T(8,128)(2,1)}, bf16[400,1536]{1,0:T(8,128)(2,1)S(1)}, u32[]{:S(2)}, u32[]{:S(2)}) %collective-permute-start) | collective-permute-done | bytes 1228832 | tf_op jit(solution)/shard_map/ppermute | solution.py:407
  36.3 5.3 %collective-permute-done.1.prev_ref.refs_4_ = bf16[400,1536]{1,0:T(8,128)(2,1)} collective-permute-done((bf16[400,1536]{1,0:T(8,128)(2,1)}, bf16[400,1536]{1,0:T(8,128)(2,1)}, u32[]{:S(2)}, u32[]{:S(2)}) %collective-permute-start.1) | collective-permute-done | bytes 1228832 | tf_op jit(solution)/shard_map/ppermute | solution.py:411
  41.6 0.0 copy-done.1
  41.6 2.4 %shard_map.87 = (bf16[208,1536]{1,0:T(8,128)(2,1)}, bf16[192,1536]{1,0:T(8,128)(2,1)}) custom-call(bf16[400,1536]{1,0:T(8,128)(2,1)} %copy-done.1, bf16[400,1536]{1,0:T(8,128)(2,1)} %collective-permute-done.1.prev_ref.refs_4_), custom_call_target="tpu_custom_call" | custom-call | flops 49999998976 | tf_op jit(solution)/shard_map/pallas_call | solution.py:396
  44.0 1.9 %collective-permute-start.2 = (bf16[208,1536]{1,0:T(8,128)(2,1)}, bf16[208,1536]{1,0:T(8,128)(2,1)S(1)}, u32[]{:S(2)}, u32[]{:S(2)}) collective-permute-start(bf16[208,1536]{1,0:T(8,128)(2,1)} %get-tuple-element.29), channel_id=1, source_target_pairs={{0,24},{8,0},{16,8},{24,16},{1,25},{9,1},{17,9},{25,17},{2,26},{10... | collective-permute-start | bytes 1916936 | tf_op jit(solution)/shard_map/ppermute | solution.py:407
  45.9 3.9 %collective-permute-start.3 = (bf16[192,1536]{1,0:T(8,128)(2,1)}, bf16[192,1536]{1,0:T(8,128)(2,1)S(1)}, u32[]{:S(2)}, u32[]{:S(2)}) collective-permute-start(bf16[192,1536]{1,0:T(8,128)(2,1)} %get-tuple-element.30), channel_id=1, source_target_pairs={{0,8},{8,16},{16,24},{24,0},{1,9},{9,17},{17,25},{25,1},{2,10},{10... | collective-permute-start | bytes 1769480 | tf_op jit(solution)/shard_map/ppermute | solution.py:411
  49.9 10.3 %all-to-all-done = bf16[16,16,1280]{2,1,0:T(8,128)(2,1)} async-done(((bf16[16,16,1280]{2,1,0:T(8,128)(2,1)}), bf16[16,16,1280]{2,1,0:T(8,128)(2,1)}, u32[]{:S(2)}, u32[]{:S(2)}) %all-to-all-start) | async-done | bytes 655392 | tf_op jit(solution)/shard_map/all_to_all | solution.py:443
  60.1 1.7 shard_map.86
  61.8 1.3 collective-permute-done.3.refs_3_
  63.1 0.0 collective-permute-done.2.refs_2_
  63.1 0.0 copy-done.8
  63.2 0.0 copy-done
  63.2 0.0 copy-start.2
  63.2 1.7 %copy-done.2 = bf16[400,1536]{1,0:T(8,128)(2,1)S(1)} copy-done((bf16[400,1536]{1,0:T(8,128)(2,1)S(1)}, bf16[400,1536]{1,0:T(8,128)(2,1)}, u32[]{:S(2)}) %copy-start.2) | copy-done | bytes 1228824
  64.9 5.0 %shard_map.88 = (bf16[8,240,128]{2,1,0:T(8,128)(2,1)}, f32[4,16,384]{2,1,0:T(8,128)S(1)}) custom-call(s32[3]{0:T(128)S(1)} %copy-done.8, bf16[256,1536]{1,0:T(8,128)(2,1)S(1)} %get-tuple-element.27.x_ref, bf16[400,1536]{1,0:T(8,128)(2,1)S(1)} %copy-done, bf16[400,1536]{1,0:T(8,128)(2,1)S(1)} %copy-done.2, ...), custom_call_target="tpu_custom_call" | custom-call | flops 1207959552 | bytes 6000000 | tf_op jit(solution)/shard_map/pallas_call | solution.py:55
  69.9 4.7 %all-to-all-start.1 = ((bf16[8,240,128]{2,1,0:T(8,128)(2,1)}), bf16[8,240,128]{2,1,0:T(8,128)(2,1)S(1)}, u32[]{:S(2)}, u32[]{:S(2)}) async-start(bf16[8,240,128]{2,1,0:T(8,128)(2,1)} %get-tuple-element.31), calls=%async_computation.1 | async-start | bytes 983040 | tf_op jit(solution)/shard_map/all_to_all | solution.py:464
  74.6 3.5 %collective-permute-start.5 = (bf16[160,1536]{1,0:T(8,128)(2,1)S(1)}, bf16[160,1536]{1,0:T(8,128)(2,1)}, u32[]{:S(2)}, u32[]{:S(2)}) collective-permute-start(bf16[160,1536]{1,0:T(8,128)(2,1)S(1)} %get-tuple-element.43.refs_0_), channel_id=1, source_target_pairs={{0,24},{8,0},{16,8},{24,16},{1,25},{9,1},{17,9},{25,17},{2,26},{10... | collective-permute-start | bytes 1474568 | tf_op jit(solution)/shard_map/ppermute | solution.py:407
  78.1 2.9 %collective-permute-start.6 = (bf16[160,1536]{1,0:T(8,128)(2,1)S(1)}, bf16[160,1536]{1,0:T(8,128)(2,1)}, u32[]{:S(2)}, u32[]{:S(2)}) collective-permute-start(bf16[160,1536]{1,0:T(8,128)(2,1)S(1)} %get-tuple-element.43.refs_0_), channel_id=1, source_target_pairs={{0,16},{8,24},{16,0},{24,8},{1,17},{9,25},{17,1},{25,9},{2,18},{10... | collective-permute-start | bytes 1474568 | tf_op jit(solution)/shard_map/ppermute | solution.py:415
  81.0 1.9 %collective-permute-start.7 = (bf16[160,1536]{1,0:T(8,128)(2,1)S(1)}, bf16[160,1536]{1,0:T(8,128)(2,1)}, u32[]{:S(2)}, u32[]{:S(2)}) collective-permute-start(bf16[160,1536]{1,0:T(8,128)(2,1)S(1)} %get-tuple-element.43.refs_0_), channel_id=1, source_target_pairs={{0,8},{8,16},{16,24},{24,0},{1,9},{9,17},{17,25},{25,1},{2,10},{10... | collective-permute-start | bytes 1474568 | tf_op jit(solution)/shard_map/ppermute | solution.py:411
  82.9 0.0 all-to-all-done.1.parts_ref
  83.0 1.2 shard_map.89
  84.2 1.9 %collective-permute-start.4 = (bf16[240,128]{1,0:T(8,128)(2,1)S(1)}, bf16[240,128]{1,0:T(8,128)(2,1)S(1)}, u32[]{:S(2)}, u32[]{:S(2)}) collective-permute-start(bf16[240,128]{1,0:T(8,128)(2,1)S(1)} %get-tuple-element.36.low_ref), channel_id=1, source_target_pairs={{0,1},{1,0},{2,3},{3,2},{4,5},{5,4},{6,7},{7,6},{8,9},{9,8},{10,11... | collective-permute-start | bytes 184328 | tf_op jit(solution)/shard_map/ppermute | solution.py:472
  86.1 1.2 collective-permute-done.4.other_ref
  87.3 2.0 %shard_map.90 = bf16[1024,128]{1,0:T(8,128)(2,1)} custom-call(s32[3]{0:T(128)S(1)} %copy-done.8, bf16[240,128]{1,0:T(8,128)(2,1)S(1)} %get-tuple-element.36.low_ref, bf16[240,128]{1,0:T(8,128)(2,1)S(1)} %collective-permute-done.4.other_ref, bf16[16,128]{1,0:T(8,128)(2,1)S(1)} %get-tuple-element.35.sums_ref, f32[4,16,384]{2,1,0:T(8,128)S(1)} %get-tuple-element.33.side_ref), custom_call_target="tpu_custom_call" | custom-call | flops 75497472 | bytes 1000000 | tf_op jit(solution)/shard_map/pallas_call | solution.py:55
  89.3 19.1 %all-to-all-start.2 = ((bf16[64,16,128]{2,1,0:T(8,128)(2,1)}), bf16[64,16,128]{2,1,0:T(8,128)(2,1)S(1)}, u32[]{:S(2)}, u32[]{:S(2)}) async-start(bf16[64,16,128]{2,1,0:T(8,128)(2,1)} %bitcast.7), calls=%async_computation.2 | async-start | bytes 524288 | tf_op jit(solution)/shard_map/all_to_all | solution.py:481
  108.4 0.0 copy-start.3
  108.4 0.0 collective-permute-done.5.refs_0_
  108.4 0.0 collective-permute-done.6.refs_1_
  108.4 0.0 collective-permute-done.7.refs_2_
  108.5 13.2 %all-gather = bf16[1920,128]{1,0:T(8,128)(2,1)S(1)} all-gather(bf16[240,128]{1,0:T(8,128)(2,1)S(1)} %get-tuple-element.36.low_ref), channel_id=2, replica_groups=mesh['z'=16,'x'=4,'y'=4,'core'=2] {'y','core'}, dimensions={0}, use_global_device_ids=true | all-gather | bytes 552960 | tf_op jit(solution)/shard_map/all_gather | solution.py:483
  121.7 0.0 copy-done.3
  121.7 1.1 copy-done.5
  122.8 1.1 copy-done.7
  123.8 5.6 %shard_map.91 = bf16[256,1024]{1,0:T(8,128)(2,1)} custom-call(s32[3]{0:T(128)S(1)} %copy-done.8, bf16[8,240,128]{2,1,0:T(8,128)(2,1)S(1)} %bitcast.12, bf16[400,1536]{1,0:T(8,128)(2,1)S(1)} %copy-done, bf16[400,1536]{1,0:T(8,128)(2,1)S(1)} %copy-done.3, bf16[208,1536]{1,0:T(8,128)(2,1)S(1)} %copy-done.5, bf16[192,1536]{1,0:T(8,128)(2,1)S(1)} %copy-done.7, ...), custom_call_target="tpu_custom_call" | custom-call | flops 2214592512 | bytes 6000000 | tf_op jit(solution)/shard_map/pallas_call | solution.py:55
  129.5 1.7 %all-to-all-done.2.in_ref = bf16[64,16,128]{2,1,0:T(8,128)(2,1)S(1)} async-done(((bf16[64,16,128]{2,1,0:T(8,128)(2,1)}), bf16[64,16,128]{2,1,0:T(8,128)(2,1)S(1)}, u32[]{:S(2)}, u32[]{:S(2)}) %all-to-all-start.2) | async-done | bytes 262176 | tf_op jit(solution)/shard_map/all_to_all | solution.py:481
  131.2 10.1 %all-to-all-start.3 = ((bf16[16,16,1024]{2,1,0:T(8,128)(2,1)}), bf16[16,16,1024]{2,1,0:T(8,128)(2,1)S(1)}, u32[]{:S(2)}, u32[]{:S(2)}) async-start(bf16[16,16,1024]{2,1,0:T(8,128)(2,1)} %bitcast.8), calls=%async_computation.3 | async-start | bytes 1048576 | tf_op jit(solution)/shard_map/all_to_all | solution.py:499
  141.2 1.1 shard_map.94
  142.3 14.0 %all-gather.1 = bf16[3968,128]{1,0:T(8,128)(2,1)S(1)} all-gather(bf16[496,128]{1,0:T(8,128)(2,1)S(1)} %shard_map.94), channel_id=3, replica_groups=mesh['z'=16,'x'=4,'y'=4,'core'=2] {'y','core'}, dimensions={0}, use_global_device_ids=true | all-gather | bytes 1142784 | tf_op jit(solution)/shard_map/all_gather | solution.py:508
  156.4 6.8 %shard_map.95 = (bf16[6,128,1536]{2,1,0:T(8,128)(2,1)}, f32[1,384]{1,0:T(1,128)S(1)}) custom-call(s32[3]{0:T(128)S(1)} %copy-done.8, bf16[8,496,128]{2,1,0:T(8,128)(2,1)S(1)} %bitcast.11, bf16[160,1536]{1,0:T(8,128)(2,1)S(1)} %get-tuple-element.43.refs_0_, bf16[160,1536]{1,0:T(8,128)(2,1)} %get-tuple-element.44.refs_1_, ...), custom_call_target="tpu_custom_call" | custom-call | flops 1509949440 | bytes 5000000 | tf_op jit(solution)/shard_map/pallas_call | solution.py:55
  163.2 0.6 reduce
  163.8 6.8 %all-to-all-done.3.in_ref = bf16[16,16,1024]{2,1,0:T(8,128)(2,1)S(1)} async-done(((bf16[16,16,1024]{2,1,0:T(8,128)(2,1)}), bf16[16,16,1024]{2,1,0:T(8,128)(2,1)S(1)}, u32[]{:S(2)}, u32[]{:S(2)}) %all-to-all-start.3) | async-done | bytes 524320 | tf_op jit(solution)/shard_map/all_to_all | solution.py:499
  170.6 0.8 shard_map.93
  (11 shorter events, 0.0 us)
Async XLA Ops:
  5.0 31.3 %collective-permute-start = (bf16[400,1536]{1,0:T(8,128)(2,1)}, bf16[400,1536]{1,0:T(8,128)(2,1)S(1)}, u32[]{:S(2)}, u32[]{:S(2)}) collective-permute-start(bf16[400,1536]{1,0:T(8,128)(2,1)} %get-tuple-element.28.refs_0_), channel_id=1, source_target_pairs={{0,24},{8,0},{16,8},{24,16},{1,25},{9,1},{17,9},{25,17},{2,26},{10... | collective-permute-start | bytes 3686408 | tf_op jit(solution)/shard_map/ppermute | solution.py:407
  9.7 31.9 %collective-permute-start.1 = (bf16[400,1536]{1,0:T(8,128)(2,1)}, bf16[400,1536]{1,0:T(8,128)(2,1)}, u32[]{:S(2)}, u32[]{:S(2)}) collective-permute-start(bf16[400,1536]{1,0:T(8,128)(2,1)} %get-tuple-element.28.refs_0_), channel_id=1, source_target_pairs={{0,8},{8,16},{16,24},{24,0},{1,9},{9,17},{17,25},{25,1},{2,10},{10... | collective-permute-start | bytes 3686408 | tf_op jit(solution)/shard_map/ppermute | solution.py:411
  11.6 48.5 %all-to-all-start = ((bf16[16,16,1280]{2,1,0:T(8,128)(2,1)}), bf16[16,16,1280]{2,1,0:T(8,128)(2,1)}, u32[]{:S(2)}, u32[]{:S(2)}) async-start(bf16[16,16,1280]{2,1,0:T(8,128)(2,1)} %get-tuple-element.26), calls=%async_computation | async-start | bytes 1310720 | tf_op jit(solution)/shard_map/all_to_all | solution.py:443
  26.9 36.3 %copy-start.8 = (s32[3]{0:T(128)S(1)}, s32[3]{0:T(128)}, u32[]{:S(2)}) copy-start(s32[3]{0:T(128)} %pad_add_fusion.place) | copy-start | bytes 40
  36.3 5.3 %copy-start.1 = (bf16[400,1536]{1,0:T(8,128)(2,1)}, bf16[400,1536]{1,0:T(8,128)(2,1)S(1)}, u32[]{:S(2)}) copy-start(bf16[400,1536]{1,0:T(8,128)(2,1)S(1)} %collective-permute-done.next_ref.refs_1_) | copy-start | bytes 3686404
  41.6 21.6 %copy-start = (bf16[400,1536]{1,0:T(8,128)(2,1)S(1)}, bf16[400,1536]{1,0:T(8,128)(2,1)}, u32[]{:S(2)}) copy-start(bf16[400,1536]{1,0:T(8,128)(2,1)} %get-tuple-element.28.refs_0_) | copy-start | bytes 3686404
  44.0 19.1 %collective-permute-start.2 = (bf16[208,1536]{1,0:T(8,128)(2,1)}, bf16[208,1536]{1,0:T(8,128)(2,1)S(1)}, u32[]{:S(2)}, u32[]{:S(2)}) collective-permute-start(bf16[208,1536]{1,0:T(8,128)(2,1)} %get-tuple-element.29), channel_id=1, source_target_pairs={{0,24},{8,0},{16,8},{24,16},{1,25},{9,1},{17,9},{25,17},{2,26},{10... | collective-permute-start | bytes 1916936 | tf_op jit(solution)/shard_map/ppermute | solution.py:407
  45.9 17.2 %collective-permute-start.3 = (bf16[192,1536]{1,0:T(8,128)(2,1)}, bf16[192,1536]{1,0:T(8,128)(2,1)S(1)}, u32[]{:S(2)}, u32[]{:S(2)}) collective-permute-start(bf16[192,1536]{1,0:T(8,128)(2,1)} %get-tuple-element.30), channel_id=1, source_target_pairs={{0,8},{8,16},{16,24},{24,0},{1,9},{9,17},{17,25},{25,1},{2,10},{10... | collective-permute-start | bytes 1769480 | tf_op jit(solution)/shard_map/ppermute | solution.py:411
  63.1 6.7 %copy-start.6 = (bf16[192,1536]{1,0:T(8,128)(2,1)}, bf16[192,1536]{1,0:T(8,128)(2,1)S(1)}, u32[]{:S(2)}) copy-start(bf16[192,1536]{1,0:T(8,128)(2,1)S(1)} %collective-permute-done.3.refs_3_) | copy-start | bytes 1769476
  63.1 6.7 %copy-start.4 = (bf16[208,1536]{1,0:T(8,128)(2,1)}, bf16[208,1536]{1,0:T(8,128)(2,1)S(1)}, u32[]{:S(2)}) copy-start(bf16[208,1536]{1,0:T(8,128)(2,1)S(1)} %collective-permute-done.2.refs_2_) | copy-start | bytes 1916932
  63.2 1.7 %copy-start.2 = (bf16[400,1536]{1,0:T(8,128)(2,1)S(1)}, bf16[400,1536]{1,0:T(8,128)(2,1)}, u32[]{:S(2)}) copy-start(bf16[400,1536]{1,0:T(8,128)(2,1)} %copy-done.1) | copy-start | bytes 3686404
  64.9 18.1 %copy-start.9 = (s32[64]{0:T(128)S(1)}, s32[64]{0:T(128)}, u32[]{:S(2)}) copy-start(s32[64]{0:T(128)} %param.7) | copy-start | bytes 772
  69.9 13.0 %all-to-all-start.1 = ((bf16[8,240,128]{2,1,0:T(8,128)(2,1)}), bf16[8,240,128]{2,1,0:T(8,128)(2,1)S(1)}, u32[]{:S(2)}, u32[]{:S(2)}) async-start(bf16[8,240,128]{2,1,0:T(8,128)(2,1)} %get-tuple-element.31), calls=%async_computation.1 | async-start | bytes 983040 | tf_op jit(solution)/shard_map/all_to_all | solution.py:464
  74.6 33.8 %collective-permute-start.5 = (bf16[160,1536]{1,0:T(8,128)(2,1)S(1)}, bf16[160,1536]{1,0:T(8,128)(2,1)}, u32[]{:S(2)}, u32[]{:S(2)}) collective-permute-start(bf16[160,1536]{1,0:T(8,128)(2,1)S(1)} %get-tuple-element.43.refs_0_), channel_id=1, source_target_pairs={{0,24},{8,0},{16,8},{24,16},{1,25},{9,1},{17,9},{25,17},{2,26},{10... | collective-permute-start | bytes 1474568 | tf_op jit(solution)/shard_map/ppermute | solution.py:407
  78.1 30.3 %collective-permute-start.6 = (bf16[160,1536]{1,0:T(8,128)(2,1)S(1)}, bf16[160,1536]{1,0:T(8,128)(2,1)}, u32[]{:S(2)}, u32[]{:S(2)}) collective-permute-start(bf16[160,1536]{1,0:T(8,128)(2,1)S(1)} %get-tuple-element.43.refs_0_), channel_id=1, source_target_pairs={{0,16},{8,24},{16,0},{24,8},{1,17},{9,25},{17,1},{25,9},{2,18},{10... | collective-permute-start | bytes 1474568 | tf_op jit(solution)/shard_map/ppermute | solution.py:415
  81.0 27.4 %collective-permute-start.7 = (bf16[160,1536]{1,0:T(8,128)(2,1)S(1)}, bf16[160,1536]{1,0:T(8,128)(2,1)}, u32[]{:S(2)}, u32[]{:S(2)}) collective-permute-start(bf16[160,1536]{1,0:T(8,128)(2,1)S(1)} %get-tuple-element.43.refs_0_), channel_id=1, source_target_pairs={{0,8},{8,16},{16,24},{24,0},{1,9},{9,17},{17,25},{25,1},{2,10},{10... | collective-permute-start | bytes 1474568 | tf_op jit(solution)/shard_map/ppermute | solution.py:411
  84.2 3.1 %collective-permute-start.4 = (bf16[240,128]{1,0:T(8,128)(2,1)S(1)}, bf16[240,128]{1,0:T(8,128)(2,1)S(1)}, u32[]{:S(2)}, u32[]{:S(2)}) collective-permute-start(bf16[240,128]{1,0:T(8,128)(2,1)S(1)} %get-tuple-element.36.low_ref), channel_id=1, source_target_pairs={{0,1},{1,0},{2,3},{3,2},{4,5},{5,4},{6,7},{7,6},{8,9},{9,8},{10,11... | collective-permute-start | bytes 184328 | tf_op jit(solution)/shard_map/ppermute | solution.py:472
  89.3 41.9 %all-to-all-start.2 = ((bf16[64,16,128]{2,1,0:T(8,128)(2,1)}), bf16[64,16,128]{2,1,0:T(8,128)(2,1)S(1)}, u32[]{:S(2)}, u32[]{:S(2)}) async-start(bf16[64,16,128]{2,1,0:T(8,128)(2,1)} %bitcast.7), calls=%async_computation.2 | async-start | bytes 524288 | tf_op jit(solution)/shard_map/all_to_all | solution.py:481
  108.4 13.3 %copy-start.3 = (bf16[400,1536]{1,0:T(8,128)(2,1)S(1)}, bf16[400,1536]{1,0:T(8,128)(2,1)}, u32[]{:S(2)}) copy-start(bf16[400,1536]{1,0:T(8,128)(2,1)} %copy-done.1) | copy-start | bytes 3686404
  121.7 1.1 copy-start.5
  122.8 1.1 copy-start.7
  131.2 39.4 %all-to-all-start.3 = ((bf16[16,16,1024]{2,1,0:T(8,128)(2,1)}), bf16[16,16,1024]{2,1,0:T(8,128)(2,1)S(1)}, u32[]{:S(2)}, u32[]{:S(2)}) async-start(bf16[16,16,1024]{2,1,0:T(8,128)(2,1)} %bitcast.8), calls=%async_computation.3 | async-start | bytes 1048576 | tf_op jit(solution)/shard_map/all_to_all | solution.py:499

commit v4 on v3

--- a/solution.py
+++ b/solution.py
@@ -25,7 +25,9 @@
 FIRST = SIDE + SHARE
 FULL = SIDE + HID
 MOVED = (NX + 1) * BR
-LIMIT = 24 * 1024 * 1024
+LIMIT = 16 * 1024 * 1024
+LARGE = 56 * 1024 * 1024
+WIDTH = 2 * HALF + 128
 
 
 def iota(shape, dim):
@@ -69,7 +71,7 @@
     return high, mid, value - high - mid
 
 
-def pack_kernel(place, x_in, up_in, w_in, bias_in, owner_in, full_ref, out_ref, x_ref, up_ref, bias_ref, owner_ref, rows, ups, sems):
+def pack_kernel(place, x_in, up_in, w_in, bias_in, owner_in, top_ref, bottom_ref, out_ref, x_ref, up_ref, bias_ref, owner_ref, rows, ups, sems):
     copies = [
         pltpu.make_async_copy(source, target, sems.at[i])
         for i, (source, target) in enumerate(
@@ -78,14 +80,24 @@
                 (x_in, x_ref),
                 (bias_in, bias_ref),
                 (owner_in, owner_ref),
-                (w_in, full_ref.at[pl.ds(SIDE, HID), :]),
+                (w_in.at[pl.ds(0, SHARE), :], top_ref.at[pl.ds(SIDE, SHARE), :]),
+                (w_in.at[pl.ds(SHARE, SHARE), :], bottom_ref),
             ]
         )
     ]
     for copy in copies:
         copy.start()
-    k, lane = iota((GROUP, 256), 0), iota((GROUP, 256), 1)
-    pick = onehot((k == place[0] * SHARE + lane) & (lane < SHARE))
+    skip = place[0] % 2 * 64
+    k, lane = iota((256, 384), 0) - skip, iota((256, 384), 1)
+    pick = (lane < 128) & (k == lane)
+    pick = pick | ((lane >= 128) & (lane < 192) & (k == lane))
+    pick = onehot(pick | ((lane >= 320) & (k == lane - 192)))
+    k, lane = iota((RHO, RHO), 0), iota((RHO, RHO), 1)
+    block = k // 16 == lane // 16
+    k, lane = k % 16, lane % 16
+    kept = onehot(block & (k == lane) & (k < SLOTS))
+    kept_even = onehot(block & (lane == 2 * (k - SLOTS)))
+    kept_odd = onehot(block & (lane == 2 * (k - SLOTS) + 1))
     r, c = iota((16, 16), 0), iota((16, 16), 1)
     same = onehot((r == c) & (r < SLOTS))
     even = onehot(c == 2 * (r - SLOTS))
@@ -94,8 +106,11 @@
     ups[...] = jnp.zeros_like(ups)
     copies[0].wait()
     for z in range(NZ):
-        ups[z * 16 : z * 16 + SLOTS, :] = up_ref[:, z * GROUP : (z + 1) * GROUP]
+        start = pl.multiple_of(z * GROUP + place[0] * 3 // 2 * 128, 128)
+        ups[z * 16 : z * 16 + SLOTS, :] = up_ref[:, pl.ds(start, 256)]
     chosen = dot(ups[...], pick).astype(BF)
+    chosen = dot(kept, chosen[:, :128]) + dot(kept_even, chosen[:, 128:256]) + dot(kept_odd, chosen[:, 256:])
+    chosen = chosen.astype(BF)
     copies[1].wait()
     rows[0:SLOTS, :] = x_ref[...]
     a, b, last = rows[:, :HALF], rows[:, HALF : 2 * HALF], rows[:, 2 * HALF :]
@@ -112,9 +127,10 @@
     copies[3].wait()
     owner = jnp.where(iota((SIDE, DP), 0) == 0, owner_ref[...].astype(F32), 0.0).astype(BF)
     owner = dot(owner, onehot(iota((DP, HID), 0) == iota((DP, HID), 1)))
-    full_ref[:SIDE, :HID] = (owner + side).astype(BF)
-    full_ref[:SIDE, HID:] = jnp.zeros((SIDE, 3 * HALF - HID), BF)
+    top_ref[:SIDE, :HID] = (owner + side).astype(BF)
+    top_ref[:SIDE, HID:] = jnp.zeros((SIDE, 3 * HALF - HID), BF)
     copies[4].wait()
+    copies[5].wait()
 
 
 def sum_rows(total):
@@ -125,7 +141,8 @@
     r, c = iota((16, 16), 0), iota((16, 16), 1)
     shift = onehot(iota((128, 128), 0) + 64 == iota((128, 128), 1))
     rest = dot(pieces[:, 128:], shift).astype(BF)
-    rows = dot(onehot((r == c + 12) & (c < 3)), pieces[:, :128]) + dot(onehot((r == c + 6) & (c < 3)), rest)
+    head = (c < 3) & (r == jnp.where(c < 2, c + 6, 14))
+    rows = dot(onehot(head), pieces[:, :128]) + dot(onehot((r == c + 8) & (c < 3)), rest)
     return rows.astype(BF)
 
 
@@ -150,54 +167,53 @@
     return found
 
 
-def rows_kernel(rz_ref, x_ref, column_ref, ug_ref):
-    left, right = rz_ref[:, :HALF], rz_ref[:, HALF : 2 * HALF]
-    first = selector(0)
+def rows_kernel(_, rz_ref, x_ref, column_ref, ug_out, ug_ref):
+    left, right, ups = rz_ref[:, :HALF], rz_ref[:, HALF : 2 * HALF], rz_ref[:, 2 * HALF :]
+    first, even, odd = selector(0), selector(1), selector(2)
     x_ref[:, :HALF] = dot(first, left).astype(BF)
     x_ref[:, HALF : 2 * HALF] = dot(first, right).astype(BF)
-    x_ref[:, 2 * HALF :] = (dot(selector(1), left) + dot(selector(2), right)).astype(BF)
+    x_ref[:, 2 * HALF :] = (dot(even, left) + dot(odd, right)).astype(BF)
+    r, c = iota((128, 128), 0), iota((128, 128), 1)
+    low, high = dot(ups, onehot((r == c) & (r < 64))).astype(BF), dot(ups, onehot(r == c + 64)).astype(BF)
+    for part, rest in (
+        (dot(first, ups), slice(0, 128)),
+        (dot(even, low) + dot(odd, high), slice(128, SHARE)),
+    ):
+        main, tail = part[:MAIN].T, part[MAIN:].T
+        ug_ref[rest, :MAIN] = main[: rest.stop - rest.start]
+        ug_ref[rest, MAIN:] = tail[: rest.stop - rest.start]
+    ug_out[:SHARE, :] = ug_ref[:, :MAIN]
+    ug_out[SHARE:, :] = by_quarter([ug_ref[g * QUARTER : (g + 1) * QUARTER, MAIN:] for g in range(4)])
     column_ref[...] = x_ref[: MAIN + TAIL, :]
-    ups = dot(first, rz_ref[:, 2 * HALF :])
-    main, tail = ups[:MAIN].T, ups[MAIN:].T
-    ug_ref[:SHARE, :] = main[:SHARE]
-    ug_ref[SHARE:, :] = by_quarter([tail[g * QUARTER : (g + 1) * QUARTER] for g in range(4)])
-
-
-def load(refs, held, sems):
-    own, following, first, second, previous = refs
-    copies = [
-        pltpu.make_async_copy(source, target, sems.at[i])
-        for i, (source, target) in enumerate(
-            [
-                (own, held.at[0]),
-                (following, held.at[1]),
-                (first, held.at[2, pl.ds(0, FIRST), :]),
-                (second, held.at[2, pl.ds(FIRST, SHARE), :]),
-                (previous, held.at[3]),
-            ]
-        )
-    ]
-    for copy in copies:
-        copy.start()
-    return [copies[:1], copies[1:2], copies[2:4], copies[4:]]
-
-
-def pre_kernel(place, x_ref, *refs):
-    out_ref, side_ref, held, sems = refs[5:]
-    copies = load(refs[:5], held, sems)
+
+
+def partial(piece, start, x, out):
+    found = dot_nt(piece[start : start + SHARE, :], x)
+    out[:SHARE, :] = found[:, :MAIN].astype(BF)
+    tail = [found[g * QUARTER : (g + 1) * QUARTER, MAIN:] for g in range(4)]
+    out[SHARE:, :] = by_quarter(tail).astype(BF)
+
+
+def near_kernel(x_ref, *refs):
+    pieces, (out_ref, side_ref) = refs[:6], refs[6:]
     x = x_ref[...]
-    for k in range(NX):
-        for copy in copies[k]:
-            copy.wait()
-        source = (place[1] + k) % NX
-        side_ref[source] = held[k, :SIDE, :HID].astype(F32)
-        for h in range(2):
-            start = SIDE + h * SHARE
-            j = 2 * source + h
-            found = dot_nt(held[k, start : start + SHARE, :], x)
-            out_ref[j, :SHARE, :] = found[:, :MAIN].astype(BF)
-            tail = [found[g * QUARTER : (g + 1) * QUARTER, MAIN:] for g in range(4)]
-            out_ref[j, SHARE:, :] = by_quarter(tail).astype(BF)
+    for n, piece in enumerate(pieces):
+        partial(piece, SIDE if n % 2 == 0 else 0, x, out_ref.at[n])
+        if n % 2 == 0:
+            side_ref[n // 2] = piece[:SIDE, :HID]
+
+
+def pre_kernel(place, x_ref, near_ref, near_side, top_ref, bottom_ref, out_ref, side_ref):
+    x = x_ref[...]
+    far = (place[1] + 2) % NX
+    partial(top_ref, SIDE, x, out_ref.at[2 * far])
+    partial(bottom_ref, 0, x, out_ref.at[2 * far + 1])
+    side_ref[far] = top_ref[:SIDE, :HID].astype(F32)
+    for n, step in enumerate((0, 1, 3)):
+        source = (place[1] + step) % NX
+        out_ref[2 * source] = near_ref[2 * n]
+        out_ref[2 * source + 1] = near_ref[2 * n + 1]
+        side_ref[source] = near_side[n].astype(F32)
 
 
 def gelu_slope(values):
@@ -263,20 +279,20 @@
     tail = jnp.concatenate([unpacked(g[SHARE:PACK]) for g in both], axis=0)
     r, c = iota((128, 128), 0), iota((128, 128), 1)
     tail = dot(tail, onehot((r % TAIL == c) & (c < TAIL))).astype(BF)
-    rho = iota((DP * 16, 1), 0)
-    dest, row = rho // 16, rho % 16
-    wanted = (dest * MOST + m) * BR + row % BR
-    wanted = jnp.where(row < 2 * BR, wanted, -1).astype(F32)
+    rho = iota((DP * 8, 1), 0)
+    dest, row = rho // 8, rho % 8
+    wanted = (dest * MOST + m) * BR + row
+    wanted = jnp.where(row < BR, wanted, -1).astype(F32)
     found = dot(onehot(wanted == key), jnp.concatenate([main, tail], axis=1))
-    found = jnp.where(row < BR, found[:, :128], found[:, 128:]).astype(BF)
-    sums = sums_ref[...]
+    sums = sums_ref[...].astype(F32)
     for e in range(DP):
-        out_ref[e * 16 : (e + 1) * 16, :] = found[e * 16 : (e + 1) * 16] + sums
+        here = found[e * 8 : (e + 1) * 8]
+        here = jnp.concatenate([here[:, :128], here[:, 128:]], axis=0) + sums
+        out_ref[e * 16 : (e + 1) * 16, :] = here.astype(BF)
 
 
 def out_kernel(place, g_ref, *refs):
-    px_ref, full, held, sems = refs[5:]
-    copies = load(refs[:5], held, sems)
+    pieces, (px_ref, full) = refs[: 2 * NX], refs[2 * NX :]
     for n in range(2 * NX):
         j = (place[1] + n // 2) % NX * 2 + n % 2
         full[n * SHARE : (n + 1) * SHARE, :MAIN] = g_ref[j, :SHARE, :]
@@ -284,22 +300,22 @@
     g = full[...]
     here = [dot_nt(selector(i, True), g).astype(BF) for i in range(3)]
     total = [jnp.zeros((RHO, HALF), F32), jnp.zeros((RHO, HALF), F32)]
-    for k in range(NX):
-        for copy in copies[k]:
-            copy.wait()
-        span = slice(k * HID, (k + 1) * HID)
-        last = held[k, SIDE:, 2 * HALF :]
+    for n, piece in enumerate(pieces):
+        span = slice(n * SHARE, (n + 1) * SHARE)
+        start = SIDE if n % 2 == 0 else 0
+        last = piece[start:, 2 * HALF :]
         for side in range(2):
-            part = dot(here[0][:, span], held[k, SIDE:, side * HALF : (side + 1) * HALF])
+            part = dot(here[0][:, span], piece[start:, side * HALF : (side + 1) * HALF])
             total[side] = total[side] + part + dot(here[1 + side][:, span], last)
     for side in range(2):
         px_ref[:, side * HALF : (side + 1) * HALF] = total[side].astype(BF)
 
 
-def order_kernel(place, in_ref, out_ref, block):
+def order_kernel(place, _, in_ref, out_ref, block):
     n = BR * NZ
     r, c = iota((2 * n, RHO), 0), iota((2 * n, RHO), 1)
-    pick = onehot((c // 16 == r % NZ) & (c % 16 == r // NZ))
+    row = r // NZ
+    pick = onehot((c // 16 == r % NZ) & (c % 16 == jnp.where(row < BR, row, row + 8 - BR)))
     r, c = iota((128, 128), 0), iota((128, 128), 1)
     tail = jnp.zeros((n, 128), F32)
     sums = jnp.zeros((16, 128), F32)
@@ -312,8 +328,8 @@
         sums = sums + in_ref[place[2] * NX + x].astype(F32)
     out_ref[NX * n : MOVED * NZ, :] = tail.astype(BF)
     row = iota((8, 128), 0)
-    for i, first in enumerate((12, 6)):
-        total = sums[first + 2 : first + 3] + sums[first + 1 : first + 2] + sums[first : first + 1]
+    for i, (a, b, c) in enumerate(((6, 7, 14), (8, 9, 10))):
+        total = sums[c : c + 1] + sums[b : b + 1] + sums[a : a + 1]
         high, mid, low = pieces_of(total)
         part = jnp.where(row == 0, high, jnp.where(row == 1, mid, jnp.where(row == 2, low, 0.0)))
         parts = part if i == 0 else jnp.concatenate([parts, part], axis=0)
@@ -344,7 +360,7 @@
             mine = (unit == h * SHARE + i * 64 + lane) & (lane >= i * 64)
             total = total + dot(jnp.where(row // 8 == i, sums, jnp.zeros((), BF)), onehot(mine))
     total = total[:8] + total[8:]
-    bias_ref[...] = total[2:3] + total[1:2] + total[0:1]
+    bias_ref[...] = (total[2:3] + total[1:2] + total[0:1]).reshape(HID)
     n = BR * NZ
     for j in range(NT):
         for k in range(NX + 1):
@@ -366,41 +382,18 @@
         out_ref[b] = total.astype(BF)
 
 
-def hold_kernel(*refs):
-    del refs
-
-
-def hold(arrays):
+def arrived_kernel(*refs):
+    refs[-1][...] = jnp.zeros_like(refs[-1])
+
+
+def arrived(arrays):
     return pl.pallas_call(
-        hold_kernel,
-        out_shape=[jax.ShapeDtypeStruct(a.shape, a.dtype) for a in arrays],
+        arrived_kernel,
+        out_shape=jax.ShapeDtypeStruct((8, 128), F32),
         in_specs=[pl.BlockSpec(memory_space=ANY)] * len(arrays),
-        out_specs=[pl.BlockSpec(memory_space=ANY)] * len(arrays),
-        input_output_aliases={i: i for i in range(len(arrays))},
+        out_specs=pl.BlockSpec(memory_space=VMEM),
         cost_estimate=pl.CostEstimate(flops=50 * 10**9, bytes_accessed=0, transcendentals=0),
     )(*arrays)
-
-
-def halves_kernel(next_ref, prev_ref, first_ref, second_ref, sems):
-    copies = [
-        pltpu.make_async_copy(next_ref.at[pl.ds(0, FIRST), :], first_ref, sems.at[0]),
-        pltpu.make_async_copy(prev_ref.at[pl.ds(FIRST, SHARE), :], second_ref, sems.at[1]),
-    ]
-    for copy in copies:
-        copy.start()
-    for copy in copies:
-        copy.wait()
-
-
-def halves(following, previous):
-    return pl.pallas_call(
-        halves_kernel,
-        out_shape=[jax.ShapeDtypeStruct((n, 3 * HALF), BF) for n in (FIRST, SHARE)],
-        in_specs=[pl.BlockSpec(memory_space=ANY)] * 2,
-        out_specs=[pl.BlockSpec(memory_space=VMEM)] * 2,
-        scratch_shapes=[pltpu.SemaphoreType.DMA((2,))],
-        cost_estimate=pl.CostEstimate(flops=50 * 10**9, bytes_accessed=0, transcendentals=0),
-    )(following, previous)
 
 
 def to_left(value):
@@ -419,9 +412,9 @@
     tensor = lax.axis_index(("y", "core")).astype(I32)
     x_me = lax.axis_index("x").astype(I32)
     place = jnp.stack([tensor, x_me, lax.axis_index("z").astype(I32)])
-    full, packed = call(
+    top, bottom, packed = call(
         pack_kernel,
-        [((FULL, 3 * HALF), BF), ((NZ, 16, 2 * HALF + 256), BF)],
+        [((FIRST, 3 * HALF), BF), ((SHARE, 3 * HALF), BF), ((NZ, 16, WIDTH), BF)],
         [place, x_slots, upstream, w, bias, owners.reshape(1, DP)],
         1,
         [
@@ -430,37 +423,48 @@
             VMEM((HID,), F32),
             VMEM((1, DP), I32),
             VMEM((16, 3 * HALF), BF),
-            VMEM((RHO, GROUP), BF),
-            pltpu.SemaphoreType.DMA((5,)),
+            VMEM((RHO, 256), BF),
+            pltpu.SemaphoreType.DMA((6,)),
         ],
         2 * RHO * GROUP * 256,
         5 * 10**6,
         (1, 2, 3, 4, 5),
         HBM,
-        56 * 1024 * 1024,
-    )
-    following, previous = to_left(full), to_right(full)
+        LARGE,
+    )
+    next_top, prev_bottom = to_left(top), to_right(bottom)
     along_z = lax.all_to_all(packed, "z", 0, 0, tiled=True)
-    first, second = halves(following, previous)
-    pieces = [full, following, to_left(first), to_right(second), previous]
+    there = arrived([next_top, prev_bottom])
+    top, bottom, next_top, prev_bottom, there = lax.optimization_barrier((top, bottom, next_top, prev_bottom, there))
+    far_top, far_bottom = to_left(next_top), to_right(prev_bottom)
+    next_bottom, prev_top = to_left(bottom), to_right(top)
+    pieces = [top, bottom, next_top, next_bottom, far_top, far_bottom, prev_top, prev_bottom]
     rows, column, ug = call(
         rows_kernel,
         [((256, 3 * HALF), BF), ((MAIN + TAIL, 3 * HALF), BF), ((PACK, 128), F32)],
-        [along_z.reshape(RHO, 2 * HALF + 256)],
+        [there, along_z.reshape(RHO, WIDTH)],
+        0,
+        [VMEM((SHARE, 256), F32)],
         flops=2 * 256 * 256 * 9 * 256,
         moved=2 * 10**6,
+    )
+    near, near_side = call(
+        near_kernel,
+        [((6, PACK, 128), BF), ((3, SIDE, HID), BF)],
+        [rows] + pieces[:4] + pieces[6:],
+        flops=2 * GROUP * 256 * 3 * HALF,
+        moved=4 * 10**6,
     )
     part, side = call(
         pre_kernel,
         [((NT, PACK, 128), BF), ((NX, SIDE, HID), F32)],
-        [place, rows] + pieces,
-        1,
-        [VMEM((NX, FULL, 3 * HALF), BF), pltpu.SemaphoreType.DMA((5,))],
-        2 * GROUP * 256 * 3 * HALF,
-        6 * 10**6,
-        range(2, 7),
-    )
-    columns = [column] + list(hold([to_left(column), across(column), to_right(column)]))
+        [place, rows, near, near_side] + pieces[4:6],
+        1,
+        flops=GROUP * 256 * HALF,
+        moved=2 * 10**6,
+    )
+    columns = [column, to_left(column), across(column), to_right(column)]
+    there = arrived(columns[1::2])
     parts = lax.all_to_all(part, ("y", "core"), 0, 0, tiled=True)
     low, sums = call(
         grad_kernel,
@@ -486,21 +490,16 @@
         [((RHO, 2 * HALF), BF)],
         [place, grad] + pieces,
         1,
-        [
-            VMEM((GROUP, 256), BF),
-            VMEM((NX, FULL, 3 * HALF), BF),
-            pltpu.SemaphoreType.DMA((5,)),
-        ],
+        [VMEM((GROUP, 256), BF)],
         2 * RHO * GROUP * (4 * HALF + 3 * 256),
         6 * 10**6,
-        range(2, 7),
-    )
-    px, moved, *columns = lax.optimization_barrier((px, moved, *columns))
+    )
+    px, moved, there = lax.optimization_barrier((px, moved, there))
     pz = lax.all_to_all(px.reshape(NZ, 16, 2 * HALF), "z", 0, 0, tiled=True)
     moved, = call(
         order_kernel,
         [((MOVED * NZ + 16, 128), BF)],
-        [place, moved],
+        [place, there, moved],
         1,
         [VMEM((RHO, 128), BF)],
         moved=10**6,
@@ -508,7 +507,7 @@
     moved = lax.all_gather(moved, ("y", "core"), axis=0)
     found, grad_bias = call(
         weight_kernel,
-        [((BR, MOST * DP, 3 * HALF), BF), ((1, HID), F32)],
+        [((BR, MOST * DP, 3 * HALF), BF), ((HID,), F32)],
         [place, moved] + columns,
         1,
         [VMEM((NT * BR * NZ, 640), BF), VMEM((NX, TAIL, 3 * HALF), BF)],
@@ -516,7 +515,7 @@
         5 * 10**6,
     )
     grad_slots, = call(slots_kernel, [((SLOTS, 3 * HALF), BF)], [pz], moved=10**6)
-    return grad_slots, grad_bias.reshape(HID), found.transpose(1, 0, 2)
+    return grad_slots, grad_bias, found.transpose(1, 0, 2)
 
 
 def solution(mesh):

time: 173 us -> 169 us (0.977)
  the two profiles are of different devices: /device:TPU:24 before, /device:TPU:32 now
where the time goes in v4:
time: 169 us; the launch traced here: 168 us
  starting transfers between devices  79.5 us (47%)
  Pallas kernels  27.5 us (16%)
  blocking collectives  27.1 us (16%)
  waiting for transfers between devices  24.4 us (14%)
  local copies, waits for them, and re-layouts  7.63 us (5%)
    pallas_call x10, Pallas kernels, call(): pl.pallas_call(kernel, out_shape=[jax.ShapeDtypeStruct(s, d) for s, d in...  26.3 us
    ppermute x4, starting transfers between devices, to_left(): return lax.ppermute(value, 'x', [(i, (i - 1) % NX) for i in range(NX)])  17.7 us
    all_to_all x1, starting transfers between devices, body(): lax.all_to_all(sent.reshape(DP, 16, 128), ('z', 'x'), 0, 0, tiled=True)  15.7 us
    all_to_all x1, starting transfers between devices, body(): along_z = lax.all_to_all(packed, 'z', 0, 0, tiled=True)  15.2 us
    all_to_all x1, waiting for transfers between devices, body(): along_z = lax.all_to_all(packed, 'z', 0, 0, tiled=True)  15.1 us
    all_gather x1, blocking collectives, body(): moved = lax.all_gather(moved, ('y', 'core'), axis=0)  14 us
    all_gather x1, blocking collectives, body(): grad = lax.all_gather(low, ('y', 'core'), axis=0)  13.1 us
    all_to_all x1, starting transfers between devices, body(): pz = lax.all_to_all(px.reshape(NZ, 16, 2 * HALF), 'z', 0, 0, tiled=True)  10.8 us
  transfers between devices with their start and end apart: 14, of which 6 were waited for; matrix products, arithmetic and copies ran while one was open for 0% of the time, Pallas kernels for 12%

profile of v4, /device:TPU:32, one launch (start us, length us, event | category | flops | bytes accessed | tf_op | source)
XLA Modules:
  0.0 167.7 jit_solution(15053584562274831917)
XLA Ops:
  0.6 0.6 pad_add_fusion.place
  1.2 3.9 %shard_map.85 = (bf16[208,1536]{1,0:T(8,128)(2,1)}, bf16[192,1536]{1,0:T(8,128)(2,1)}, bf16[16,16,1152]{2,1,0:T(8,128)(2,1)}) custom-call(s32[3]{0:T(128)} %pad_add_fusion.place, bf16[10,1536]{1,0:T(8,128)(2,1)} %x_in.1, bf16[10,24576]{1,0:T(8,128)(2,1)} %up_in.1, bf16[384,1536]{1,0:T(8,128)(2,1)} %w_in.1, f32[384]{0:T(512)} %bias_in.1, s32[1,64]{1,0:T(1,128)} %bitcast.15), custom_call_target="tpu_custom_call" | custom-call | flops 201326592 | bytes 5000000 | tf_op jit(solution)/shard_map/pallas_call | solution.py:57
  5.1 4.7 %collective-permute-start = (bf16[208,1536]{1,0:T(8,128)(2,1)}, bf16[208,1536]{1,0:T(8,128)(2,1)S(1)}, u32[]{:S(2)}, u32[]{:S(2)}) collective-permute-start(bf16[208,1536]{1,0:T(8,128)(2,1)} %get-tuple-element.31.refs_0_), channel_id=1, source_target_pairs={{0,24},{8,0},{16,8},{24,16},{1,25},{9,1},{17,9},{25,17},{2,26},{10... | collective-permute-start | bytes 1916936 | tf_op jit(solution)/shard_map/ppermute | solution.py:400
  9.8 1.9 %collective-permute-start.1 = (bf16[192,1536]{1,0:T(8,128)(2,1)}, bf16[192,1536]{1,0:T(8,128)(2,1)S(1)}, u32[]{:S(2)}, u32[]{:S(2)}) collective-permute-start(bf16[192,1536]{1,0:T(8,128)(2,1)} %get-tuple-element.32.refs_1_), channel_id=1, source_target_pairs={{0,8},{8,16},{16,24},{24,0},{1,9},{9,17},{17,25},{25,1},{2,10},{10... | collective-permute-start | bytes 1769480 | tf_op jit(solution)/shard_map/ppermute | solution.py:404
  11.7 15.2 %all-to-all-start = ((bf16[16,16,1152]{2,1,0:T(8,128)(2,1)}), bf16[16,16,1152]{2,1,0:T(8,128)(2,1)}, u32[]{:S(2)}, u32[]{:S(2)}) async-start(bf16[16,16,1152]{2,1,0:T(8,128)(2,1)} %get-tuple-element.29), calls=%async_computation | async-start | bytes 1179648 | tf_op jit(solution)/shard_map/all_to_all | solution.py:436
  27.0 0.9 collective-permute-done.1.refs_1_.refs_5_.refs_7_
  27.9 0.8 copy-done.6
  28.7 0.8 copy-done.1
  29.5 0.6 shard_map.86._
  30.1 1.9 %collective-permute-start.3 = (bf16[208,1536]{1,0:T(8,128)(2,1)S(1)}, bf16[208,1536]{1,0:T(8,128)(2,1)S(1)}, u32[]{:S(2)}, u32[]{:S(2)}) collective-permute-start(bf16[208,1536]{1,0:T(8,128)(2,1)S(1)} %copy-done), channel_id=1, source_target_pairs={{0,8},{8,16},{16,24},{24,0},{1,9},{9,17},{17,25},{25,1},{2,10},{10... | collective-permute-start | bytes 1916936 | tf_op jit(solution)/shard_map/ppermute | solution.py:404
  32.1 5.1 %collective-permute-start.2 = (bf16[192,1536]{1,0:T(8,128)(2,1)S(1)}, bf16[192,1536]{1,0:T(8,128)(2,1)S(1)}, u32[]{:S(2)}, u32[]{:S(2)}) collective-permute-start(bf16[192,1536]{1,0:T(8,128)(2,1)S(1)} %copy-done.4), channel_id=1, source_target_pairs={{0,24},{8,0},{16,8},{24,16},{1,25},{9,1},{17,9},{25,17},{2,26},{10... | collective-permute-start | bytes 1769480 | tf_op jit(solution)/shard_map/ppermute | solution.py:400
  37.2 3.0 %collective-permute-start.4 = (bf16[208,1536]{1,0:T(8,128)(2,1)}, bf16[208,1536]{1,0:T(8,128)(2,1)S(1)}, u32[]{:S(2)}, u32[]{:S(2)}) collective-permute-start(bf16[208,1536]{1,0:T(8,128)(2,1)} %copy-done.1), channel_id=1, source_target_pairs={{0,24},{8,0},{16,8},{24,16},{1,25},{9,1},{17,9},{25,17},{2,26},{10... | collective-permute-start | bytes 1916936 | tf_op jit(solution)/shard_map/ppermute | solution.py:400
  40.2 2.8 %collective-permute-start.5 = (bf16[192,1536]{1,0:T(8,128)(2,1)}, bf16[192,1536]{1,0:T(8,128)(2,1)}, u32[]{:S(2)}, u32[]{:S(2)}) collective-permute-start(bf16[192,1536]{1,0:T(8,128)(2,1)} %copy-done.6), channel_id=1, source_target_pairs={{0,8},{8,16},{16,24},{24,0},{1,9},{9,17},{17,25},{25,1},{2,10},{10... | collective-permute-start | bytes 1769480 | tf_op jit(solution)/shard_map/ppermute | solution.py:404
  43.1 15.1 %all-to-all-done = bf16[16,16,1152]{2,1,0:T(8,128)(2,1)} async-done(((bf16[16,16,1152]{2,1,0:T(8,128)(2,1)}), bf16[16,16,1152]{2,1,0:T(8,128)(2,1)}, u32[]{:S(2)}, u32[]{:S(2)}) %all-to-all-start) | async-done | bytes 589856 | tf_op jit(solution)/shard_map/all_to_all | solution.py:436
  58.2 0.7 copy-done.15
  58.8 2.3 %shard_map.87 = (bf16[256,1536]{1,0:T(8,128)(2,1)S(1)}, bf16[160,1536]{1,0:T(8,128)(2,1)}, f32[240,128]{1,0:T(8,128)S(1)}) custom-call(f32[8,128]{1,0:T(8,128)S(1)} %copy-done.15, bf16[256,1152]{1,0:T(8,128)(2,1)} %bitcast.4.rz_ref), custom_call_target="tpu_custom_call" | custom-call | flops 301989888 | bytes 2000000 | tf_op jit(solution)/shard_map/pallas_call | solution.py:57
  61.2 0.0 collective-permute-done.2.refs_3_
  61.2 0.0 collective-permute-done.3.refs_4_.refs_6_
  61.2 1.3 copy-done.2
  62.5 1.1 copy-done.7
  63.6 1.7 shard_map.88
  65.2 0.0 copy-start.14
  65.2 0.0 collective-permute-done.5.bottom_ref.refs_5_
  65.2 0.0 collective-permute-done.4.top_ref.refs_4_
  65.3 2.6 %shard_map.89 = (bf16[8,240,128]{2,1,0:T(8,128)(2,1)}, f32[4,16,384]{2,1,0:T(8,128)S(1)}) custom-call(s32[3]{0:T(128)S(1)} %copy-done.12, bf16[256,1536]{1,0:T(8,128)(2,1)S(1)} %get-tuple-element.30.x_ref, bf16[6,240,128]{2,1,0:T(8,128)(2,1)S(1)} %get-tuple-element.35.near_ref, bf16[3,16,384]{2,1,0:T(8,128)(2,1)S(1)} %get-tuple-element.36.near_side, ...), custom_call_target="tpu_custom_call" | custom-call | flops 201326592 | bytes 2000000 | tf_op jit(solution)/shard_map/pallas_call | solution.py:57
  67.8 4.5 %all-to-all-start.1 = ((bf16[8,240,128]{2,1,0:T(8,128)(2,1)}), bf16[8,240,128]{2,1,0:T(8,128)(2,1)S(1)}, u32[]{:S(2)}, u32[]{:S(2)}) async-start(bf16[8,240,128]{2,1,0:T(8,128)(2,1)} %get-tuple-element.37), calls=%async_computation.1 | async-start | bytes 983040 | tf_op jit(solution)/shard_map/all_to_all | solution.py:468
  72.3 2.2 %collective-permute-start.8 = (bf16[160,1536]{1,0:T(8,128)(2,1)}, bf16[160,1536]{1,0:T(8,128)(2,1)}, u32[]{:S(2)}, u32[]{:S(2)}) collective-permute-start(bf16[160,1536]{1,0:T(8,128)(2,1)} %get-tuple-element.43.refs_0_), channel_id=1, source_target_pairs={{0,8},{8,16},{16,24},{24,0},{1,9},{9,17},{17,25},{25,1},{2,10},{10... | collective-permute-start | bytes 1474568 | tf_op jit(solution)/shard_map/ppermute | solution.py:404
  74.5 4.9 %collective-permute-start.7 = (bf16[160,1536]{1,0:T(8,128)(2,1)}, bf16[160,1536]{1,0:T(8,128)(2,1)}, u32[]{:S(2)}, u32[]{:S(2)}) collective-permute-start(bf16[160,1536]{1,0:T(8,128)(2,1)} %get-tuple-element.43.refs_0_), channel_id=1, source_target_pairs={{0,24},{8,0},{16,8},{24,16},{1,25},{9,1},{17,9},{25,17},{2,26},{10... | collective-permute-start | bytes 1474568 | tf_op jit(solution)/shard_map/ppermute | solution.py:400
  79.3 2.9 %all-to-all-done.1.parts_ref = bf16[8,240,128]{2,1,0:T(8,128)(2,1)S(1)} async-done(((bf16[8,240,128]{2,1,0:T(8,128)(2,1)}), bf16[8,240,128]{2,1,0:T(8,128)(2,1)S(1)}, u32[]{:S(2)}, u32[]{:S(2)}) %all-to-all-start.1) | async-done | bytes 491552 | tf_op jit(solution)/shard_map/all_to_all | solution.py:468
  82.3 1.2 shard_map.90
  83.5 1.9 %collective-permute-start.6 = (bf16[240,128]{1,0:T(8,128)(2,1)S(1)}, bf16[240,128]{1,0:T(8,128)(2,1)S(1)}, u32[]{:S(2)}, u32[]{:S(2)}) collective-permute-start(bf16[240,128]{1,0:T(8,128)(2,1)S(1)} %get-tuple-element.42.low_ref), channel_id=1, source_target_pairs={{0,1},{1,0},{2,3},{3,2},{4,5},{5,4},{6,7},{7,6},{8,9},{9,8},{10,11... | collective-permute-start | bytes 184328 | tf_op jit(solution)/shard_map/ppermute | solution.py:476
  85.4 1.2 collective-permute-done.6.other_ref
  86.6 1.8 %shard_map.91 = bf16[1024,128]{1,0:T(8,128)(2,1)} custom-call(s32[3]{0:T(128)S(1)} %copy-done.12, bf16[240,128]{1,0:T(8,128)(2,1)S(1)} %get-tuple-element.42.low_ref, bf16[240,128]{1,0:T(8,128)(2,1)S(1)} %collective-permute-done.6.other_ref, bf16[16,128]{1,0:T(8,128)(2,1)S(1)} %get-tuple-element.41.sums_ref, f32[4,16,384]{2,1,0:T(8,128)S(1)} %get-tuple-element.39.side_ref), custom_call_target="tpu_custom_call" | custom-call | flops 75497472 | bytes 1000000 | tf_op jit(solution)/shard_map/pallas_call | solution.py:57
  88.5 15.7 %all-to-all-start.2 = ((bf16[64,16,128]{2,1,0:T(8,128)(2,1)}), bf16[64,16,128]{2,1,0:T(8,128)(2,1)S(1)}, u32[]{:S(2)}, u32[]{:S(2)}) async-start(bf16[64,16,128]{2,1,0:T(8,128)(2,1)} %bitcast.7), calls=%async_computation.2 | async-start | bytes 524288 | tf_op jit(solution)/shard_map/all_to_all | solution.py:485
  104.2 0.6 shard_map.93._
  104.8 13.1 %all-gather = bf16[1920,128]{1,0:T(8,128)(2,1)S(1)} all-gather(bf16[240,128]{1,0:T(8,128)(2,1)S(1)} %get-tuple-element.42.low_ref), channel_id=2, replica_groups=mesh['z'=16,'x'=4,'y'=4,'core'=2] {'y','core'}, dimensions={0}, use_global_device_ids=true | all-gather | bytes 552960 | tf_op jit(solution)/shard_map/all_gather | solution.py:487
  117.9 1.1 copy-done.5
  119.0 1.1 copy-done.10
  120.0 4.1 %shard_map.92 = bf16[256,1024]{1,0:T(8,128)(2,1)S(1)} custom-call(s32[3]{0:T(128)S(1)} %copy-done.12, bf16[8,240,128]{2,1,0:T(8,128)(2,1)S(1)} %bitcast.13, bf16[208,1536]{1,0:T(8,128)(2,1)S(1)} %copy-done, bf16[192,1536]{1,0:T(8,128)(2,1)S(1)} %copy-done.5, bf16[208,1536]{1,0:T(8,128)(2,1)S(1)} %copy-done.3, bf16[192,1536]{1,0:T(8,128)(2,1)S(1)} %copy-done.10, ...), custom_call_target="tpu_custom_call" | custom-call | flops 2214592512 | bytes 6000000 | tf_op jit(solution)/shard_map/pallas_call | solution.py:57
  124.2 0.8 copy-done.11
  124.9 1.3 all-to-all-done.2.in_ref
  126.3 10.8 %all-to-all-start.3 = ((bf16[16,16,1024]{2,1,0:T(8,128)(2,1)}), bf16[16,16,1024]{2,1,0:T(8,128)(2,1)S(1)}, u32[]{:S(2)}, u32[]{:S(2)}) async-start(bf16[16,16,1024]{2,1,0:T(8,128)(2,1)} %bitcast.12), calls=%async_computation.3 | async-start | bytes 1048576 | tf_op jit(solution)/shard_map/all_to_all | solution.py:498
  137.1 4.9 %collective-permute-start.9 = (bf16[160,1536]{1,0:T(8,128)(2,1)}, bf16[160,1536]{1,0:T(8,128)(2,1)S(1)}, u32[]{:S(2)}, u32[]{:S(2)}) collective-permute-start(bf16[160,1536]{1,0:T(8,128)(2,1)} %get-tuple-element.43.refs_0_), channel_id=1, source_target_pairs={{0,16},{8,24},{16,0},{24,8},{1,17},{9,25},{17,1},{25,9},{2,18},{10... | collective-permute-start | bytes 1474568 | tf_op jit(solution)/shard_map/ppermute | solution.py:408
  142.0 1.1 shard_map.95
  143.1 14.0 %all-gather.1 = bf16[3968,128]{1,0:T(8,128)(2,1)S(1)} all-gather(bf16[496,128]{1,0:T(8,128)(2,1)S(1)} %shard_map.95), channel_id=3, replica_groups=mesh['z'=16,'x'=4,'y'=4,'core'=2] {'y','core'}, dimensions={0}, use_global_device_ids=true | all-gather | bytes 1142784 | tf_op jit(solution)/shard_map/all_gather | solution.py:507
  157.1 6.8 %shard_map.96 = (bf16[6,128,1536]{2,1,0:T(8,128)(2,1)}, f32[384]{0:T(512)}) custom-call(s32[3]{0:T(128)S(1)} %copy-done.12, bf16[8,496,128]{2,1,0:T(8,128)(2,1)S(1)} %bitcast.11, bf16[160,1536]{1,0:T(8,128)(2,1)} %get-tuple-element.43.refs_0_, bf16[160,1536]{1,0:T(8,128)(2,1)} %collective-permute-done.7.refs_0_.refs_1_, ...), custom_call_target="tpu_custom_call" | custom-call | flops 1509949440 | bytes 5000000 | tf_op jit(solution)/shard_map/pallas_call | solution.py:57
  163.9 2.9 %all-to-all-done.3.in_ref = bf16[16,16,1024]{2,1,0:T(8,128)(2,1)S(1)} async-done(((bf16[16,16,1024]{2,1,0:T(8,128)(2,1)}), bf16[16,16,1024]{2,1,0:T(8,128)(2,1)S(1)}, u32[]{:S(2)}, u32[]{:S(2)}) %all-to-all-start.3) | async-done | bytes 524320 | tf_op jit(solution)/shard_map/all_to_all | solution.py:498
  166.9 0.8 shard_map.94
  (27 shorter events, 0.1 us)
Async XLA Ops:
  5.1 22.8 %collective-permute-start = (bf16[208,1536]{1,0:T(8,128)(2,1)}, bf16[208,1536]{1,0:T(8,128)(2,1)S(1)}, u32[]{:S(2)}, u32[]{:S(2)}) collective-permute-start(bf16[208,1536]{1,0:T(8,128)(2,1)} %get-tuple-element.31.refs_0_), channel_id=1, source_target_pairs={{0,24},{8,0},{16,8},{24,16},{1,25},{9,1},{17,9},{25,17},{2,26},{10... | collective-permute-start | bytes 1916936 | tf_op jit(solution)/shard_map/ppermute | solution.py:400
  9.8 18.1 %collective-permute-start.1 = (bf16[192,1536]{1,0:T(8,128)(2,1)}, bf16[192,1536]{1,0:T(8,128)(2,1)S(1)}, u32[]{:S(2)}, u32[]{:S(2)}) collective-permute-start(bf16[192,1536]{1,0:T(8,128)(2,1)} %get-tuple-element.32.refs_1_), channel_id=1, source_target_pairs={{0,8},{8,16},{16,24},{24,0},{1,9},{9,17},{17,25},{25,1},{2,10},{10... | collective-permute-start | bytes 1769480 | tf_op jit(solution)/shard_map/ppermute | solution.py:404
  11.7 46.4 %all-to-all-start = ((bf16[16,16,1152]{2,1,0:T(8,128)(2,1)}), bf16[16,16,1152]{2,1,0:T(8,128)(2,1)}, u32[]{:S(2)}, u32[]{:S(2)}) async-start(bf16[16,16,1152]{2,1,0:T(8,128)(2,1)} %get-tuple-element.29), calls=%async_computation | async-start | bytes 1179648 | tf_op jit(solution)/shard_map/all_to_all | solution.py:436
  26.9 3.2 %copy-start = (bf16[208,1536]{1,0:T(8,128)(2,1)S(1)}, bf16[208,1536]{1,0:T(8,128)(2,1)}, u32[]{:S(2)}) copy-start(bf16[208,1536]{1,0:T(8,128)(2,1)} %get-tuple-element.31.refs_0_) | copy-start | bytes 1916932
  26.9 5.1 %copy-start.4 = (bf16[192,1536]{1,0:T(8,128)(2,1)S(1)}, bf16[192,1536]{1,0:T(8,128)(2,1)}, u32[]{:S(2)}) copy-start(bf16[192,1536]{1,0:T(8,128)(2,1)} %get-tuple-element.32.refs_1_) | copy-start | bytes 1769476
  27.9 0.8 copy-start.6
  28.7 0.8 copy-start.1
  30.1 31.1 %collective-permute-start.3 = (bf16[208,1536]{1,0:T(8,128)(2,1)S(1)}, bf16[208,1536]{1,0:T(8,128)(2,1)S(1)}, u32[]{:S(2)}, u32[]{:S(2)}) collective-permute-start(bf16[208,1536]{1,0:T(8,128)(2,1)S(1)} %copy-done), channel_id=1, source_target_pairs={{0,8},{8,16},{16,24},{24,0},{1,9},{9,17},{17,25},{25,1},{2,10},{10... | collective-permute-start | bytes 1916936 | tf_op jit(solution)/shard_map/ppermute | solution.py:404
  32.1 29.1 %collective-permute-start.2 = (bf16[192,1536]{1,0:T(8,128)(2,1)S(1)}, bf16[192,1536]{1,0:T(8,128)(2,1)S(1)}, u32[]{:S(2)}, u32[]{:S(2)}) collective-permute-start(bf16[192,1536]{1,0:T(8,128)(2,1)S(1)} %copy-done.4), channel_id=1, source_target_pairs={{0,24},{8,0},{16,8},{24,16},{1,25},{9,1},{17,9},{25,17},{2,26},{10... | collective-permute-start | bytes 1769480 | tf_op jit(solution)/shard_map/ppermute | solution.py:400
  37.2 28.0 %collective-permute-start.4 = (bf16[208,1536]{1,0:T(8,128)(2,1)}, bf16[208,1536]{1,0:T(8,128)(2,1)S(1)}, u32[]{:S(2)}, u32[]{:S(2)}) collective-permute-start(bf16[208,1536]{1,0:T(8,128)(2,1)} %copy-done.1), channel_id=1, source_target_pairs={{0,24},{8,0},{16,8},{24,16},{1,25},{9,1},{17,9},{25,17},{2,26},{10... | collective-permute-start | bytes 1916936 | tf_op jit(solution)/shard_map/ppermute | solution.py:400
  40.2 25.0 %collective-permute-start.5 = (bf16[192,1536]{1,0:T(8,128)(2,1)}, bf16[192,1536]{1,0:T(8,128)(2,1)}, u32[]{:S(2)}, u32[]{:S(2)}) collective-permute-start(bf16[192,1536]{1,0:T(8,128)(2,1)} %copy-done.6), channel_id=1, source_target_pairs={{0,8},{8,16},{16,24},{24,0},{1,9},{9,17},{17,25},{25,1},{2,10},{10... | collective-permute-start | bytes 1769480 | tf_op jit(solution)/shard_map/ppermute | solution.py:404
  58.2 0.7 copy-start.15
  61.2 4.1 %copy-start.12 = (s32[3]{0:T(128)S(1)}, s32[3]{0:T(128)}, u32[]{:S(2)}) copy-start(s32[3]{0:T(128)} %pad_add_fusion.place) | copy-start | bytes 40
  61.2 6.6 %copy-start.9 = (bf16[192,1536]{1,0:T(8,128)(2,1)}, bf16[192,1536]{1,0:T(8,128)(2,1)S(1)}, u32[]{:S(2)}) copy-start(bf16[192,1536]{1,0:T(8,128)(2,1)S(1)} %collective-permute-done.2.refs_3_) | copy-start | bytes 1769476
  61.2 1.3 copy-start.2
  62.5 1.1 copy-start.7
  65.2 17.1 %copy-start.14 = (s32[64]{0:T(128)S(1)}, s32[64]{0:T(128)}, u32[]{:S(2)}) copy-start(s32[64]{0:T(128)} %param.7) | copy-start | bytes 772
  67.8 14.5 %all-to-all-start.1 = ((bf16[8,240,128]{2,1,0:T(8,128)(2,1)}), bf16[8,240,128]{2,1,0:T(8,128)(2,1)S(1)}, u32[]{:S(2)}, u32[]{:S(2)}) async-start(bf16[8,240,128]{2,1,0:T(8,128)(2,1)} %get-tuple-element.37), calls=%async_computation.1 | async-start | bytes 983040 | tf_op jit(solution)/shard_map/all_to_all | solution.py:468
  72.3 31.9 %collective-permute-start.8 = (bf16[160,1536]{1,0:T(8,128)(2,1)}, bf16[160,1536]{1,0:T(8,128)(2,1)}, u32[]{:S(2)}, u32[]{:S(2)}) collective-permute-start(bf16[160,1536]{1,0:T(8,128)(2,1)} %get-tuple-element.43.refs_0_), channel_id=1, source_target_pairs={{0,8},{8,16},{16,24},{24,0},{1,9},{9,17},{17,25},{25,1},{2,10},{10... | collective-permute-start | bytes 1474568 | tf_op jit(solution)/shard_map/ppermute | solution.py:404
  74.5 29.7 %collective-permute-start.7 = (bf16[160,1536]{1,0:T(8,128)(2,1)}, bf16[160,1536]{1,0:T(8,128)(2,1)}, u32[]{:S(2)}, u32[]{:S(2)}) collective-permute-start(bf16[160,1536]{1,0:T(8,128)(2,1)} %get-tuple-element.43.refs_0_), channel_id=1, source_target_pairs={{0,24},{8,0},{16,8},{24,16},{1,25},{9,1},{17,9},{25,17},{2,26},{10... | collective-permute-start | bytes 1474568 | tf_op jit(solution)/shard_map/ppermute | solution.py:400
  83.5 3.1 %collective-permute-start.6 = (bf16[240,128]{1,0:T(8,128)(2,1)S(1)}, bf16[240,128]{1,0:T(8,128)(2,1)S(1)}, u32[]{:S(2)}, u32[]{:S(2)}) collective-permute-start(bf16[240,128]{1,0:T(8,128)(2,1)S(1)} %get-tuple-element.42.low_ref), channel_id=1, source_target_pairs={{0,1},{1,0},{2,3},{3,2},{4,5},{5,4},{6,7},{7,6},{8,9},{9,8},{10,11... | collective-permute-start | bytes 184328 | tf_op jit(solution)/shard_map/ppermute | solution.py:476
  88.5 37.8 %all-to-all-start.2 = ((bf16[64,16,128]{2,1,0:T(8,128)(2,1)}), bf16[64,16,128]{2,1,0:T(8,128)(2,1)S(1)}, u32[]{:S(2)}, u32[]{:S(2)}) async-start(bf16[64,16,128]{2,1,0:T(8,128)(2,1)} %bitcast.7), calls=%async_computation.2 | async-start | bytes 524288 | tf_op jit(solution)/shard_map/all_to_all | solution.py:485
  104.2 13.7 %copy-start.3 = (bf16[208,1536]{1,0:T(8,128)(2,1)S(1)}, bf16[208,1536]{1,0:T(8,128)(2,1)}, u32[]{:S(2)}) copy-start(bf16[208,1536]{1,0:T(8,128)(2,1)} %copy-done.1) | copy-start | bytes 1916932
  104.2 13.7 %copy-start.8 = (bf16[192,1536]{1,0:T(8,128)(2,1)S(1)}, bf16[192,1536]{1,0:T(8,128)(2,1)}, u32[]{:S(2)}) copy-start(bf16[192,1536]{1,0:T(8,128)(2,1)} %copy-done.6) | copy-start | bytes 1769476
  117.9 1.1 copy-start.5
  119.0 1.1 copy-start.10
  120.0 21.9 %copy-start.13 = (f32[8,128]{1,0:T(8,128)S(1)}, f32[8,128]{1,0:T(8,128)}, u32[]{:S(2)}) copy-start(f32[8,128]{1,0:T(8,128)} %shard_map.93._) | copy-start | bytes 12292
  124.1 0.8 copy-start.11
  126.3 40.6 %all-to-all-start.3 = ((bf16[16,16,1024]{2,1,0:T(8,128)(2,1)}), bf16[16,16,1024]{2,1,0:T(8,128)(2,1)S(1)}, u32[]{:S(2)}, u32[]{:S(2)}) async-start(bf16[16,16,1024]{2,1,0:T(8,128)(2,1)} %bitcast.12), calls=%async_computation.3 | async-start | bytes 1048576 | tf_op jit(solution)/shard_map/all_to_all | solution.py:498
  137.1 20.0 %collective-permute-start.9 = (bf16[160,1536]{1,0:T(8,128)(2,1)}, bf16[160,1536]{1,0:T(8,128)(2,1)S(1)}, u32[]{:S(2)}, u32[]{:S(2)}) collective-permute-start(bf16[160,1536]{1,0:T(8,128)(2,1)} %get-tuple-element.43.refs_0_), channel_id=1, source_target_pairs={{0,16},{8,24},{16,0},{24,8},{1,17},{9,25},{17,1},{25,9},{2,18},{10... | collective-permute-start | bytes 1474568 | tf_op jit(solution)/shard_map/ppermute | solution.py:408

commit v5 on v4

--- a/solution.py
+++ b/solution.py
@@ -28,6 +28,8 @@
 LIMIT = 16 * 1024 * 1024
 LARGE = 56 * 1024 * 1024
 WIDTH = 2 * HALF + 128
+TILES = 3 * HALF // 128
+ROWS = SLOTS * TILES
 
 
 def iota(shape, dim):
@@ -151,8 +153,8 @@
     return jnp.where(i < MAIN, i // 8, tail // 2), jnp.where(i < MAIN, i % 8, 8 + tail % 2)
 
 
-def selector(third, flip=False):
-    i, rho = iota((256, RHO), 1 if flip else 0), iota((256, RHO), 0 if flip else 1)
+def selector(third):
+    i, rho = iota((256, RHO), 0), iota((256, RHO), 1)
     z, slot = slot_of(i)
     if third == 0:
         return onehot(rho == z * 16 + slot)
@@ -167,24 +169,28 @@
     return found
 
 
-def rows_kernel(_, rz_ref, x_ref, column_ref, ug_out, ug_ref):
-    left, right, ups = rz_ref[:, :HALF], rz_ref[:, HALF : 2 * HALF], rz_ref[:, 2 * HALF :]
-    first, even, odd = selector(0), selector(1), selector(2)
+def select_rows(rz_ref, x_ref, column_ref):
+    left, right = rz_ref[:, :HALF], rz_ref[:, HALF : 2 * HALF]
+    first = selector(0)
     x_ref[:, :HALF] = dot(first, left).astype(BF)
     x_ref[:, HALF : 2 * HALF] = dot(first, right).astype(BF)
-    x_ref[:, 2 * HALF :] = (dot(even, left) + dot(odd, right)).astype(BF)
+    x_ref[:, 2 * HALF :] = (dot(selector(1), left) + dot(selector(2), right)).astype(BF)
+    column_ref[...] = x_ref[: MAIN + TAIL, :]
+
+
+def ups_kernel(rz_ref, ug_ref, held):
+    ups = rz_ref[:, 2 * HALF :]
     r, c = iota((128, 128), 0), iota((128, 128), 1)
     low, high = dot(ups, onehot((r == c) & (r < 64))).astype(BF), dot(ups, onehot(r == c + 64)).astype(BF)
     for part, rest in (
-        (dot(first, ups), slice(0, 128)),
-        (dot(even, low) + dot(odd, high), slice(128, SHARE)),
+        (dot(selector(0), ups), slice(0, 128)),
+        (dot(selector(1), low) + dot(selector(2), high), slice(128, SHARE)),
     ):
         main, tail = part[:MAIN].T, part[MAIN:].T
-        ug_ref[rest, :MAIN] = main[: rest.stop - rest.start]
-        ug_ref[rest, MAIN:] = tail[: rest.stop - rest.start]
-    ug_out[:SHARE, :] = ug_ref[:, :MAIN]
-    ug_out[SHARE:, :] = by_quarter([ug_ref[g * QUARTER : (g + 1) * QUARTER, MAIN:] for g in range(4)])
-    column_ref[...] = x_ref[: MAIN + TAIL, :]
+        held[rest, :MAIN] = main[: rest.stop - rest.start]
+        held[rest, MAIN:] = tail[: rest.stop - rest.start]
+    ug_ref[:SHARE, :] = held[:, :MAIN]
+    ug_ref[SHARE:, :] = by_quarter([held[g * QUARTER : (g + 1) * QUARTER, MAIN:] for g in range(4)])
 
 
 def partial(piece, start, x, out):
@@ -194,8 +200,9 @@
     out[SHARE:, :] = by_quarter(tail).astype(BF)
 
 
-def near_kernel(x_ref, *refs):
-    pieces, (out_ref, side_ref) = refs[:6], refs[6:]
+def near_kernel(rz_ref, *refs):
+    pieces, (x_ref, column_ref, out_ref, side_ref) = refs[:6], refs[6:]
+    select_rows(rz_ref, x_ref, column_ref)
     x = x_ref[...]
     for n, piece in enumerate(pieces):
         partial(piece, SIDE if n % 2 == 0 else 0, x, out_ref.at[n])
@@ -298,20 +305,32 @@
         full[n * SHARE : (n + 1) * SHARE, :MAIN] = g_ref[j, :SHARE, :]
         full[n * SHARE : (n + 1) * SHARE, MAIN:] = unpacked(g_ref[j, SHARE:PACK, :])
     g = full[...]
-    here = [dot_nt(selector(i, True), g).astype(BF) for i in range(3)]
-    total = [jnp.zeros((RHO, HALF), F32), jnp.zeros((RHO, HALF), F32)]
+    rho, lane = iota((2 * MAIN, 256), 0), iota((2 * MAIN, 256), 1)
+    tail = (lane >= MAIN) & (lane % TAIL == (rho - MAIN) // 4)
+    tail = tail & (rho >= MAIN)
+    here = dot_nt(onehot(tail | ((lane == rho) & (rho < MAIN))), g).astype(BF)
+    total = jnp.zeros((2 * MAIN, 3 * HALF), F32)
     for n, piece in enumerate(pieces):
-        span = slice(n * SHARE, (n + 1) * SHARE)
         start = SIDE if n % 2 == 0 else 0
-        last = piece[start:, 2 * HALF :]
-        for side in range(2):
-            part = dot(here[0][:, span], piece[start:, side * HALF : (side + 1) * HALF])
-            total[side] = total[side] + part + dot(here[1 + side][:, span], last)
-    for side in range(2):
-        px_ref[:, side * HALF : (side + 1) * HALF] = total[side].astype(BF)
-
-
-def order_kernel(place, _, in_ref, out_ref, block):
+        total = total + dot(here[:, n * SHARE : (n + 1) * SHARE], piece[start:, :])
+    tiles = [total[:MAIN, t * 128 : (t + 1) * 128] for t in range(TILES)]
+    quarter = iota((MAIN, 128), 0) % 4
+    for i in range(TILES // 4):
+        tile = jnp.zeros((MAIN, 128), F32)
+        for q in range(4):
+            t = 4 * i + q
+            tile = jnp.where(quarter == q, total[MAIN:, t * 128 : (t + 1) * 128], tile)
+        tiles.append(tile)
+    for z in range(NZ):
+        blocks = [tile[z * 8 : (z + 1) * 8] for tile in tiles]
+        for u in range(len(blocks) // 2):
+            both = jnp.concatenate([blocks[2 * u], blocks[2 * u + 1]], axis=0)
+            px_ref[z, u * 16 : (u + 1) * 16, :] = both.astype(BF)
+        px_ref[z, ROWS - 8 :, :] = blocks[-1].astype(BF)
+
+
+def order_kernel(place, in_ref, weights_there, columns_there, out_ref, block):
+    del weights_there, columns_there
     n = BR * NZ
     r, c = iota((2 * n, RHO), 0), iota((2 * n, RHO), 1)
     row = r // NZ
@@ -336,21 +355,21 @@
     out_ref[MOVED * NZ :, :] = parts.astype(BF)
 
 
-def slots_kernel(in_ref, out_ref):
+def slots_kernel(in_ref, out_ref, held):
     total = in_ref[0].astype(F32)
     for z in range(1, NZ):
         total = total + in_ref[z].astype(F32)
-    total = total.astype(BF)
-    left, right = total[:, :HALF], total[:, HALF:]
-    r, c = iota((16, 16), 0), iota((16, 16), 1)
-    halfway = (c - SLOTS) * 2
-    last = dot(onehot(r == halfway), left) + dot(onehot(r == halfway + 1), right)
-    out_ref[:, : 2 * HALF] = total[:SLOTS]
-    out_ref[:, 2 * HALF :] = last[:SLOTS].astype(BF)
+    for t in range(TILES):
+        span = slice(t * 128, (t + 1) * 128)
+        held[:8, span] = total[t * 8 : (t + 1) * 8]
+        for s in range(2):
+            row = 8 * TILES + t // 4 * 8 + s * 4 + t % 4
+            held[8 + s : 9 + s, span] = total[row : row + 1]
+    out_ref[...] = held[:SLOTS, :].astype(BF)
 
 
 def weight_kernel(place, m_ref, *refs):
-    columns, (out_ref, bias_ref, found, tails) = refs[:NX], refs[NX:]
+    columns, (out_ref, bias_ref, found, held) = refs[:NX], refs[NX:]
     lane, unit = iota((128, HID), 0), iota((128, HID), 1)
     row = iota((16, 128), 0)
     total = jnp.zeros((16, HID), F32)
@@ -371,15 +390,18 @@
                 found[row : row + NZ, k * 128 : (k + 1) * 128] = block[b * NZ : (b + 1) * NZ]
     r, c = iota((MOST * DP, MOST * DP), 0), iota((MOST * DP, MOST * DP), 1)
     order = onehot(c == r % NT * NZ + r // NT)
-    for k in range(NX):
-        tails[(place[1] + k) % NX] = columns[k][MAIN:, :]
-    tail = tails[...].reshape(NX * TAIL, 3 * HALF)
+    for k, column in enumerate(columns):
+        held[k * MAIN : (k + 1) * MAIN, :] = column[:MAIN, :]
+        start = pl.multiple_of(NX * MAIN + (place[1] + k) % NX * TAIL, TAIL)
+        held[pl.ds(start, TAIL), :] = column[MAIN:, :]
     for b in range(BR):
-        mine = dot(order, found[b * MOST * DP : (b + 1) * MOST * DP, :]).astype(BF)
-        total = dot(mine[:, NX * 128 :], tail)
-        for k in range(NX):
-            total = total + dot(mine[:, k * 128 : (k + 1) * 128], columns[k][:MAIN, :])
-        out_ref[b] = total.astype(BF)
+        span = slice(b * MOST * DP, (b + 1) * MOST * DP)
+        found[span, :] = dot(order, found[span, :]).astype(BF)
+    for third in range(3):
+        span = slice(third * HALF, (third + 1) * HALF)
+        total = dot(found[...], held[:, span]).astype(BF)
+        for b in range(BR):
+            out_ref[b, :, span] = total[b * MOST * DP : (b + 1) * MOST * DP]
 
 
 def arrived_kernel(*refs):
@@ -439,19 +461,10 @@
     far_top, far_bottom = to_left(next_top), to_right(prev_bottom)
     next_bottom, prev_top = to_left(bottom), to_right(top)
     pieces = [top, bottom, next_top, next_bottom, far_top, far_bottom, prev_top, prev_bottom]
-    rows, column, ug = call(
-        rows_kernel,
-        [((256, 3 * HALF), BF), ((MAIN + TAIL, 3 * HALF), BF), ((PACK, 128), F32)],
-        [there, along_z.reshape(RHO, WIDTH)],
-        0,
-        [VMEM((SHARE, 256), F32)],
-        flops=2 * 256 * 256 * 9 * 256,
-        moved=2 * 10**6,
-    )
-    near, near_side = call(
+    rows, column, near, near_side = call(
         near_kernel,
-        [((6, PACK, 128), BF), ((3, SIDE, HID), BF)],
-        [rows] + pieces[:4] + pieces[6:],
+        [((256, 3 * HALF), BF), ((MAIN + TAIL, 3 * HALF), BF), ((6, PACK, 128), BF), ((3, SIDE, HID), BF)],
+        [along_z.reshape(RHO, WIDTH)] + pieces[:4] + pieces[6:],
         flops=2 * GROUP * 256 * 3 * HALF,
         moved=4 * 10**6,
     )
@@ -463,8 +476,18 @@
         flops=GROUP * 256 * HALF,
         moved=2 * 10**6,
     )
+    part, along_z = lax.optimization_barrier((part, along_z))
+    ug, = call(
+        ups_kernel,
+        [((PACK, 128), F32)],
+        [along_z.reshape(RHO, WIDTH)],
+        0,
+        [VMEM((SHARE, 256), F32)],
+        flops=10**9,
+        moved=10**6,
+    )
     columns = [column, to_left(column), across(column), to_right(column)]
-    there = arrived(columns[1::2])
+    columns_there = arrived(columns[1::2])
     parts = lax.all_to_all(part, ("y", "core"), 0, 0, tiled=True)
     low, sums = call(
         grad_kernel,
@@ -487,19 +510,19 @@
     grad = lax.all_gather(low, ("y", "core"), axis=0)
     px, = call(
         out_kernel,
-        [((RHO, 2 * HALF), BF)],
+        [((NZ, ROWS, 128), BF)],
         [place, grad] + pieces,
         1,
         [VMEM((GROUP, 256), BF)],
         2 * RHO * GROUP * (4 * HALF + 3 * 256),
         6 * 10**6,
     )
-    px, moved, there = lax.optimization_barrier((px, moved, there))
-    pz = lax.all_to_all(px.reshape(NZ, 16, 2 * HALF), "z", 0, 0, tiled=True)
+    px, moved, columns_there = lax.optimization_barrier((px, moved, columns_there))
+    pz = lax.all_to_all(px, "z", 0, 0, tiled=True)
     moved, = call(
         order_kernel,
         [((MOVED * NZ + 16, 128), BF)],
-        [place, there, moved],
+        [place, moved, there, columns_there],
         1,
         [VMEM((RHO, 128), BF)],
         moved=10**6,
@@ -510,11 +533,13 @@
         [((BR, MOST * DP, 3 * HALF), BF), ((HID,), F32)],
         [place, moved] + columns,
         1,
-        [VMEM((NT * BR * NZ, 640), BF), VMEM((NX, TAIL, 3 * HALF), BF)],
+        [VMEM((NT * BR * NZ, 640), BF), VMEM((NX * (MAIN + TAIL), 3 * HALF), BF)],
         2 * 768 * 640 * 1536,
         5 * 10**6,
     )
-    grad_slots, = call(slots_kernel, [((SLOTS, 3 * HALF), BF)], [pz], moved=10**6)
+    grad_slots, = call(
+        slots_kernel, [((SLOTS, 3 * HALF), BF)], [pz], 0, [VMEM((16, 3 * HALF), F32)], moved=10**6
+    )
     return grad_slots, grad_bias, found.transpose(1, 0, 2)
 
 

time: 169 us -> 166 us (0.982)
  the two profiles are of different devices: /device:TPU:32 before, /device:TPU:24 now
where the time goes in v5:
time: 166 us; the launch traced here: 163 us
  starting transfers between devices  80.1 us (48%)
  blocking collectives  26.7 us (16%)
  Pallas kernels  24.3 us (15%)
  waiting for transfers between devices  23 us (14%)
  local copies, waits for them, and re-layouts  7.88 us (5%)
    pallas_call x10, Pallas kernels, call(): pl.pallas_call(kernel, out_shape=[jax.ShapeDtypeStruct(s, d) for s, d in...  23.2 us
    all_to_all x1, starting transfers between devices, body(): lax.all_to_all(sent.reshape(DP, 16, 128), ('z', 'x'), 0, 0, tiled=True)  17.7 us
    ppermute x4, starting transfers between devices, to_left(): return lax.ppermute(value, 'x', [(i, (i - 1) % NX) for i in range(NX)])  17.7 us
    all_to_all x1, starting transfers between devices, body(): along_z = lax.all_to_all(packed, 'z', 0, 0, tiled=True)  15.2 us
    all_gather x1, blocking collectives, body(): moved = lax.all_gather(moved, ('y', 'core'), axis=0)  13.6 us
    all_gather x1, blocking collectives, body(): grad = lax.all_gather(low, ('y', 'core'), axis=0)  13.1 us
    ppermute x4, starting transfers between devices, to_right(): return lax.ppermute(value, 'x', [(i, (i + 1) % NX) for i in range(NX)])  8.98 us
    all_to_all x1, starting transfers between devices, body(): pz = lax.all_to_all(px, 'z', 0, 0, tiled=True)  8.91 us
  transfers between devices with their start and end apart: 14, of which 7 were waited for; matrix products, arithmetic and copies ran while one was open for 0% of the time, Pallas kernels for 11%

profile of v5, /device:TPU:24, one launch (start us, length us, event | category | flops | bytes accessed | tf_op | source)
XLA Modules:
  0.0 163.5 jit_solution(3903182745384836292)
XLA Ops:
  0.6 0.6 pad_add_fusion.place
  1.2 3.9 %shard_map.85 = (bf16[208,1536]{1,0:T(8,128)(2,1)}, bf16[192,1536]{1,0:T(8,128)(2,1)}, bf16[16,16,1152]{2,1,0:T(8,128)(2,1)}) custom-call(s32[3]{0:T(128)} %pad_add_fusion.place, bf16[10,1536]{1,0:T(8,128)(2,1)} %x_in.1, bf16[10,24576]{1,0:T(8,128)(2,1)} %up_in.1, bf16[384,1536]{1,0:T(8,128)(2,1)} %w_in.1, f32[384]{0:T(512)} %bias_in.1, s32[1,64]{1,0:T(1,128)} %bitcast.16), custom_call_target="tpu_custom_call" | custom-call | flops 201326592 | bytes 5000000 | tf_op jit(solution)/shard_map/pallas_call | solution.py:59
  5.1 4.7 %collective-permute-start = (bf16[208,1536]{1,0:T(8,128)(2,1)}, bf16[208,1536]{1,0:T(8,128)(2,1)S(1)}, u32[]{:S(2)}, u32[]{:S(2)}) collective-permute-start(bf16[208,1536]{1,0:T(8,128)(2,1)} %get-tuple-element.30.refs_0_), channel_id=1, source_target_pairs={{0,24},{8,0},{16,8},{24,16},{1,25},{9,1},{17,9},{25,17},{2,26},{10... | collective-permute-start | bytes 1916936 | tf_op jit(solution)/shard_map/ppermute | solution.py:422
  9.8 1.9 %collective-permute-start.1 = (bf16[192,1536]{1,0:T(8,128)(2,1)}, bf16[192,1536]{1,0:T(8,128)(2,1)S(1)}, u32[]{:S(2)}, u32[]{:S(2)}) collective-permute-start(bf16[192,1536]{1,0:T(8,128)(2,1)} %get-tuple-element.31.refs_1_), channel_id=1, source_target_pairs={{0,8},{8,16},{16,24},{24,0},{1,9},{9,17},{17,25},{25,1},{2,10},{10... | collective-permute-start | bytes 1769480 | tf_op jit(solution)/shard_map/ppermute | solution.py:426
  11.7 15.2 %all-to-all-start = ((bf16[16,16,1152]{2,1,0:T(8,128)(2,1)}), bf16[16,16,1152]{2,1,0:T(8,128)(2,1)S(1)}, u32[]{:S(2)}, u32[]{:S(2)}) async-start(bf16[16,16,1152]{2,1,0:T(8,128)(2,1)} %get-tuple-element.27), calls=%async_computation | async-start | bytes 1179648 | tf_op jit(solution)/shard_map/all_to_all | solution.py:458
  27.0 0.0 copy-start.4
  27.0 0.9 collective-permute-done.1.refs_1_.refs_5_.refs_7_
  27.9 0.0 collective-permute-done.refs_0_.refs_2_
  27.9 0.8 copy-done.10
  28.7 0.9 copy-done.5
  29.6 0.6 shard_map.86.weights_there
  30.2 2.0 %collective-permute-start.3 = (bf16[208,1536]{1,0:T(8,128)(2,1)S(1)}, bf16[208,1536]{1,0:T(8,128)(2,1)S(1)}, u32[]{:S(2)}, u32[]{:S(2)}) collective-permute-start(bf16[208,1536]{1,0:T(8,128)(2,1)S(1)} %copy-done.4), channel_id=1, source_target_pairs={{0,8},{8,16},{16,24},{24,0},{1,9},{9,17},{17,25},{25,1},{2,10},{10... | collective-permute-start | bytes 1916936 | tf_op jit(solution)/shard_map/ppermute | solution.py:426
  32.2 5.1 %collective-permute-start.2 = (bf16[192,1536]{1,0:T(8,128)(2,1)}, bf16[192,1536]{1,0:T(8,128)(2,1)S(1)}, u32[]{:S(2)}, u32[]{:S(2)}) collective-permute-start(bf16[192,1536]{1,0:T(8,128)(2,1)} %get-tuple-element.31.refs_1_), channel_id=1, source_target_pairs={{0,24},{8,0},{16,8},{24,16},{1,25},{9,1},{17,9},{25,17},{2,26},{10... | collective-permute-start | bytes 1769480 | tf_op jit(solution)/shard_map/ppermute | solution.py:422
  37.4 3.0 %collective-permute-start.4 = (bf16[208,1536]{1,0:T(8,128)(2,1)}, bf16[208,1536]{1,0:T(8,128)(2,1)S(1)}, u32[]{:S(2)}, u32[]{:S(2)}) collective-permute-start(bf16[208,1536]{1,0:T(8,128)(2,1)} %copy-done.5), channel_id=1, source_target_pairs={{0,24},{8,0},{16,8},{24,16},{1,25},{9,1},{17,9},{25,17},{2,26},{10... | collective-permute-start | bytes 1916936 | tf_op jit(solution)/shard_map/ppermute | solution.py:422
  40.4 2.9 %collective-permute-start.5 = (bf16[192,1536]{1,0:T(8,128)(2,1)}, bf16[192,1536]{1,0:T(8,128)(2,1)S(1)}, u32[]{:S(2)}, u32[]{:S(2)}) collective-permute-start(bf16[192,1536]{1,0:T(8,128)(2,1)} %copy-done.10), channel_id=1, source_target_pairs={{0,8},{8,16},{16,24},{24,0},{1,9},{9,17},{17,25},{25,1},{2,10},{10... | collective-permute-start | bytes 1769480 | tf_op jit(solution)/shard_map/ppermute | solution.py:426
  43.2 8.2 %collective-permute-done.2.refs_3_ = bf16[192,1536]{1,0:T(8,128)(2,1)S(1)} collective-permute-done((bf16[192,1536]{1,0:T(8,128)(2,1)}, bf16[192,1536]{1,0:T(8,128)(2,1)S(1)}, u32[]{:S(2)}, u32[]{:S(2)}) %collective-permute-start.2) | collective-permute-done | bytes 589856 | tf_op jit(solution)/shard_map/ppermute | solution.py:422
  51.5 0.8 copy-done.13
  52.3 0.0 collective-permute-done.3.refs_4_.refs_6_
  52.3 5.3 %all-to-all-done = bf16[16,16,1152]{2,1,0:T(8,128)(2,1)S(1)} async-done(((bf16[16,16,1152]{2,1,0:T(8,128)(2,1)}), bf16[16,16,1152]{2,1,0:T(8,128)(2,1)S(1)}, u32[]{:S(2)}, u32[]{:S(2)}) %all-to-all-start) | async-done | bytes 589856 | tf_op jit(solution)/shard_map/all_to_all | solution.py:458
  57.6 1.1 copy-done.6
  58.7 1.1 copy-done.11
  59.8 1.1 copy-done.14
  60.8 3.0 %shard_map.87 = (bf16[256,1536]{1,0:T(8,128)(2,1)S(1)}, bf16[160,1536]{1,0:T(8,128)(2,1)S(1)}, bf16[6,240,128]{2,1,0:T(8,128)(2,1)S(1)}, bf16[3,16,384]{2,1,0:T(8,128)(2,1)S(1)}) custom-call(bf16[256,1152]{1,0:T(8,128)(2,1)S(1)} %bitcast.12, bf16[208,1536]{1,0:T(8,128)(2,1)S(1)} %copy-done.4, bf16[192,1536]{1,0:T(8,128)(2,1)} %get-tuple-element.31.refs_1_, ...), custom_call_target="tpu_custom_call" | custom-call | flops 1207959552 | bytes 4000000 | tf_op jit(solution)/shard_map/pallas_call | solution.py:59
  63.9 2.0 %shard_map.88 = (bf16[8,240,128]{2,1,0:T(8,128)(2,1)}, f32[4,16,384]{2,1,0:T(8,128)S(1)}) custom-call(s32[3]{0:T(128)S(1)} %copy-done, bf16[256,1536]{1,0:T(8,128)(2,1)S(1)} %get-tuple-element.34.x_ref, bf16[6,240,128]{2,1,0:T(8,128)(2,1)S(1)} %get-tuple-element.35.near_ref, bf16[3,16,384]{2,1,0:T(8,128)(2,1)S(1)} %get-tuple-element.36.near_side, ...), custom_call_target="tpu_custom_call" | custom-call | flops 201326592 | bytes 2000000 | tf_op jit(solution)/shard_map/pallas_call | solution.py:59
  65.9 4.8 %all-to-all-start.1 = ((bf16[8,240,128]{2,1,0:T(8,128)(2,1)}), bf16[8,240,128]{2,1,0:T(8,128)(2,1)S(1)}, u32[]{:S(2)}, u32[]{:S(2)}) async-start(bf16[8,240,128]{2,1,0:T(8,128)(2,1)} %get-tuple-element.38), calls=%async_computation.1 | async-start | bytes 983040 | tf_op jit(solution)/shard_map/all_to_all | solution.py:491
  70.8 2.2 %collective-permute-start.8 = (bf16[160,1536]{1,0:T(8,128)(2,1)}, bf16[160,1536]{1,0:T(8,128)(2,1)}, u32[]{:S(2)}, u32[]{:S(2)}) collective-permute-start(bf16[160,1536]{1,0:T(8,128)(2,1)} %copy-done.16), channel_id=1, source_target_pairs={{0,8},{8,16},{16,24},{24,0},{1,9},{9,17},{17,25},{25,1},{2,10},{10... | collective-permute-start | bytes 1474568 | tf_op jit(solution)/shard_map/ppermute | solution.py:426
  72.9 4.9 %collective-permute-start.7 = (bf16[160,1536]{1,0:T(8,128)(2,1)}, bf16[160,1536]{1,0:T(8,128)(2,1)}, u32[]{:S(2)}, u32[]{:S(2)}) collective-permute-start(bf16[160,1536]{1,0:T(8,128)(2,1)} %copy-done.16), channel_id=1, source_target_pairs={{0,24},{8,0},{16,8},{24,16},{1,25},{9,1},{17,9},{25,17},{2,26},{10... | collective-permute-start | bytes 1474568 | tf_op jit(solution)/shard_map/ppermute | solution.py:422
  77.8 0.4 shard_map.89.ug_ref
  78.3 0.4 all-to-all-done.1.parts_ref
  78.7 1.2 shard_map.90
  79.9 1.9 %collective-permute-start.6 = (bf16[240,128]{1,0:T(8,128)(2,1)S(1)}, bf16[240,128]{1,0:T(8,128)(2,1)S(1)}, u32[]{:S(2)}, u32[]{:S(2)}) collective-permute-start(bf16[240,128]{1,0:T(8,128)(2,1)S(1)} %get-tuple-element.43.low_ref), channel_id=1, source_target_pairs={{0,1},{1,0},{2,3},{3,2},{4,5},{5,4},{6,7},{7,6},{8,9},{9,8},{10,11... | collective-permute-start | bytes 184328 | tf_op jit(solution)/shard_map/ppermute | solution.py:499
  81.8 1.2 collective-permute-done.6.other_ref
  83.0 1.8 %shard_map.91 = bf16[1024,128]{1,0:T(8,128)(2,1)} custom-call(s32[3]{0:T(128)S(1)} %copy-done, bf16[240,128]{1,0:T(8,128)(2,1)S(1)} %get-tuple-element.43.low_ref, bf16[240,128]{1,0:T(8,128)(2,1)S(1)} %collective-permute-done.6.other_ref, bf16[16,128]{1,0:T(8,128)(2,1)S(1)} %get-tuple-element.42.sums_ref, f32[4,16,384]{2,1,0:T(8,128)S(1)} %get-tuple-element.40.side_ref), custom_call_target="tpu_custom_call" | custom-call | flops 75497472 | bytes 1000000 | tf_op jit(solution)/shard_map/pallas_call | solution.py:59
  84.9 17.7 %all-to-all-start.2 = ((bf16[64,16,128]{2,1,0:T(8,128)(2,1)}), bf16[64,16,128]{2,1,0:T(8,128)(2,1)S(1)}, u32[]{:S(2)}, u32[]{:S(2)}) async-start(bf16[64,16,128]{2,1,0:T(8,128)(2,1)} %bitcast.8), calls=%async_computation.2 | async-start | bytes 524288 | tf_op jit(solution)/shard_map/all_to_all | solution.py:508
  102.6 0.0 copy-start.9
  102.6 0.6 shard_map.93.columns_there
  103.2 13.1 %all-gather = bf16[1920,128]{1,0:T(8,128)(2,1)S(1)} all-gather(bf16[240,128]{1,0:T(8,128)(2,1)S(1)} %get-tuple-element.43.low_ref), channel_id=2, replica_groups=mesh['z'=16,'x'=4,'y'=4,'core'=2] {'y','core'}, dimensions={0}, use_global_device_ids=true | all-gather | bytes 552960 | tf_op jit(solution)/shard_map/all_gather | solution.py:510
  116.3 1.1 copy-done.12
  117.3 1.1 copy-done.15
  118.4 3.9 %shard_map.92 = bf16[16,120,128]{2,1,0:T(8,128)(2,1)} custom-call(s32[3]{0:T(128)S(1)} %copy-done, bf16[8,240,128]{2,1,0:T(8,128)(2,1)S(1)} %bitcast.14, bf16[208,1536]{1,0:T(8,128)(2,1)S(1)} %copy-done.4, bf16[192,1536]{1,0:T(8,128)(2,1)} %get-tuple-element.31.refs_1_, bf16[208,1536]{1,0:T(8,128)(2,1)S(1)} %copy-done.7, bf16[192,1536]{1,0:T(8,128)(2,1)S(1)} %copy-done.15, ...), custom_call_target="tpu_custom_call" | custom-call | flops 2214592512 | bytes 6000000 | tf_op jit(solution)/shard_map/pallas_call | solution.py:59
  122.3 3.0 %all-to-all-done.2.in_ref = bf16[64,16,128]{2,1,0:T(8,128)(2,1)S(1)} async-done(((bf16[64,16,128]{2,1,0:T(8,128)(2,1)}), bf16[64,16,128]{2,1,0:T(8,128)(2,1)S(1)}, u32[]{:S(2)}, u32[]{:S(2)}) %all-to-all-start.2) | async-done | bytes 262176 | tf_op jit(solution)/shard_map/all_to_all | solution.py:508
  125.3 8.9 %all-to-all-start.3 = ((bf16[16,120,128]{2,1,0:T(8,128)(2,1)}), bf16[16,120,128]{2,1,0:T(8,128)(2,1)S(1)}, u32[]{:S(2)}, u32[]{:S(2)}) async-start(bf16[16,120,128]{2,1,0:T(8,128)(2,1)} %shard_map.92), calls=%async_computation.3 | async-start | bytes 983040 | tf_op jit(solution)/shard_map/all_to_all | solution.py:521
  134.3 4.9 %collective-permute-start.9 = (bf16[160,1536]{1,0:T(8,128)(2,1)}, bf16[160,1536]{1,0:T(8,128)(2,1)S(1)}, u32[]{:S(2)}, u32[]{:S(2)}) collective-permute-start(bf16[160,1536]{1,0:T(8,128)(2,1)} %copy-done.16), channel_id=1, source_target_pairs={{0,16},{8,24},{16,0},{24,8},{1,17},{9,25},{17,1},{25,9},{2,18},{10... | collective-permute-start | bytes 1474568 | tf_op jit(solution)/shard_map/ppermute | solution.py:430
  139.2 1.1 shard_map.95
  140.3 13.6 %all-gather.1 = bf16[3968,128]{1,0:T(8,128)(2,1)S(1)} all-gather(bf16[496,128]{1,0:T(8,128)(2,1)S(1)} %shard_map.95), channel_id=3, replica_groups=mesh['z'=16,'x'=4,'y'=4,'core'=2] {'y','core'}, dimensions={0}, use_global_device_ids=true | all-gather | bytes 1142784 | tf_op jit(solution)/shard_map/all_gather | solution.py:530
  153.9 5.0 %shard_map.96 = (bf16[6,128,1536]{2,1,0:T(8,128)(2,1)}, f32[384]{0:T(512)}) custom-call(s32[3]{0:T(128)S(1)} %copy-done, bf16[8,496,128]{2,1,0:T(8,128)(2,1)S(1)} %bitcast.11, bf16[160,1536]{1,0:T(8,128)(2,1)S(1)} %copy-done.17, bf16[160,1536]{1,0:T(8,128)(2,1)} %collective-permute-done.7.refs_0_.refs_1_, ...), custom_call_target="tpu_custom_call" | custom-call | flops 1509949440 | bytes 5000000 | tf_op jit(solution)/shard_map/pallas_call | solution.py:59
  158.9 3.9 %all-to-all-done.3.in_ref = bf16[16,120,128]{2,1,0:T(8,128)(2,1)S(1)} async-done(((bf16[16,120,128]{2,1,0:T(8,128)(2,1)}), bf16[16,120,128]{2,1,0:T(8,128)(2,1)S(1)}, u32[]{:S(2)}, u32[]{:S(2)}) %all-to-all-start.3) | async-done | bytes 491552 | tf_op jit(solution)/shard_map/all_to_all | solution.py:521
  162.8 0.7 shard_map.94
  (31 shorter events, 0.1 us)
Async XLA Ops:
  5.1 22.8 %collective-permute-start = (bf16[208,1536]{1,0:T(8,128)(2,1)}, bf16[208,1536]{1,0:T(8,128)(2,1)S(1)}, u32[]{:S(2)}, u32[]{:S(2)}) collective-permute-start(bf16[208,1536]{1,0:T(8,128)(2,1)} %get-tuple-element.30.refs_0_), channel_id=1, source_target_pairs={{0,24},{8,0},{16,8},{24,16},{1,25},{9,1},{17,9},{25,17},{2,26},{10... | collective-permute-start | bytes 1916936 | tf_op jit(solution)/shard_map/ppermute | solution.py:422
  9.8 18.1 %collective-permute-start.1 = (bf16[192,1536]{1,0:T(8,128)(2,1)}, bf16[192,1536]{1,0:T(8,128)(2,1)S(1)}, u32[]{:S(2)}, u32[]{:S(2)}) collective-permute-start(bf16[192,1536]{1,0:T(8,128)(2,1)} %get-tuple-element.31.refs_1_), channel_id=1, source_target_pairs={{0,8},{8,16},{16,24},{24,0},{1,9},{9,17},{17,25},{25,1},{2,10},{10... | collective-permute-start | bytes 1769480 | tf_op jit(solution)/shard_map/ppermute | solution.py:426
  11.7 45.9 %all-to-all-start = ((bf16[16,16,1152]{2,1,0:T(8,128)(2,1)}), bf16[16,16,1152]{2,1,0:T(8,128)(2,1)S(1)}, u32[]{:S(2)}, u32[]{:S(2)}) async-start(bf16[16,16,1152]{2,1,0:T(8,128)(2,1)} %get-tuple-element.27), calls=%async_computation | async-start | bytes 1179648 | tf_op jit(solution)/shard_map/all_to_all | solution.py:458
  27.0 3.2 %copy-start.4 = (bf16[208,1536]{1,0:T(8,128)(2,1)S(1)}, bf16[208,1536]{1,0:T(8,128)(2,1)}, u32[]{:S(2)}) copy-start(bf16[208,1536]{1,0:T(8,128)(2,1)} %get-tuple-element.30.refs_0_) | copy-start | bytes 1916932
  27.9 0.8 copy-start.10
  28.7 0.9 copy-start.5
  30.2 33.7 %copy-start = (s32[3]{0:T(128)S(1)}, s32[3]{0:T(128)}, u32[]{:S(2)}) copy-start(s32[3]{0:T(128)} %pad_add_fusion.place) | copy-start | bytes 40
  30.2 22.1 %collective-permute-start.3 = (bf16[208,1536]{1,0:T(8,128)(2,1)S(1)}, bf16[208,1536]{1,0:T(8,128)(2,1)S(1)}, u32[]{:S(2)}, u32[]{:S(2)}) collective-permute-start(bf16[208,1536]{1,0:T(8,128)(2,1)S(1)} %copy-done.4), channel_id=1, source_target_pairs={{0,8},{8,16},{16,24},{24,0},{1,9},{9,17},{17,25},{25,1},{2,10},{10... | collective-permute-start | bytes 1916936 | tf_op jit(solution)/shard_map/ppermute | solution.py:426
  32.2 19.2 %collective-permute-start.2 = (bf16[192,1536]{1,0:T(8,128)(2,1)}, bf16[192,1536]{1,0:T(8,128)(2,1)S(1)}, u32[]{:S(2)}, u32[]{:S(2)}) collective-permute-start(bf16[192,1536]{1,0:T(8,128)(2,1)} %get-tuple-element.31.refs_1_), channel_id=1, source_target_pairs={{0,24},{8,0},{16,8},{24,16},{1,25},{9,1},{17,9},{25,17},{2,26},{10... | collective-permute-start | bytes 1769480 | tf_op jit(solution)/shard_map/ppermute | solution.py:422
  37.4 26.5 %collective-permute-start.4 = (bf16[208,1536]{1,0:T(8,128)(2,1)}, bf16[208,1536]{1,0:T(8,128)(2,1)S(1)}, u32[]{:S(2)}, u32[]{:S(2)}) collective-permute-start(bf16[208,1536]{1,0:T(8,128)(2,1)} %copy-done.5), channel_id=1, source_target_pairs={{0,24},{8,0},{16,8},{24,16},{1,25},{9,1},{17,9},{25,17},{2,26},{10... | collective-permute-start | bytes 1916936 | tf_op jit(solution)/shard_map/ppermute | solution.py:422
  40.4 23.5 %collective-permute-start.5 = (bf16[192,1536]{1,0:T(8,128)(2,1)}, bf16[192,1536]{1,0:T(8,128)(2,1)S(1)}, u32[]{:S(2)}, u32[]{:S(2)}) collective-permute-start(bf16[192,1536]{1,0:T(8,128)(2,1)} %copy-done.10), channel_id=1, source_target_pairs={{0,8},{8,16},{16,24},{24,0},{1,9},{9,17},{17,25},{25,1},{2,10},{10... | collective-permute-start | bytes 1769480 | tf_op jit(solution)/shard_map/ppermute | solution.py:426
  51.5 0.8 copy-start.13
  52.3 11.6 %copy-start.8 = (bf16[208,1536]{1,0:T(8,128)(2,1)}, bf16[208,1536]{1,0:T(8,128)(2,1)S(1)}, u32[]{:S(2)}) copy-start(bf16[208,1536]{1,0:T(8,128)(2,1)S(1)} %collective-permute-done.3.refs_4_.refs_6_) | copy-start | bytes 1916932
  57.6 1.1 copy-start.6
  58.7 1.1 copy-start.11
  59.8 1.1 copy-start.14
  63.9 2.1 %copy-start.16 = (bf16[160,1536]{1,0:T(8,128)(2,1)}, bf16[160,1536]{1,0:T(8,128)(2,1)S(1)}, u32[]{:S(2)}) copy-start(bf16[160,1536]{1,0:T(8,128)(2,1)S(1)} %get-tuple-element.44.refs_0_) | copy-start | bytes 1474564
  65.9 12.8 %copy-start.3 = (s32[64]{0:T(128)S(1)}, s32[64]{0:T(128)}, u32[]{:S(2)}) copy-start(s32[64]{0:T(128)} %param.7) | copy-start | bytes 772
  65.9 12.8 %all-to-all-start.1 = ((bf16[8,240,128]{2,1,0:T(8,128)(2,1)}), bf16[8,240,128]{2,1,0:T(8,128)(2,1)S(1)}, u32[]{:S(2)}, u32[]{:S(2)}) async-start(bf16[8,240,128]{2,1,0:T(8,128)(2,1)} %get-tuple-element.38), calls=%async_computation.1 | async-start | bytes 983040 | tf_op jit(solution)/shard_map/all_to_all | solution.py:491
  70.8 31.8 %collective-permute-start.8 = (bf16[160,1536]{1,0:T(8,128)(2,1)}, bf16[160,1536]{1,0:T(8,128)(2,1)}, u32[]{:S(2)}, u32[]{:S(2)}) collective-permute-start(bf16[160,1536]{1,0:T(8,128)(2,1)} %copy-done.16), channel_id=1, source_target_pairs={{0,8},{8,16},{16,24},{24,0},{1,9},{9,17},{17,25},{25,1},{2,10},{10... | collective-permute-start | bytes 1474568 | tf_op jit(solution)/shard_map/ppermute | solution.py:426
  72.9 29.7 %collective-permute-start.7 = (bf16[160,1536]{1,0:T(8,128)(2,1)}, bf16[160,1536]{1,0:T(8,128)(2,1)}, u32[]{:S(2)}, u32[]{:S(2)}) collective-permute-start(bf16[160,1536]{1,0:T(8,128)(2,1)} %copy-done.16), channel_id=1, source_target_pairs={{0,24},{8,0},{16,8},{24,16},{1,25},{9,1},{17,9},{25,17},{2,26},{10... | collective-permute-start | bytes 1474568 | tf_op jit(solution)/shard_map/ppermute | solution.py:422
  79.9 3.1 %collective-permute-start.6 = (bf16[240,128]{1,0:T(8,128)(2,1)S(1)}, bf16[240,128]{1,0:T(8,128)(2,1)S(1)}, u32[]{:S(2)}, u32[]{:S(2)}) collective-permute-start(bf16[240,128]{1,0:T(8,128)(2,1)S(1)} %get-tuple-element.43.low_ref), channel_id=1, source_target_pairs={{0,1},{1,0},{2,3},{3,2},{4,5},{5,4},{6,7},{7,6},{8,9},{9,8},{10,11... | collective-permute-start | bytes 184328 | tf_op jit(solution)/shard_map/ppermute | solution.py:499
  84.9 40.5 %all-to-all-start.2 = ((bf16[64,16,128]{2,1,0:T(8,128)(2,1)}), bf16[64,16,128]{2,1,0:T(8,128)(2,1)S(1)}, u32[]{:S(2)}, u32[]{:S(2)}) async-start(bf16[64,16,128]{2,1,0:T(8,128)(2,1)} %bitcast.8), calls=%async_computation.2 | async-start | bytes 524288 | tf_op jit(solution)/shard_map/all_to_all | solution.py:508
  102.6 13.7 %copy-start.7 = (bf16[208,1536]{1,0:T(8,128)(2,1)S(1)}, bf16[208,1536]{1,0:T(8,128)(2,1)}, u32[]{:S(2)}) copy-start(bf16[208,1536]{1,0:T(8,128)(2,1)} %copy-done.5) | copy-start | bytes 1916932
  102.6 13.7 %copy-start.9 = (bf16[208,1536]{1,0:T(8,128)(2,1)S(1)}, bf16[208,1536]{1,0:T(8,128)(2,1)}, u32[]{:S(2)}) copy-start(bf16[208,1536]{1,0:T(8,128)(2,1)} %copy-done.8) | copy-start | bytes 1916932
  116.3 1.1 copy-start.12
  117.3 1.1 copy-start.15
  118.4 20.8 %copy-start.1 = (f32[8,128]{1,0:T(8,128)S(1)}, f32[8,128]{1,0:T(8,128)}, u32[]{:S(2)}) copy-start(f32[8,128]{1,0:T(8,128)} %shard_map.86.weights_there) | copy-start | bytes 12292
  118.4 20.8 %copy-start.2 = (f32[8,128]{1,0:T(8,128)S(1)}, f32[8,128]{1,0:T(8,128)}, u32[]{:S(2)}) copy-start(f32[8,128]{1,0:T(8,128)} %shard_map.93.columns_there) | copy-start | bytes 12292
  122.3 31.6 %copy-start.17 = (bf16[160,1536]{1,0:T(8,128)(2,1)S(1)}, bf16[160,1536]{1,0:T(8,128)(2,1)}, u32[]{:S(2)}) copy-start(bf16[160,1536]{1,0:T(8,128)(2,1)} %copy-done.16) | copy-start | bytes 1474564
  125.3 37.5 %all-to-all-start.3 = ((bf16[16,120,128]{2,1,0:T(8,128)(2,1)}), bf16[16,120,128]{2,1,0:T(8,128)(2,1)S(1)}, u32[]{:S(2)}, u32[]{:S(2)}) async-start(bf16[16,120,128]{2,1,0:T(8,128)(2,1)} %shard_map.92), calls=%async_computation.3 | async-start | bytes 983040 | tf_op jit(solution)/shard_map/all_to_all | solution.py:521
  134.3 19.6 %collective-permute-start.9 = (bf16[160,1536]{1,0:T(8,128)(2,1)}, bf16[160,1536]{1,0:T(8,128)(2,1)S(1)}, u32[]{:S(2)}, u32[]{:S(2)}) collective-permute-start(bf16[160,1536]{1,0:T(8,128)(2,1)} %copy-done.16), channel_id=1, source_target_pairs={{0,16},{8,24},{16,0},{24,8},{1,17},{9,25},{17,1},{25,9},{2,18},{10... | collective-permute-start | bytes 1474568 | tf_op jit(solution)/shard_map/ppermute | solution.py:430

commit v6 on v5

--- a/solution.py
+++ b/solution.py
@@ -329,7 +329,7 @@
         px_ref[z, ROWS - 8 :, :] = blocks[-1].astype(BF)
 
 
-def order_kernel(place, in_ref, weights_there, columns_there, out_ref, block):
+def order_kernel(place, weights_there, columns_there, in_ref, out_ref, block):
     del weights_there, columns_there
     n = BR * NZ
     r, c = iota((2 * n, RHO), 0), iota((2 * n, RHO), 1)
@@ -405,15 +405,15 @@
 
 
 def arrived_kernel(*refs):
-    refs[-1][...] = jnp.zeros_like(refs[-1])
+    refs[-1][0] = 0
 
 
 def arrived(arrays):
     return pl.pallas_call(
         arrived_kernel,
-        out_shape=jax.ShapeDtypeStruct((8, 128), F32),
+        out_shape=jax.ShapeDtypeStruct((1,), I32),
         in_specs=[pl.BlockSpec(memory_space=ANY)] * len(arrays),
-        out_specs=pl.BlockSpec(memory_space=VMEM),
+        out_specs=pl.BlockSpec(memory_space=SMEM),
         cost_estimate=pl.CostEstimate(flops=50 * 10**9, bytes_accessed=0, transcendentals=0),
     )(*arrays)
 
@@ -522,8 +522,8 @@
     moved, = call(
         order_kernel,
         [((MOVED * NZ + 16, 128), BF)],
-        [place, moved, there, columns_there],
-        1,
+        [place, there, columns_there, moved],
+        3,
         [VMEM((RHO, 128), BF)],
         moved=10**6,
     )

time: 166 us -> 166 us (level)
    unnamed x36 -> x32, local copies, waits for them, and re-layouts: 7.88 us -> 7.86 us
  transfers between devices with their start and end apart: 14 -> 14, of which waited for: 7 -> 7; matrix products, arithmetic and copies ran while one was open for 0% -> 0% of each run, Pallas kernels for 11% -> 12%
where the time goes in v6:
time: 166 us; the launch traced here: 163 us
  starting transfers between devices  79.7 us (48%)
  blocking collectives  26.7 us (16%)
  Pallas kernels  25.5 us (15%)
  waiting for transfers between devices  22 us (13%)
  local copies, waits for them, and re-layouts  7.86 us (5%)
    pallas_call x10, Pallas kernels, call(): pl.pallas_call(kernel, out_shape=[jax.ShapeDtypeStruct(s, d) for s, d in...  24.4 us
    ppermute x4, starting transfers between devices, to_left(): return lax.ppermute(value, 'x', [(i, (i - 1) % NX) for i in range(NX)])  17.7 us
    all_to_all x1, starting transfers between devices, body(): lax.all_to_all(sent.reshape(DP, 16, 128), ('z', 'x'), 0, 0, tiled=True)  17.5 us
    all_to_all x1, starting transfers between devices, body(): along_z = lax.all_to_all(packed, 'z', 0, 0, tiled=True)  15.2 us
    all_gather x1, blocking collectives, body(): moved = lax.all_gather(moved, ('y', 'core'), axis=0)  13.6 us
    all_gather x1, blocking collectives, body(): grad = lax.all_gather(low, ('y', 'core'), axis=0)  13.1 us
    all_to_all x1, starting transfers between devices, body(): pz = lax.all_to_all(px, 'z', 0, 0, tiled=True)  8.85 us
    ppermute x4, starting transfers between devices, to_right(): return lax.ppermute(value, 'x', [(i, (i + 1) % NX) for i in range(NX)])  8.85 us
  transfers between devices with their start and end apart: 14, of which 7 were waited for; matrix products, arithmetic and copies ran while one was open for 0% of the time, Pallas kernels for 12%

profile of v6, /device:TPU:24, one launch (start us, length us, event | category | flops | bytes accessed | tf_op | source)
XLA Modules:
  0.0 163.3 jit_solution(11638025159043852290)
XLA Ops:
  0.6 0.6 pad_add_fusion.place
  1.2 3.9 %shard_map.85 = (bf16[208,1536]{1,0:T(8,128)(2,1)}, bf16[192,1536]{1,0:T(8,128)(2,1)}, bf16[16,16,1152]{2,1,0:T(8,128)(2,1)}) custom-call(s32[3]{0:T(128)} %pad_add_fusion.place, bf16[10,1536]{1,0:T(8,128)(2,1)} %x_in.1, bf16[10,24576]{1,0:T(8,128)(2,1)} %up_in.1, bf16[384,1536]{1,0:T(8,128)(2,1)} %w_in.1, f32[384]{0:T(512)} %bias_in.1, s32[1,64]{1,0:T(1,128)} %bitcast.16), custom_call_target="tpu_custom_call" | custom-call | flops 201326592 | bytes 5000000 | tf_op jit(solution)/shard_map/pallas_call | solution.py:59
  5.1 4.7 %collective-permute-start = (bf16[208,1536]{1,0:T(8,128)(2,1)}, bf16[208,1536]{1,0:T(8,128)(2,1)S(1)}, u32[]{:S(2)}, u32[]{:S(2)}) collective-permute-start(bf16[208,1536]{1,0:T(8,128)(2,1)} %get-tuple-element.30.refs_0_), channel_id=1, source_target_pairs={{0,24},{8,0},{16,8},{24,16},{1,25},{9,1},{17,9},{25,17},{2,26},{10... | collective-permute-start | bytes 1916936 | tf_op jit(solution)/shard_map/ppermute | solution.py:422
  9.8 1.9 %collective-permute-start.1 = (bf16[192,1536]{1,0:T(8,128)(2,1)}, bf16[192,1536]{1,0:T(8,128)(2,1)S(1)}, u32[]{:S(2)}, u32[]{:S(2)}) collective-permute-start(bf16[192,1536]{1,0:T(8,128)(2,1)} %get-tuple-element.31.refs_1_), channel_id=1, source_target_pairs={{0,8},{8,16},{16,24},{24,0},{1,9},{9,17},{17,25},{25,1},{2,10},{10... | collective-permute-start | bytes 1769480 | tf_op jit(solution)/shard_map/ppermute | solution.py:426
  11.7 15.2 %all-to-all-start = ((bf16[16,16,1152]{2,1,0:T(8,128)(2,1)}), bf16[16,16,1152]{2,1,0:T(8,128)(2,1)S(1)}, u32[]{:S(2)}, u32[]{:S(2)}) async-start(bf16[16,16,1152]{2,1,0:T(8,128)(2,1)} %get-tuple-element.27), calls=%async_computation | async-start | bytes 1179648 | tf_op jit(solution)/shard_map/all_to_all | solution.py:458
  27.0 0.0 copy-start.2
  27.0 0.9 collective-permute-done.1.refs_1_.refs_5_.refs_7_
  27.9 0.0 collective-permute-done.refs_0_.refs_2_
  27.9 0.8 copy-done.8
  28.8 0.8 copy-done.3
  29.6 0.5 shard_map.86.weights_there
  30.1 1.9 %collective-permute-start.3 = (bf16[208,1536]{1,0:T(8,128)(2,1)S(1)}, bf16[208,1536]{1,0:T(8,128)(2,1)S(1)}, u32[]{:S(2)}, u32[]{:S(2)}) collective-permute-start(bf16[208,1536]{1,0:T(8,128)(2,1)S(1)} %copy-done.2), channel_id=1, source_target_pairs={{0,8},{8,16},{16,24},{24,0},{1,9},{9,17},{17,25},{25,1},{2,10},{10... | collective-permute-start | bytes 1916936 | tf_op jit(solution)/shard_map/ppermute | solution.py:426
  32.1 5.1 %collective-permute-start.2 = (bf16[192,1536]{1,0:T(8,128)(2,1)}, bf16[192,1536]{1,0:T(8,128)(2,1)S(1)}, u32[]{:S(2)}, u32[]{:S(2)}) collective-permute-start(bf16[192,1536]{1,0:T(8,128)(2,1)} %get-tuple-element.31.refs_1_), channel_id=1, source_target_pairs={{0,24},{8,0},{16,8},{24,16},{1,25},{9,1},{17,9},{25,17},{2,26},{10... | collective-permute-start | bytes 1769480 | tf_op jit(solution)/shard_map/ppermute | solution.py:422
  37.2 3.0 %collective-permute-start.4 = (bf16[208,1536]{1,0:T(8,128)(2,1)}, bf16[208,1536]{1,0:T(8,128)(2,1)S(1)}, u32[]{:S(2)}, u32[]{:S(2)}) collective-permute-start(bf16[208,1536]{1,0:T(8,128)(2,1)} %copy-done.3), channel_id=1, source_target_pairs={{0,24},{8,0},{16,8},{24,16},{1,25},{9,1},{17,9},{25,17},{2,26},{10... | collective-permute-start | bytes 1916936 | tf_op jit(solution)/shard_map/ppermute | solution.py:422
  40.2 2.9 %collective-permute-start.5 = (bf16[192,1536]{1,0:T(8,128)(2,1)}, bf16[192,1536]{1,0:T(8,128)(2,1)S(1)}, u32[]{:S(2)}, u32[]{:S(2)}) collective-permute-start(bf16[192,1536]{1,0:T(8,128)(2,1)} %copy-done.8), channel_id=1, source_target_pairs={{0,8},{8,16},{16,24},{24,0},{1,9},{9,17},{17,25},{25,1},{2,10},{10... | collective-permute-start | bytes 1769480 | tf_op jit(solution)/shard_map/ppermute | solution.py:426
  43.1 8.2 %collective-permute-done.2.refs_3_ = bf16[192,1536]{1,0:T(8,128)(2,1)S(1)} collective-permute-done((bf16[192,1536]{1,0:T(8,128)(2,1)}, bf16[192,1536]{1,0:T(8,128)(2,1)S(1)}, u32[]{:S(2)}, u32[]{:S(2)}) %collective-permute-start.2) | collective-permute-done | bytes 589856 | tf_op jit(solution)/shard_map/ppermute | solution.py:422
  51.3 0.8 copy-done.11
  52.1 0.0 collective-permute-done.3.refs_4_.refs_6_
  52.1 5.5 %all-to-all-done = bf16[16,16,1152]{2,1,0:T(8,128)(2,1)S(1)} async-done(((bf16[16,16,1152]{2,1,0:T(8,128)(2,1)}), bf16[16,16,1152]{2,1,0:T(8,128)(2,1)S(1)}, u32[]{:S(2)}, u32[]{:S(2)}) %all-to-all-start) | async-done | bytes 589856 | tf_op jit(solution)/shard_map/all_to_all | solution.py:458
  57.6 1.1 copy-done.4
  58.7 1.1 copy-done.9
  59.8 1.1 copy-done.12
  60.9 3.0 %shard_map.87 = (bf16[256,1536]{1,0:T(8,128)(2,1)S(1)}, bf16[160,1536]{1,0:T(8,128)(2,1)S(1)}, bf16[6,240,128]{2,1,0:T(8,128)(2,1)S(1)}, bf16[3,16,384]{2,1,0:T(8,128)(2,1)S(1)}) custom-call(bf16[256,1152]{1,0:T(8,128)(2,1)S(1)} %bitcast.12, bf16[208,1536]{1,0:T(8,128)(2,1)S(1)} %copy-done.2, bf16[192,1536]{1,0:T(8,128)(2,1)} %get-tuple-element.31.refs_1_, ...), custom_call_target="tpu_custom_call" | custom-call | flops 1207959552 | bytes 4000000 | tf_op jit(solution)/shard_map/pallas_call | solution.py:59
  63.9 2.0 %shard_map.88 = (bf16[8,240,128]{2,1,0:T(8,128)(2,1)}, f32[4,16,384]{2,1,0:T(8,128)S(1)}) custom-call(s32[3]{0:T(128)S(1)} %copy-done, bf16[256,1536]{1,0:T(8,128)(2,1)S(1)} %get-tuple-element.34.x_ref, bf16[6,240,128]{2,1,0:T(8,128)(2,1)S(1)} %get-tuple-element.35.near_ref, bf16[3,16,384]{2,1,0:T(8,128)(2,1)S(1)} %get-tuple-element.36.near_side, ...), custom_call_target="tpu_custom_call" | custom-call | flops 201326592 | bytes 2000000 | tf_op jit(solution)/shard_map/pallas_call | solution.py:59
  66.0 4.8 %all-to-all-start.1 = ((bf16[8,240,128]{2,1,0:T(8,128)(2,1)}), bf16[8,240,128]{2,1,0:T(8,128)(2,1)S(1)}, u32[]{:S(2)}, u32[]{:S(2)}) async-start(bf16[8,240,128]{2,1,0:T(8,128)(2,1)} %get-tuple-element.38), calls=%async_computation.1 | async-start | bytes 983040 | tf_op jit(solution)/shard_map/all_to_all | solution.py:491
  70.8 2.2 %collective-permute-start.8 = (bf16[160,1536]{1,0:T(8,128)(2,1)}, bf16[160,1536]{1,0:T(8,128)(2,1)}, u32[]{:S(2)}, u32[]{:S(2)}) collective-permute-start(bf16[160,1536]{1,0:T(8,128)(2,1)} %copy-done.14), channel_id=1, source_target_pairs={{0,8},{8,16},{16,24},{24,0},{1,9},{9,17},{17,25},{25,1},{2,10},{10... | collective-permute-start | bytes 1474568 | tf_op jit(solution)/shard_map/ppermute | solution.py:426
  72.9 4.9 %collective-permute-start.7 = (bf16[160,1536]{1,0:T(8,128)(2,1)}, bf16[160,1536]{1,0:T(8,128)(2,1)}, u32[]{:S(2)}, u32[]{:S(2)}) collective-permute-start(bf16[160,1536]{1,0:T(8,128)(2,1)} %copy-done.14), channel_id=1, source_target_pairs={{0,24},{8,0},{16,8},{24,16},{1,25},{9,1},{17,9},{25,17},{2,26},{10... | collective-permute-start | bytes 1474568 | tf_op jit(solution)/shard_map/ppermute | solution.py:422
  77.8 0.4 shard_map.89.ug_ref
  78.3 0.4 all-to-all-done.1.parts_ref
  78.7 1.2 shard_map.90
  79.9 1.9 %collective-permute-start.6 = (bf16[240,128]{1,0:T(8,128)(2,1)S(1)}, bf16[240,128]{1,0:T(8,128)(2,1)S(1)}, u32[]{:S(2)}, u32[]{:S(2)}) collective-permute-start(bf16[240,128]{1,0:T(8,128)(2,1)S(1)} %get-tuple-element.43.low_ref), channel_id=1, source_target_pairs={{0,1},{1,0},{2,3},{3,2},{4,5},{5,4},{6,7},{7,6},{8,9},{9,8},{10,11... | collective-permute-start | bytes 184328 | tf_op jit(solution)/shard_map/ppermute | solution.py:499
  81.8 1.2 collective-permute-done.6.other_ref
  83.0 1.8 %shard_map.91 = bf16[1024,128]{1,0:T(8,128)(2,1)} custom-call(s32[3]{0:T(128)S(1)} %copy-done, bf16[240,128]{1,0:T(8,128)(2,1)S(1)} %get-tuple-element.43.low_ref, bf16[240,128]{1,0:T(8,128)(2,1)S(1)} %collective-permute-done.6.other_ref, bf16[16,128]{1,0:T(8,128)(2,1)S(1)} %get-tuple-element.42.sums_ref, f32[4,16,384]{2,1,0:T(8,128)S(1)} %get-tuple-element.40.side_ref), custom_call_target="tpu_custom_call" | custom-call | flops 75497472 | bytes 1000000 | tf_op jit(solution)/shard_map/pallas_call | solution.py:59
  84.9 17.5 %all-to-all-start.2 = ((bf16[64,16,128]{2,1,0:T(8,128)(2,1)}), bf16[64,16,128]{2,1,0:T(8,128)(2,1)S(1)}, u32[]{:S(2)}, u32[]{:S(2)}) async-start(bf16[64,16,128]{2,1,0:T(8,128)(2,1)} %bitcast.8), calls=%async_computation.2 | async-start | bytes 524288 | tf_op jit(solution)/shard_map/all_to_all | solution.py:508
  102.4 0.0 copy-start.7
  102.4 0.5 shard_map.93.columns_there
  103.0 13.1 %all-gather = bf16[1920,128]{1,0:T(8,128)(2,1)S(1)} all-gather(bf16[240,128]{1,0:T(8,128)(2,1)S(1)} %get-tuple-element.43.low_ref), channel_id=2, replica_groups=mesh['z'=16,'x'=4,'y'=4,'core'=2] {'y','core'}, dimensions={0}, use_global_device_ids=true | all-gather | bytes 552960 | tf_op jit(solution)/shard_map/all_gather | solution.py:510
  116.1 1.1 copy-done.10
  117.1 1.1 copy-done.13
  118.2 3.9 %shard_map.92 = bf16[16,120,128]{2,1,0:T(8,128)(2,1)} custom-call(s32[3]{0:T(128)S(1)} %copy-done, bf16[8,240,128]{2,1,0:T(8,128)(2,1)S(1)} %bitcast.14, bf16[208,1536]{1,0:T(8,128)(2,1)S(1)} %copy-done.2, bf16[192,1536]{1,0:T(8,128)(2,1)} %get-tuple-element.31.refs_1_, bf16[208,1536]{1,0:T(8,128)(2,1)S(1)} %copy-done.5, bf16[192,1536]{1,0:T(8,128)(2,1)S(1)} %copy-done.13, ...), custom_call_target="tpu_custom_call" | custom-call | flops 2214592512 | bytes 6000000 | tf_op jit(solution)/shard_map/pallas_call | solution.py:59
  122.1 3.0 %all-to-all-done.2.in_ref = bf16[64,16,128]{2,1,0:T(8,128)(2,1)S(1)} async-done(((bf16[64,16,128]{2,1,0:T(8,128)(2,1)}), bf16[64,16,128]{2,1,0:T(8,128)(2,1)S(1)}, u32[]{:S(2)}, u32[]{:S(2)}) %all-to-all-start.2) | async-done | bytes 262176 | tf_op jit(solution)/shard_map/all_to_all | solution.py:508
  125.2 8.9 %all-to-all-start.3 = ((bf16[16,120,128]{2,1,0:T(8,128)(2,1)}), bf16[16,120,128]{2,1,0:T(8,128)(2,1)S(1)}, u32[]{:S(2)}, u32[]{:S(2)}) async-start(bf16[16,120,128]{2,1,0:T(8,128)(2,1)} %shard_map.92), calls=%async_computation.3 | async-start | bytes 983040 | tf_op jit(solution)/shard_map/all_to_all | solution.py:521
  134.0 4.9 %collective-permute-start.9 = (bf16[160,1536]{1,0:T(8,128)(2,1)}, bf16[160,1536]{1,0:T(8,128)(2,1)S(1)}, u32[]{:S(2)}, u32[]{:S(2)}) collective-permute-start(bf16[160,1536]{1,0:T(8,128)(2,1)} %copy-done.14), channel_id=1, source_target_pairs={{0,16},{8,24},{16,0},{24,8},{1,17},{9,25},{17,1},{25,9},{2,18},{10... | collective-permute-start | bytes 1474568 | tf_op jit(solution)/shard_map/ppermute | solution.py:430
  138.9 2.4 %shard_map.95 = bf16[496,128]{1,0:T(8,128)(2,1)S(1)} custom-call(s32[3]{0:T(128)S(1)} %copy-done, s32[1]{0:T(128)} %shard_map.86.weights_there, s32[1]{0:T(128)} %shard_map.93.columns_there, bf16[64,16,128]{2,1,0:T(8,128)(2,1)S(1)} %all-to-all-done.2.in_ref), custom_call_target="tpu_custom_call" | custom-call | bytes 1000000 | tf_op jit(solution)/shard_map/pallas_call | solution.py:59
  141.3 13.6 %all-gather.1 = bf16[3968,128]{1,0:T(8,128)(2,1)S(1)} all-gather(bf16[496,128]{1,0:T(8,128)(2,1)S(1)} %shard_map.95), channel_id=3, replica_groups=mesh['z'=16,'x'=4,'y'=4,'core'=2] {'y','core'}, dimensions={0}, use_global_device_ids=true | all-gather | bytes 1142784 | tf_op jit(solution)/shard_map/all_gather | solution.py:530
  154.9 5.0 %shard_map.96 = (bf16[6,128,1536]{2,1,0:T(8,128)(2,1)}, f32[384]{0:T(512)}) custom-call(s32[3]{0:T(128)S(1)} %copy-done, bf16[8,496,128]{2,1,0:T(8,128)(2,1)S(1)} %bitcast.11, bf16[160,1536]{1,0:T(8,128)(2,1)S(1)} %copy-done.15, bf16[160,1536]{1,0:T(8,128)(2,1)} %collective-permute-done.7.refs_0_.refs_1_, ...), custom_call_target="tpu_custom_call" | custom-call | flops 1509949440 | bytes 5000000 | tf_op jit(solution)/shard_map/pallas_call | solution.py:59
  160.0 2.6 %all-to-all-done.3.in_ref = bf16[16,120,128]{2,1,0:T(8,128)(2,1)S(1)} async-done(((bf16[16,120,128]{2,1,0:T(8,128)(2,1)}), bf16[16,120,128]{2,1,0:T(8,128)(2,1)S(1)}, u32[]{:S(2)}, u32[]{:S(2)}) %all-to-all-start.3) | async-done | bytes 491552 | tf_op jit(solution)/shard_map/all_to_all | solution.py:521
  162.6 0.7 shard_map.94
  (27 shorter events, 0.1 us)
Async XLA Ops:
  5.1 22.8 %collective-permute-start = (bf16[208,1536]{1,0:T(8,128)(2,1)}, bf16[208,1536]{1,0:T(8,128)(2,1)S(1)}, u32[]{:S(2)}, u32[]{:S(2)}) collective-permute-start(bf16[208,1536]{1,0:T(8,128)(2,1)} %get-tuple-element.30.refs_0_), channel_id=1, source_target_pairs={{0,24},{8,0},{16,8},{24,16},{1,25},{9,1},{17,9},{25,17},{2,26},{10... | collective-permute-start | bytes 1916936 | tf_op jit(solution)/shard_map/ppermute | solution.py:422
  9.8 18.1 %collective-permute-start.1 = (bf16[192,1536]{1,0:T(8,128)(2,1)}, bf16[192,1536]{1,0:T(8,128)(2,1)S(1)}, u32[]{:S(2)}, u32[]{:S(2)}) collective-permute-start(bf16[192,1536]{1,0:T(8,128)(2,1)} %get-tuple-element.31.refs_1_), channel_id=1, source_target_pairs={{0,8},{8,16},{16,24},{24,0},{1,9},{9,17},{17,25},{25,1},{2,10},{10... | collective-permute-start | bytes 1769480 | tf_op jit(solution)/shard_map/ppermute | solution.py:426
  11.7 45.9 %all-to-all-start = ((bf16[16,16,1152]{2,1,0:T(8,128)(2,1)}), bf16[16,16,1152]{2,1,0:T(8,128)(2,1)S(1)}, u32[]{:S(2)}, u32[]{:S(2)}) async-start(bf16[16,16,1152]{2,1,0:T(8,128)(2,1)} %get-tuple-element.27), calls=%async_computation | async-start | bytes 1179648 | tf_op jit(solution)/shard_map/all_to_all | solution.py:458
  27.0 3.2 %copy-start.2 = (bf16[208,1536]{1,0:T(8,128)(2,1)S(1)}, bf16[208,1536]{1,0:T(8,128)(2,1)}, u32[]{:S(2)}) copy-start(bf16[208,1536]{1,0:T(8,128)(2,1)} %get-tuple-element.30.refs_0_) | copy-start | bytes 1916932
  27.9 0.8 copy-start.8
  28.8 0.8 copy-start.3
  30.1 33.8 %copy-start = (s32[3]{0:T(128)S(1)}, s32[3]{0:T(128)}, u32[]{:S(2)}) copy-start(s32[3]{0:T(128)} %pad_add_fusion.place) | copy-start | bytes 40
  30.1 22.0 %collective-permute-start.3 = (bf16[208,1536]{1,0:T(8,128)(2,1)S(1)}, bf16[208,1536]{1,0:T(8,128)(2,1)S(1)}, u32[]{:S(2)}, u32[]{:S(2)}) collective-permute-start(bf16[208,1536]{1,0:T(8,128)(2,1)S(1)} %copy-done.2), channel_id=1, source_target_pairs={{0,8},{8,16},{16,24},{24,0},{1,9},{9,17},{17,25},{25,1},{2,10},{10... | collective-permute-start | bytes 1916936 | tf_op jit(solution)/shard_map/ppermute | solution.py:426
  32.1 19.2 %collective-permute-start.2 = (bf16[192,1536]{1,0:T(8,128)(2,1)}, bf16[192,1536]{1,0:T(8,128)(2,1)S(1)}, u32[]{:S(2)}, u32[]{:S(2)}) collective-permute-start(bf16[192,1536]{1,0:T(8,128)(2,1)} %get-tuple-element.31.refs_1_), channel_id=1, source_target_pairs={{0,24},{8,0},{16,8},{24,16},{1,25},{9,1},{17,9},{25,17},{2,26},{10... | collective-permute-start | bytes 1769480 | tf_op jit(solution)/shard_map/ppermute | solution.py:422
  37.2 26.7 %collective-permute-start.4 = (bf16[208,1536]{1,0:T(8,128)(2,1)}, bf16[208,1536]{1,0:T(8,128)(2,1)S(1)}, u32[]{:S(2)}, u32[]{:S(2)}) collective-permute-start(bf16[208,1536]{1,0:T(8,128)(2,1)} %copy-done.3), channel_id=1, source_target_pairs={{0,24},{8,0},{16,8},{24,16},{1,25},{9,1},{17,9},{25,17},{2,26},{10... | collective-permute-start | bytes 1916936 | tf_op jit(solution)/shard_map/ppermute | solution.py:422
  40.2 23.7 %collective-permute-start.5 = (bf16[192,1536]{1,0:T(8,128)(2,1)}, bf16[192,1536]{1,0:T(8,128)(2,1)S(1)}, u32[]{:S(2)}, u32[]{:S(2)}) collective-permute-start(bf16[192,1536]{1,0:T(8,128)(2,1)} %copy-done.8), channel_id=1, source_target_pairs={{0,8},{8,16},{16,24},{24,0},{1,9},{9,17},{17,25},{25,1},{2,10},{10... | collective-permute-start | bytes 1769480 | tf_op jit(solution)/shard_map/ppermute | solution.py:426
  51.3 0.8 copy-start.11
  52.1 11.8 %copy-start.6 = (bf16[208,1536]{1,0:T(8,128)(2,1)}, bf16[208,1536]{1,0:T(8,128)(2,1)S(1)}, u32[]{:S(2)}) copy-start(bf16[208,1536]{1,0:T(8,128)(2,1)S(1)} %collective-permute-done.3.refs_4_.refs_6_) | copy-start | bytes 1916932
  57.6 1.1 copy-start.4
  58.7 1.1 copy-start.9
  59.8 1.1 copy-start.12
  63.9 2.1 %copy-start.14 = (bf16[160,1536]{1,0:T(8,128)(2,1)}, bf16[160,1536]{1,0:T(8,128)(2,1)S(1)}, u32[]{:S(2)}) copy-start(bf16[160,1536]{1,0:T(8,128)(2,1)S(1)} %get-tuple-element.44.refs_0_) | copy-start | bytes 1474564
  65.9 12.8 %copy-start.1 = (s32[64]{0:T(128)S(1)}, s32[64]{0:T(128)}, u32[]{:S(2)}) copy-start(s32[64]{0:T(128)} %param.7) | copy-start | bytes 772
  66.0 12.8 %all-to-all-start.1 = ((bf16[8,240,128]{2,1,0:T(8,128)(2,1)}), bf16[8,240,128]{2,1,0:T(8,128)(2,1)S(1)}, u32[]{:S(2)}, u32[]{:S(2)}) async-start(bf16[8,240,128]{2,1,0:T(8,128)(2,1)} %get-tuple-element.38), calls=%async_computation.1 | async-start | bytes 983040 | tf_op jit(solution)/shard_map/all_to_all | solution.py:491
  70.8 31.7 %collective-permute-start.8 = (bf16[160,1536]{1,0:T(8,128)(2,1)}, bf16[160,1536]{1,0:T(8,128)(2,1)}, u32[]{:S(2)}, u32[]{:S(2)}) collective-permute-start(bf16[160,1536]{1,0:T(8,128)(2,1)} %copy-done.14), channel_id=1, source_target_pairs={{0,8},{8,16},{16,24},{24,0},{1,9},{9,17},{17,25},{25,1},{2,10},{10... | collective-permute-start | bytes 1474568 | tf_op jit(solution)/shard_map/ppermute | solution.py:426
  72.9 29.5 %collective-permute-start.7 = (bf16[160,1536]{1,0:T(8,128)(2,1)}, bf16[160,1536]{1,0:T(8,128)(2,1)}, u32[]{:S(2)}, u32[]{:S(2)}) collective-permute-start(bf16[160,1536]{1,0:T(8,128)(2,1)} %copy-done.14), channel_id=1, source_target_pairs={{0,24},{8,0},{16,8},{24,16},{1,25},{9,1},{17,9},{25,17},{2,26},{10... | collective-permute-start | bytes 1474568 | tf_op jit(solution)/shard_map/ppermute | solution.py:422
  79.9 3.1 %collective-permute-start.6 = (bf16[240,128]{1,0:T(8,128)(2,1)S(1)}, bf16[240,128]{1,0:T(8,128)(2,1)S(1)}, u32[]{:S(2)}, u32[]{:S(2)}) collective-permute-start(bf16[240,128]{1,0:T(8,128)(2,1)S(1)} %get-tuple-element.43.low_ref), channel_id=1, source_target_pairs={{0,1},{1,0},{2,3},{3,2},{4,5},{5,4},{6,7},{7,6},{8,9},{9,8},{10,11... | collective-permute-start | bytes 184328 | tf_op jit(solution)/shard_map/ppermute | solution.py:499
  84.9 40.3 %all-to-all-start.2 = ((bf16[64,16,128]{2,1,0:T(8,128)(2,1)}), bf16[64,16,128]{2,1,0:T(8,128)(2,1)S(1)}, u32[]{:S(2)}, u32[]{:S(2)}) async-start(bf16[64,16,128]{2,1,0:T(8,128)(2,1)} %bitcast.8), calls=%async_computation.2 | async-start | bytes 524288 | tf_op jit(solution)/shard_map/all_to_all | solution.py:508
  102.4 13.6 %copy-start.5 = (bf16[208,1536]{1,0:T(8,128)(2,1)S(1)}, bf16[208,1536]{1,0:T(8,128)(2,1)}, u32[]{:S(2)}) copy-start(bf16[208,1536]{1,0:T(8,128)(2,1)} %copy-done.3) | copy-start | bytes 1916932
  102.4 13.6 %copy-start.7 = (bf16[208,1536]{1,0:T(8,128)(2,1)S(1)}, bf16[208,1536]{1,0:T(8,128)(2,1)}, u32[]{:S(2)}) copy-start(bf16[208,1536]{1,0:T(8,128)(2,1)} %copy-done.6) | copy-start | bytes 1916932
  116.1 1.1 copy-start.10
  117.1 1.1 copy-start.13
  122.1 32.8 %copy-start.15 = (bf16[160,1536]{1,0:T(8,128)(2,1)S(1)}, bf16[160,1536]{1,0:T(8,128)(2,1)}, u32[]{:S(2)}) copy-start(bf16[160,1536]{1,0:T(8,128)(2,1)} %copy-done.14) | copy-start | bytes 1474564
  125.2 37.4 %all-to-all-start.3 = ((bf16[16,120,128]{2,1,0:T(8,128)(2,1)}), bf16[16,120,128]{2,1,0:T(8,128)(2,1)S(1)}, u32[]{:S(2)}, u32[]{:S(2)}) async-start(bf16[16,120,128]{2,1,0:T(8,128)(2,1)} %shard_map.92), calls=%async_computation.3 | async-start | bytes 983040 | tf_op jit(solution)/shard_map/all_to_all | solution.py:521
  134.0 20.9 %collective-permute-start.9 = (bf16[160,1536]{1,0:T(8,128)(2,1)}, bf16[160,1536]{1,0:T(8,128)(2,1)S(1)}, u32[]{:S(2)}, u32[]{:S(2)}) collective-permute-start(bf16[160,1536]{1,0:T(8,128)(2,1)} %copy-done.14), channel_id=1, source_target_pairs={{0,16},{8,24},{16,0},{24,8},{1,17},{9,25},{17,1},{25,9},{2,18},{10... | collective-permute-start | bytes 1474568 | tf_op jit(solution)/shard_map/ppermute | solution.py:430
